TPU v7x, 32 devices: a whole 2x2x4 slice. The times are simulated.
32 devices in a mesh: seq: 8 (over z, x), dp: 4 (over y, core).
Axes of the slice: x: 2, y: 2, z: 4, core: 2. Of those that a mesh axis runs over, the one named last changes fastest.
Arguments:
- tokens: bfloat16 [32, 2048, 768], P('dp', 'seq'), may hold values from -6 to 6
- segments: int32 [32, 2048], P('dp', 'seq'), may hold values from 0 to 2097151, as said below
- token_types: int32 [32, 2048], P('dp', 'seq'), may hold values from 0 to 2097151, as said below
- cotangent: bfloat16 [32, 1024, 768], P('dp', 'seq'), may hold values from -6 to 6
- query_weight: float32 [768, 768], P('dp'), may hold values from -0.21875 to 0.21875
- key_weight: float32 [768, 768], P('dp'), may hold values from -0.21875 to 0.21875
- value_weight: float32 [768, 768], P('dp'), may hold values from -0.21875 to 0.21875
- output_weight: float32 [768, 768], P('dp'), may hold values from -1.25 to 1.25
- inner_weight: float32 [768, 3072], P('dp'), may hold values from -0.21875 to 0.21875
- outer_weight: float32 [3072, 768], P('dp'), may hold values from -0.109375 to 0.109375
- value_bias: float32 [768], P('dp'), may hold values from -2 to 2
- output_bias: float32 [768], P('dp'), may hold values from -2 to 2
- inner_bias: float32 [3072], P('dp'), may hold values from -2 to 2
- outer_bias: float32 [768], P('dp'), may hold values from -2 to 2
- attention_norm_gain: float32 [768], P('dp'), may hold values from 0.25 to 1.75
- first_shift: float32 [768], P('dp'), may hold values from -2 to 2
- second_gain: float32 [768], P('dp'), may hold values from 0.25 to 1.75
- second_shift: float32 [768], P('dp'), may hold values from -2 to 2
- content_bias: float32 [12, 64], P('dp'), may hold values from -3 to 3
- position_bias: float32 [12, 64], P('dp'), may hold values from -3 to 3
- type_bias: float32 [12, 64], P('dp'), may hold values from -3 to 3
- relative_kernel: float32 [12, 64, 64], P('dp'), may hold values from -0.75 to 0.75
- type_embed: float32 [12, 2, 64], P('dp'), may hold values from -5 to 5
Outputs:
- output: bfloat16 [32, 1024, 768], P('dp', 'seq')
- grad_tokens: bfloat16 [32, 2048, 768], P('dp', 'seq')
- grad_query_weight: float32 [768, 768], P('dp')
- grad_key_weight: float32 [768, 768], P('dp')
- grad_value_weight: float32 [768, 768], P('dp')
- grad_output_weight: float32 [768, 768], P('dp')
- grad_inner_weight: float32 [768, 3072], P('dp')
- grad_outer_weight: float32 [3072, 768], P('dp')
- grad_value_bias: float32 [768], P('dp')
- grad_output_bias: float32 [768], P('dp')
- grad_inner_bias: float32 [3072], P('dp')
- grad_outer_bias: float32 [768], P('dp')
- grad_first_gain: float32 [768], P('dp')
- grad_first_shift: float32 [768], P('dp')
- grad_second_gain: float32 [768], P('dp')
- grad_second_shift: float32 [768], P('dp')
- grad_content_bias: float32 [12, 64], P('dp')
- grad_position_bias: float32 [12, 64], P('dp')
- grad_type_bias: float32 [12, 64], P('dp')
- grad_relative_kernel: float32 [12, 64, 64], P('dp')
- grad_type_embed: float32 [12, 2, 64], P('dp')
Inputs may be any that keep to these rules, and one draw needn't show every extreme that they name: `segments`: each sequence holds two or three documents, each a contiguous run of positions with a label of its own that differs from the labels of the sequence's other documents; every document has at least 204 positions; only equality of labels within a sequence has meaning. `token_types`: each sequence uses up to three type labels; only equality of labels within a sequence has meaning.
All inputs are finite; a program needn't handle non-finite values.
Results may differ from a plain program's by a relative error of at most 0.023.
The roundings to bfloat16 on the way count: a program that leaves them out, or rounds other values in their place, can miss the bound.
Values may be sent and summed in bfloat16 or wider, within the bound.
A program may use at most 256 MiB of HBM per device.

v0:
```python
from functools import partial
import math

import jax
import jax.numpy as jnp
from jax import lax
from jax.sharding import PartitionSpec as P

MODEL_WIDTH = 768
HEAD_COUNT = 12
HEAD_SIZE = 64
LEN = 2048
SG = 8
PQ = 1024


highest = lax.Precision.HIGHEST
norm_eps = 1e-05
masked_score = -1e30


def frequencies():
    half_width = HEAD_SIZE // 2
    return jnp.exp(jnp.arange(half_width, dtype=jnp.float32) * (-math.log(10000.0) / half_width))


def norm_forward(inputs, gains, shifts):
    row_mean = jnp.mean(inputs, axis=-1, keepdims=True)
    centred = inputs - row_mean
    inverse = lax.rsqrt(jnp.mean(centred * centred, axis=-1, keepdims=True) + norm_eps)
    normed = centred * inverse
    return (normed * gains + shifts, normed, inverse)


def norm_backward(upstream, normed, inverse, gains):
    scaled = upstream * gains
    along = jnp.mean(scaled * normed, axis=-1, keepdims=True)
    centre = jnp.mean(scaled, axis=-1, keepdims=True)
    return inverse * (scaled - centre - normed * along)


def doc_masks(segment_row, type_row):
    same_document = segment_row[0::2][:, None] == segment_row[None, :]
    same_type = type_row[0::2][:, None] == type_row[None, :]
    return (same_document, same_type)


def score_block(query_row, type_row_terms, pair_row, key_phase, same_document, same_type):
    key_join = jnp.concatenate([pair_row[:, :HEAD_SIZE], key_phase], axis=-1)
    raw_score = lax.dot_general(
        query_row, key_join, (((1,), (1,)), ((), ())), preferred_element_type=jnp.float32
    )
    type_float = type_row_terms.astype(jnp.float32)
    raw_score = raw_score + jnp.where(same_type, type_float[:, 1:2], type_float[:, 0:1])
    return (jnp.where(same_document, raw_score * HEAD_SIZE ** (-0.5), masked_score), key_join)


def body(
    tokens,
    segments,
    token_types,
    cotangent,
    query_weight,
    key_weight,
    value_weight,
    output_weight,
    inner_weight,
    outer_weight,
    value_bias,
    output_bias,
    inner_bias,
    outer_bias,
    attention_norm_gain,
    first_shift,
    second_gain,
    second_shift,
    content_bias,
    position_bias,
    type_bias,
    relative_kernel,
    type_embed,
):
    local_tokens = tokens.shape[1]
    local_pooled = local_tokens // 2
    group_size = lax.axis_size("seq")
    shard_rank = lax.axis_index("seq")
    item_count = SG * HEAD_COUNT // group_size
    half_width = HEAD_SIZE // 2
    score_scale = HEAD_SIZE ** (-0.5)
    frequency = frequencies()
    duplicate_params = (
        lax.all_gather(query_weight.astype(jnp.bfloat16), "dp", axis=0, tiled=True),
        lax.all_gather(key_weight.astype(jnp.bfloat16), "dp", axis=0, tiled=True),
        lax.all_gather(value_weight.astype(jnp.bfloat16), "dp", axis=0, tiled=True),
        lax.all_gather(output_weight.astype(jnp.bfloat16), "dp", axis=0, tiled=True),
        lax.all_gather(inner_weight.astype(jnp.bfloat16), "dp", axis=0, tiled=True),
        lax.all_gather(outer_weight.astype(jnp.bfloat16), "dp", axis=0, tiled=True),
        lax.all_gather(value_bias.astype(jnp.bfloat16), "dp", axis=0, tiled=True),
        lax.all_gather(output_bias.astype(jnp.bfloat16), "dp", axis=0, tiled=True),
        lax.all_gather(inner_bias.astype(jnp.bfloat16), "dp", axis=0, tiled=True),
        lax.all_gather(outer_bias.astype(jnp.bfloat16), "dp", axis=0, tiled=True),
        lax.all_gather(attention_norm_gain.astype(jnp.bfloat16), "dp", axis=0, tiled=True),
        lax.all_gather(first_shift.astype(jnp.bfloat16), "dp", axis=0, tiled=True),
        lax.all_gather(second_gain.astype(jnp.bfloat16), "dp", axis=0, tiled=True),
        lax.all_gather(second_shift.astype(jnp.bfloat16), "dp", axis=0, tiled=True),
        lax.all_gather(content_bias.astype(jnp.bfloat16), "dp", axis=0, tiled=True),
        lax.all_gather(position_bias.astype(jnp.bfloat16), "dp", axis=0, tiled=True),
        lax.all_gather(type_bias.astype(jnp.bfloat16), "dp", axis=0, tiled=True),
        lax.all_gather(relative_kernel.astype(jnp.bfloat16), "dp", axis=0, tiled=True),
        lax.all_gather(type_embed.astype(jnp.bfloat16), "dp", axis=0, tiled=True),
    )
    value_add = duplicate_params[6].astype(jnp.float32)
    output_add = duplicate_params[7].astype(jnp.float32)
    inner_add = duplicate_params[8].astype(jnp.float32)
    outer_add = duplicate_params[9].astype(jnp.float32)
    gain_one = duplicate_params[10].astype(jnp.float32)
    shift_one = duplicate_params[11].astype(jnp.float32)
    gain_two = duplicate_params[12].astype(jnp.float32)
    shift_two = duplicate_params[13].astype(jnp.float32)
    content_add = duplicate_params[14].astype(jnp.float32)[None, :, None, :]
    position_add = duplicate_params[15].astype(jnp.float32)[None, :, None, :]
    type_add = duplicate_params[16].astype(jnp.float32)[None, :, None, :]
    relative = duplicate_params[17].astype(jnp.float32)
    type_table = duplicate_params[18].astype(jnp.float32)
    whole_segments, whole_types = (
        lax.all_gather(segments, "seq", axis=1, tiled=True),
        lax.all_gather(token_types, "seq", axis=1, tiled=True),
    )
    first_rows = tokens[:, 0::2].astype(jnp.float32)
    second = tokens[:, 1::2].astype(jnp.float32)
    pair_same = (segments[:, 0::2] == segments[:, 1::2])[..., None]
    pooled = jnp.where(pair_same, (first_rows + second) * 0.5, first_rows)
    pooled_low = pooled.astype(jnp.bfloat16)
    queries = jnp.einsum(
        "spd,dhe->shpe",
        pooled_low,
        duplicate_params[0].reshape(MODEL_WIDTH, HEAD_COUNT, HEAD_SIZE),
        preferred_element_type=jnp.float32,
    )
    key_rows = jnp.einsum(
        "ukf,fra->urka",
        tokens,
        duplicate_params[1].reshape(MODEL_WIDTH, HEAD_COUNT, HEAD_SIZE),
        preferred_element_type=jnp.float32,
    )
    value_rows = (
        jnp.einsum(
            "ukf,fra->urka",
            tokens,
            duplicate_params[2].reshape(MODEL_WIDTH, HEAD_COUNT, HEAD_SIZE),
            preferred_element_type=jnp.float32,
        )
        + value_add.reshape(HEAD_COUNT, HEAD_SIZE)[None, :, None, :]
    )
    pair_rows = (
        jnp.concatenate([key_rows, value_rows], axis=-1)
        .astype(jnp.bfloat16)
        .reshape(SG * HEAD_COUNT, local_tokens, 2 * HEAD_SIZE)
    )
    shifted = queries + position_add
    relative_terms = jnp.einsum("shpe,hef->shpf", shifted, relative, precision=highest)
    pooled_place = 2.0 * (
        shard_rank * local_pooled + jnp.arange(local_pooled, dtype=jnp.int32)
    ).astype(jnp.float32)
    query_angle = pooled_place[:, None] * frequency[None, :]
    query_cos = jnp.cos(query_angle)
    query_sin = jnp.sin(query_angle)
    relative_cos = relative_terms[..., :half_width]
    relative_sin = relative_terms[..., half_width:]
    position = jnp.concatenate(
        [
            relative_cos * query_cos + relative_sin * query_sin,
            relative_cos * query_sin - relative_sin * query_cos,
        ],
        axis=-1,
    )
    query_join = (
        jnp.concatenate([queries + content_add, position], axis=-1)
        .astype(jnp.bfloat16)
        .reshape(SG * HEAD_COUNT, local_pooled, 2 * HEAD_SIZE)
    )
    typed = queries + type_add
    type_terms = (
        jnp.einsum("shpe,hbe->shpb", typed, type_table, precision=highest)
        .astype(jnp.bfloat16)
        .reshape(SG * HEAD_COUNT, local_pooled, 2)
    )
    query_heads, type_heads, pair_heads = (
        lax.all_to_all(query_join, "seq", split_axis=0, concat_axis=1, tiled=True),
        lax.all_to_all(type_terms, "seq", split_axis=0, concat_axis=1, tiled=True),
        lax.all_to_all(pair_rows, "seq", split_axis=0, concat_axis=1, tiled=True),
    )
    item_rows = (shard_rank * item_count + jnp.arange(item_count, dtype=jnp.int32)) // HEAD_COUNT
    item_segments = whole_segments[item_rows]
    item_types = whole_types[item_rows]
    key_angle = jnp.arange(LEN, dtype=jnp.float32)[:, None] * frequency[None, :]
    key_phase = jnp.concatenate([jnp.cos(key_angle), jnp.sin(key_angle)], axis=-1).astype(
        jnp.bfloat16
    )

    def attend(packed):
        query_row, type_row_terms, pair_row, segment_row, type_row = packed
        same_document, same_type = doc_masks(segment_row, type_row)
        scores, key_join = score_block(
            query_row, type_row_terms, pair_row, key_phase, same_document, same_type
        )
        row_max = jnp.max(scores, axis=1, keepdims=True)
        exponent = jnp.exp(scores - row_max)
        row_total = jnp.sum(exponent, axis=1, keepdims=True)
        weights = exponent / row_total
        mixture = jnp.dot(
            weights.astype(jnp.bfloat16),
            pair_row[:, HEAD_SIZE:],
            preferred_element_type=jnp.float32,
        )
        return (mixture.astype(jnp.bfloat16), row_max + jnp.log(row_total))

    mixed_heads, log_totals = lax.map(
        attend, (query_heads, type_heads, pair_heads, item_segments, item_types)
    )
    mixed_tokens = lax.all_to_all(
        mixed_heads.reshape(item_count, PQ // 2, 2 * HEAD_SIZE),
        "seq",
        split_axis=1,
        concat_axis=0,
        tiled=True,
    ).reshape(SG, HEAD_COUNT, local_pooled, HEAD_SIZE)
    attention = (
        jnp.einsum(
            "shpe,hed->spd",
            mixed_tokens,
            duplicate_params[3].reshape(HEAD_COUNT, HEAD_SIZE, MODEL_WIDTH),
            preferred_element_type=jnp.float32,
        )
        + output_add
    )
    hidden, normed_one, inverse_one = norm_forward(pooled + attention, gain_one, shift_one)
    hidden_low = hidden.astype(jnp.bfloat16)
    expanded = (
        jnp.einsum(
            "spd,df->spf", hidden_low, duplicate_params[4], preferred_element_type=jnp.float32
        )
        + inner_add
    )
    active = jax.nn.gelu(expanded, approximate=True).astype(jnp.bfloat16)
    branch = (
        jnp.einsum("spf,fd->spd", active, duplicate_params[5], preferred_element_type=jnp.float32)
        + outer_add
    )
    result, normed_two, inverse_two = norm_forward(hidden + branch, gain_two, shift_two)
    output = result.astype(jnp.bfloat16)
    again = (
        lax.all_gather(query_weight.astype(jnp.bfloat16), "dp", axis=0, tiled=True),
        lax.all_gather(key_weight.astype(jnp.bfloat16), "dp", axis=0, tiled=True),
        lax.all_gather(value_weight.astype(jnp.bfloat16), "dp", axis=0, tiled=True),
        lax.all_gather(output_weight.astype(jnp.bfloat16), "dp", axis=0, tiled=True),
        lax.all_gather(inner_weight.astype(jnp.bfloat16), "dp", axis=0, tiled=True),
        lax.all_gather(outer_weight.astype(jnp.bfloat16), "dp", axis=0, tiled=True),
        lax.all_gather(attention_norm_gain.astype(jnp.bfloat16), "dp", axis=0, tiled=True),
        lax.all_gather(second_gain.astype(jnp.bfloat16), "dp", axis=0, tiled=True),
        lax.all_gather(relative_kernel.astype(jnp.bfloat16), "dp", axis=0, tiled=True),
        lax.all_gather(type_embed.astype(jnp.bfloat16), "dp", axis=0, tiled=True),
    )
    query_back = again[0]
    key_back = again[1]
    value_back = again[2]
    output_back = again[3]
    inner_back = again[4]
    outer_back = again[5]
    gain_one_back = again[6].astype(jnp.float32)
    gain_two_back = again[7].astype(jnp.float32)
    relative_back = again[8].astype(jnp.float32)
    table_back = again[9].astype(jnp.float32)
    grad_result = cotangent.astype(jnp.float32)
    grad_gain_two = jnp.sum(grad_result * normed_two, axis=(0, 1))
    grad_shift_two = jnp.sum(grad_result, axis=(0, 1))
    grad_second = norm_backward(grad_result, normed_two, inverse_two, gain_two_back)
    grad_branch = grad_second.astype(jnp.bfloat16)
    grad_outer_weight = jnp.einsum(
        "spf,spd->fd", active, grad_branch, preferred_element_type=jnp.float32
    )
    grad_outer_bias = jnp.sum(grad_branch.astype(jnp.float32), axis=(0, 1))
    grad_active = jnp.einsum(
        "spd,fd->spf", grad_branch, outer_back, preferred_element_type=jnp.float32
    )
    gelu_value, gelu_pull = jax.vjp(partial(jax.nn.gelu, approximate=True), expanded)
    grad_expanded = gelu_pull(grad_active)[0].astype(jnp.bfloat16)
    grad_inner_weight = jnp.einsum(
        "spd,spf->df", hidden_low, grad_expanded, preferred_element_type=jnp.float32
    )
    grad_inner_bias = jnp.sum(grad_expanded.astype(jnp.float32), axis=(0, 1))
    grad_hidden = grad_second + jnp.einsum(
        "spf,df->spd", grad_expanded, inner_back, preferred_element_type=jnp.float32
    )
    grad_gain_one = jnp.sum(grad_hidden * normed_one, axis=(0, 1))
    grad_shift_one = jnp.sum(grad_hidden, axis=(0, 1))
    grad_first = norm_backward(grad_hidden, normed_one, inverse_one, gain_one_back)
    grad_attention = grad_first.astype(jnp.bfloat16)
    grad_output_weight = jnp.einsum(
        "shpe,spd->hed", mixed_tokens, grad_attention, preferred_element_type=jnp.float32
    ).reshape(MODEL_WIDTH, MODEL_WIDTH)
    grad_output_bias = jnp.sum(grad_attention.astype(jnp.float32), axis=(0, 1))
    grad_mixture = jnp.einsum(
        "spd,hed->shpe",
        grad_attention,
        output_back.reshape(HEAD_COUNT, HEAD_SIZE, MODEL_WIDTH),
        preferred_element_type=jnp.float32,
    ).astype(jnp.bfloat16)
    grad_mixed_heads = lax.all_to_all(
        grad_mixture.reshape(SG * HEAD_COUNT, local_pooled // 2, 2 * HEAD_SIZE),
        "seq",
        split_axis=0,
        concat_axis=1,
        tiled=True,
    ).reshape(item_count, PQ, HEAD_SIZE)

    def attend_back(packed):
        query_row, type_row_terms, pair_row, segment_row, type_row, log_row, grad_row = packed
        same_document, same_type = doc_masks(segment_row, type_row)
        scores, key_join = score_block(
            query_row, type_row_terms, pair_row, key_phase, same_document, same_type
        )
        weights = jnp.exp(scores - log_row)
        grad_weights = lax.dot_general(
            grad_row,
            pair_row[:, HEAD_SIZE:],
            (((1,), (1,)), ((), ())),
            preferred_element_type=jnp.float32,
        )
        row_dot = jnp.sum(grad_weights * weights, axis=1, keepdims=True)
        grad_scores = (weights * (grad_weights - row_dot)).astype(jnp.bfloat16)
        grad_query = (
            jnp.dot(grad_scores, key_join, preferred_element_type=jnp.float32) * score_scale
        ).astype(jnp.bfloat16)
        grad_float = grad_scores.astype(jnp.float32) * score_scale
        grad_same = jnp.sum(jnp.where(same_type, grad_float, 0.0), axis=1)
        grad_other = jnp.sum(jnp.where(same_type, 0.0, grad_float), axis=1)
        grad_kinds = jnp.stack([grad_other, grad_same], axis=-1).astype(jnp.bfloat16)
        grad_keys = (
            lax.dot_general(
                grad_scores,
                query_row[:, :HEAD_SIZE],
                (((0,), (0,)), ((), ())),
                preferred_element_type=jnp.float32,
            )
            * score_scale
        )
        grad_values = lax.dot_general(
            weights.astype(jnp.bfloat16),
            grad_row,
            (((0,), (0,)), ((), ())),
            preferred_element_type=jnp.float32,
        )
        return (
            grad_query,
            grad_kinds,
            jnp.concatenate([grad_keys, grad_values], axis=-1).astype(jnp.bfloat16),
        )

    grad_query_heads, grad_type_heads, grad_pair_heads = lax.map(
        attend_back,
        (
            query_heads,
            type_heads,
            pair_heads,
            item_segments,
            item_types,
            log_totals,
            grad_mixed_heads,
        ),
    )
    grad_query_tok, grad_type_tok, grad_pair_tok = (
        lax.all_to_all(grad_query_heads, "seq", split_axis=1, concat_axis=0, tiled=True),
        lax.all_to_all(grad_type_heads, "seq", split_axis=1, concat_axis=0, tiled=True),
        lax.all_to_all(grad_pair_heads, "seq", split_axis=1, concat_axis=0, tiled=True),
    )
    grad_query_join = grad_query_tok.astype(jnp.float32).reshape(
        SG, HEAD_COUNT, local_pooled, 2 * HEAD_SIZE
    )
    grad_content = grad_query_join[..., :HEAD_SIZE]
    grad_first_half = grad_query_join[..., HEAD_SIZE : HEAD_SIZE + half_width]
    grad_second_half = grad_query_join[..., HEAD_SIZE + half_width :]
    grad_relative_terms = jnp.concatenate(
        [
            grad_first_half * query_cos + grad_second_half * query_sin,
            grad_first_half * query_sin - grad_second_half * query_cos,
        ],
        axis=-1,
    )
    grad_shifted = jnp.einsum(
        "shpf,hef->shpe", grad_relative_terms, relative_back, precision=highest
    )
    grad_relative_kernel = jnp.einsum(
        "shpe,shpf->hef", shifted, grad_relative_terms, precision=highest
    )
    grad_type_terms = grad_type_tok.astype(jnp.float32).reshape(SG, HEAD_COUNT, local_pooled, 2)
    grad_typed = jnp.einsum("shpb,hbe->shpe", grad_type_terms, table_back, precision=highest)
    grad_type_embed = jnp.einsum("shpe,shpb->hbe", typed, grad_type_terms, precision=highest)
    query_rows_gradient = (grad_content + grad_shifted + grad_typed).astype(jnp.bfloat16)
    grad_content_bias = jnp.sum(grad_content, axis=(0, 2))
    grad_position_bias = jnp.sum(grad_shifted, axis=(0, 2))
    grad_type_bias = jnp.sum(grad_typed, axis=(0, 2))
    grad_query_weight = jnp.einsum(
        "spd,shpe->dhe", pooled_low, query_rows_gradient, preferred_element_type=jnp.float32
    ).reshape(MODEL_WIDTH, MODEL_WIDTH)
    grad_pooled = grad_first + jnp.einsum(
        "shpe,dhe->spd",
        query_rows_gradient,
        query_back.reshape(MODEL_WIDTH, HEAD_COUNT, HEAD_SIZE),
        preferred_element_type=jnp.float32,
    )
    grad_pairs = grad_pair_tok.reshape(SG, HEAD_COUNT, local_tokens, 2 * HEAD_SIZE)
    key_rows_gradient = grad_pairs[..., :HEAD_SIZE]
    value_rows_gradient = grad_pairs[..., HEAD_SIZE:]
    grad_key_weight = jnp.einsum(
        "ozb,opzx->bpx", tokens, key_rows_gradient, preferred_element_type=jnp.float32
    ).reshape(MODEL_WIDTH, MODEL_WIDTH)
    grad_value_weight = jnp.einsum(
        "ozb,opzx->bpx", tokens, value_rows_gradient, preferred_element_type=jnp.float32
    ).reshape(MODEL_WIDTH, MODEL_WIDTH)
    grad_value_bias = jnp.sum(value_rows_gradient.astype(jnp.float32), axis=(0, 2)).reshape(
        MODEL_WIDTH
    )
    grad_direct = jnp.einsum(
        "mivt,git->mvg",
        key_rows_gradient,
        key_back.reshape(MODEL_WIDTH, HEAD_COUNT, HEAD_SIZE),
        preferred_element_type=jnp.float32,
    )
    grad_direct = grad_direct + jnp.einsum(
        "mivt,git->mvg",
        value_rows_gradient,
        value_back.reshape(MODEL_WIDTH, HEAD_COUNT, HEAD_SIZE),
        preferred_element_type=jnp.float32,
    )
    pool_first = jnp.where(pair_same, 0.5 * grad_pooled, grad_pooled)
    pool_second = jnp.where(pair_same, 0.5 * grad_pooled, 0.0)
    grad_tokens = (
        grad_direct
        + jnp.stack([pool_first, pool_second], axis=2).reshape(SG, local_tokens, MODEL_WIDTH)
    ).astype(jnp.bfloat16)
    summed = lax.psum(
        (
            grad_query_weight,
            grad_key_weight,
            grad_value_weight,
            grad_output_weight,
            grad_inner_weight,
            grad_outer_weight,
            grad_value_bias,
            grad_output_bias,
            grad_inner_bias,
            grad_outer_bias,
            grad_gain_one,
            grad_shift_one,
            grad_gain_two,
            grad_shift_two,
            grad_content_bias,
            grad_position_bias,
            grad_type_bias,
            grad_relative_kernel,
            grad_type_embed,
        ),
        "seq",
    )
    owned = (
        lax.psum_scatter(
            summed[0].astype(jnp.bfloat16), "dp", scatter_dimension=0, tiled=True
        ).astype(jnp.float32),
        lax.psum_scatter(
            summed[1].astype(jnp.bfloat16), "dp", scatter_dimension=0, tiled=True
        ).astype(jnp.float32),
        lax.psum_scatter(
            summed[2].astype(jnp.bfloat16), "dp", scatter_dimension=0, tiled=True
        ).astype(jnp.float32),
        lax.psum_scatter(
            summed[3].astype(jnp.bfloat16), "dp", scatter_dimension=0, tiled=True
        ).astype(jnp.float32),
        lax.psum_scatter(
            summed[4].astype(jnp.bfloat16), "dp", scatter_dimension=0, tiled=True
        ).astype(jnp.float32),
        lax.psum_scatter(
            summed[5].astype(jnp.bfloat16), "dp", scatter_dimension=0, tiled=True
        ).astype(jnp.float32),
        lax.psum_scatter(
            summed[6].astype(jnp.bfloat16), "dp", scatter_dimension=0, tiled=True
        ).astype(jnp.float32),
        lax.psum_scatter(
            summed[7].astype(jnp.bfloat16), "dp", scatter_dimension=0, tiled=True
        ).astype(jnp.float32),
        lax.psum_scatter(
            summed[8].astype(jnp.bfloat16), "dp", scatter_dimension=0, tiled=True
        ).astype(jnp.float32),
        lax.psum_scatter(
            summed[9].astype(jnp.bfloat16), "dp", scatter_dimension=0, tiled=True
        ).astype(jnp.float32),
        lax.psum_scatter(
            summed[10].astype(jnp.bfloat16), "dp", scatter_dimension=0, tiled=True
        ).astype(jnp.float32),
        lax.psum_scatter(
            summed[11].astype(jnp.bfloat16), "dp", scatter_dimension=0, tiled=True
        ).astype(jnp.float32),
        lax.psum_scatter(
            summed[12].astype(jnp.bfloat16), "dp", scatter_dimension=0, tiled=True
        ).astype(jnp.float32),
        lax.psum_scatter(
            summed[13].astype(jnp.bfloat16), "dp", scatter_dimension=0, tiled=True
        ).astype(jnp.float32),
        lax.psum_scatter(
            summed[14].astype(jnp.bfloat16), "dp", scatter_dimension=0, tiled=True
        ).astype(jnp.float32),
        lax.psum_scatter(
            summed[15].astype(jnp.bfloat16), "dp", scatter_dimension=0, tiled=True
        ).astype(jnp.float32),
        lax.psum_scatter(
            summed[16].astype(jnp.bfloat16), "dp", scatter_dimension=0, tiled=True
        ).astype(jnp.float32),
        lax.psum_scatter(
            summed[17].astype(jnp.bfloat16), "dp", scatter_dimension=0, tiled=True
        ).astype(jnp.float32),
        lax.psum_scatter(
            summed[18].astype(jnp.bfloat16), "dp", scatter_dimension=0, tiled=True
        ).astype(jnp.float32),
    )
    return (
        output,
        grad_tokens,
        owned[0],
        owned[1],
        owned[2],
        owned[3],
        owned[4],
        owned[5],
        owned[6],
        owned[7],
        owned[8],
        owned[9],
        owned[10],
        owned[11],
        owned[12],
        owned[13],
        owned[14],
        owned[15],
        owned[16],
        owned[17],
        owned[18],
    )


def solution(mesh):
    return jax.shard_map(
        body,
        mesh=mesh,
        in_specs=(
            P("dp", "seq", None),
            P("dp", "seq"),
            P("dp", "seq"),
            P("dp", "seq", None),
            P("dp", None),
            P("dp", None),
            P("dp", None),
            P("dp", None),
            P("dp", None),
            P("dp", None),
            P("dp"),
            P("dp"),
            P("dp"),
            P("dp"),
            P("dp"),
            P("dp"),
            P("dp"),
            P("dp"),
            P("dp", None),
            P("dp", None),
            P("dp", None),
            P("dp", None, None),
            P("dp", None, None),
        ),
        out_specs=(
            P("dp", "seq", None),
            P("dp", "seq", None),
            P("dp", None),
            P("dp", None),
            P("dp", None),
            P("dp", None),
            P("dp", None),
            P("dp", None),
            P("dp"),
            P("dp"),
            P("dp"),
            P("dp"),
            P("dp"),
            P("dp"),
            P("dp"),
            P("dp"),
            P("dp", None),
            P("dp", None),
            P("dp", None),
            P("dp", None, None),
            P("dp", None, None),
        ),
        check_vma=False,
    )
```

profile of v0, /device:TPU:0, one launch (start us, length us, event | category | flops | bytes accessed | tf_op | source)
XLA Modules:
  0.0 2559.9 jit_solution(6562921722423589004)
XLA Ops:
  11.1 17.6 slice.74
  28.7 11.0 slice.75
  39.8 6.0 all-gather
  45.8 5.4 all-gather.1
  51.1 5.1 all-gather.2
  56.3 5.2 all_gather.83
  61.4 5.6 all_gather.77
  69.6 5.2 add_bitcast_fusion
  78.3 6.0 all-to-all-start.2
  91.1 4.4 all-to-all-start
  102.0 11.8 all-reduce.21
  119.9 4.9 fusion.73
  126.9 10.4 all-gather.13.cloned.1.call-done
  139.6 4.9 convert_bitcast_fusion
  149.9 16.3 all-to-all-done
  166.2 4.8 all-to-all-start.1
  178.7 149.5 %all_gather.81 = s32[8,2048]{1,0:T(8,128)S(1)} all-gather(s32[8,256]{1,0:T(8,128)S(1)} %copy-done.61), channel_id=1, replica_groups=mesh['seq'=8,'dp'=4] {'seq'}, dimensions={1}, use_global_device_ids=true | all-gather | bytes 73728 | tf_op jit(solution)/shard_map/all_gather | solution.py:127
  329.5 31.0 %all_gather.73 = s32[8,2048]{1,0:T(8,128)S(1)} all-gather(s32[8,256]{1,0:T(8,128)S(1)} %copy-done.57), channel_id=1, replica_groups=mesh['seq'=8,'dp'=4] {'seq'}, dimensions={1}, use_global_device_ids=true | all-gather | bytes 73728 | tf_op jit(solution)/shard_map/all_gather | solution.py:126
  366.7 8.8 copy.260
  375.5 118.1 %while.26 = (s32[]{:T(128)}, bf16[12,1024,64]{1,2,0:T(8,128)(2,1)S(1)}, f32[12,1024,1]{1,2,0:T(1,128)}, s32[12,2048]{1,0:T(8,128)}, bf16[12,1024,128]{2,1,0:T(8,...) while((s32[]{:T(128)}, ...), condition=%wide.region_3.4_spmd, body=%wide.region_0.3_spmd.sunk | while | flops 831587328 | bytes 27807876 | solution.py:218
  508.0 5.3 all-gather.3
  513.4 31.6 %all-to-all-done.3 = bf16[12,512,128]{2,0,1:T(8,128)(2,1)S(1)} async-done(((bf16[12,512,128]{2,0,1:T(8,128)(2,1)}), bf16[12,512,128]{2,0,1:T(8,128)(2,1)S(1)}, u32[]{:S(2)}, u32[]{:S(2)}) %all-to-all-start.3) | async-done | bytes 1572896 | tf_op jit(solution)/shard_map/all_to_all | solution.py:221
  546.5 5.1 reshape.370
  551.7 5.1 fusion.157
  557.3 11.1 fusion.59
  568.4 11.9 fusion.158
  586.8 16.4 convert_reduce_fusion
  603.2 11.5 multiply_reduce_fusion.1
  629.9 33.0 %all-to-all-done.4 = bf16[96,64,128]{2,1,0:T(8,128)(2,1)S(1)} async-done(((bf16[96,64,128]{2,1,0:T(8,128)(2,1)}), bf16[96,64,128]{2,1,0:T(8,128)(2,1)S(1)}, u32[]{:S(2)}, u32[]{:S(2)}) %all-to-all-start.4) | async-done | bytes 1572896 | tf_op jit(solution)/shard_map/all_to_all | solution.py:309
  668.1 219.7 %while.27 = (s32[]{:T(128)}, bf16[12,1024,128]{2,1,0:T(8,128)(2,1)}, bf16[12,1024,2]{1,2,0:T(2,128)(2,1)S(1)}, bf16[12,2048,128]{1,2,0:T(8,128)(2,1)}, s32[12,20...) while((s32[]{:T(128)}, ...), condition=%wide.region_16.17_spmd, body=%wide.region_12.16_spmd.sunk | while | flops 1924799488 | bytes 70160576 | solution.py:360
  690.5 4.0 fusion.211
  745.4 4.0 fusion.211
  763.7 4.0 fusion.211
  782.0 4.0 fusion.211
  800.3 4.0 fusion.211
  836.9 4.0 fusion.211
  855.2 4.0 fusion.211
  873.5 4.0 fusion.211
  893.4 6.0 copy.275
  900.1 5.2 all-to-all-start.6
  905.4 12.7 copy.272
  918.1 78.9 %all-to-all-done.6 = bf16[12,1024,128]{2,0,1:T(8,128)(2,1)} async-done(((bf16[12,1024,128]{2,0,1:T(8,128)(2,1)}), bf16[12,1024,128]{2,0,1:T(8,128)(2,1)}, u32[]{:S(2)}, u32[]{:S(2)}) %all-to-all-start.6) | async-done | bytes 3145760 | tf_op jit(solution)/shard_map/all_to_all | solution.py:373
  997.0 5.0 all-to-all-start.5
  1004.5 13.5 convolution_bitcast_fusion
  1020.9 10.7 convolution_bitcast_fusion.1
  1034.9 4.1 fusion.128
  1039.0 4.7 copy.276
  1043.7 5.6 copy.277
  1063.9 5.8 fusion.119
  1069.7 114.3 %all-to-all-done.5 = bf16[12,2048,128]{2,0,1:T(8,128)(2,1)} async-done(((bf16[12,2048,128]{2,0,1:T(8,128)(2,1)}), bf16[12,2048,128]{2,0,1:T(8,128)(2,1)}, u32[]{:S(2)}, u32[]{:S(2)}) %all-to-all-start.5) | async-done | bytes 6291488 | tf_op jit(solution)/shard_map/all_to_all | solution.py:375
  1184.0 12.1 copy.274
  1199.3 6.1 fusion.74
  1205.4 4.0 fusion.76
  1216.9 1101.2 %all-reduce.23 = (bf16[768,768]{1,0:T(8,128)(2,1)}, bf16[768,768]{1,0:T(8,128)(2,1)}, bf16[768,768]{1,0:T(8,128)(2,1)}, bf16[768,768]{1,0:T(8,128)(2,1)}, bf16[7...) all-reduce(f32[768,768]{1,0:T(8,128)} %copy.283, ...), channel_id=1, replica_groups=mesh['seq'=8,'dp'=4] {'seq'}, use_global_device_ids=true, to_apply=%region_17.18 | all-reduce | flops 7139328 | bytes 42835968 | tf_op jit(solution)/shard_map/psum | solution.py:442
  2324.9 4.4 fusion.70
  2330.1 6.3 copy.281
  2336.4 10.7 all-reduce.20
  2356.3 5.3 fusion.94
  2361.7 5.4 fusion.52
  2370.4 21.8 reduce-scatter.12.cloned.1.call-done
  2394.0 26.3 %reduce-scatter.10.cloned.1.call-done = bf16[192,768]{1,0:T(8,128)(2,1)} async-done(((bf16[768,768]{1,0:T(8,128)(2,1)}), bf16[192,768]{1,0:T(8,128)(2,1)}) %reduce-scatter.10.cloned.1.call-update) | async-done | bytes 294928 | tf_op jit(solution)/shard_map/reduce_scatter | solution.py:470
  2422.2 27.2 %reduce-scatter.8.cloned.1.call-done = bf16[192,768]{1,0:T(8,128)(2,1)} async-done(((bf16[768,768]{1,0:T(8,128)(2,1)}), bf16[192,768]{1,0:T(8,128)(2,1)}) %reduce-scatter.8.cloned.1.call-update) | async-done | bytes 294928 | tf_op jit(solution)/shard_map/reduce_scatter | solution.py:467
  2451.2 48.5 %reduce-scatter.18.cloned.1.call-done = bf16[768,768]{1,0:T(8,128)(2,1)} async-done(((bf16[3072,768]{1,0:T(8,128)(2,1)}), bf16[768,768]{1,0:T(8,128)(2,1)}) %reduce-scatter.18.cloned.1.call-update) | async-done | bytes 1179664 | tf_op jit(solution)/shard_map/reduce_scatter | solution.py:482
  2502.5 47.7 %reduce-scatter.16.cloned.1.call-done = bf16[192,3072]{1,0:T(8,128)(2,1)} async-done(((bf16[768,3072]{1,0:T(8,128)(2,1)}), bf16[192,3072]{1,0:T(8,128)(2,1)}) %reduce-scatter.16.cloned.1.call-update) | async-done | bytes 1179664 | tf_op jit(solution)/shard_map/reduce_scatter | solution.py:479
  (736 shorter events, 470.2 us)
Async XLA Ops:
  7.2 21.5 copy-start.15
  7.2 60.0 %all-gather.11.cloned.1.call-start = ((), (), s32[]{:S(2)}) async-start(), calls=%async_computation.15 | async-start | bytes 1474560 | tf_op jit(solution)/shard_map/all_gather | solution.py:92
  11.0 28.7 %copy-start.72 = (f32[3,2,64]{2,1,0:T(2,128)S(1)}, f32[3,2,64]{2,1,0:T(2,128)}, u32[]{:S(2)}) copy-start(f32[3,2,64]{2,1,0:T(2,128)} %param.49) | copy-start | bytes 4612
  11.1 28.7 %copy-start.81 = (f32[3,64]{1,0:T(4,128)S(1)}, f32[3,64]{1,0:T(4,128)}, u32[]{:S(2)}) copy-start(f32[3,64]{1,0:T(4,128)} %param.45) | copy-start | bytes 2308
  11.1 34.7 %copy-start.82 = (f32[3,64]{1,0:T(4,128)S(1)}, f32[3,64]{1,0:T(4,128)}, u32[]{:S(2)}) copy-start(f32[3,64]{1,0:T(4,128)} %param.46) | copy-start | bytes 2308
  11.1 40.1 %copy-start.83 = (f32[3,64]{1,0:T(4,128)S(1)}, f32[3,64]{1,0:T(4,128)}, u32[]{:S(2)}) copy-start(f32[3,64]{1,0:T(4,128)} %param.47) | copy-start | bytes 2308
  11.1 45.1 %copy-start.46 = (f32[3,64,64]{2,1,0:T(8,128)S(1)}, f32[3,64,64]{2,1,0:T(8,128)}, u32[]{:S(2)}) copy-start(f32[3,64,64]{2,1,0:T(8,128)} %param.48) | copy-start | bytes 147460
  56.2 18.6 copy-start.68
  61.4 13.5 copy-start.51
  67.0 17.3 copy-start.17
  67.2 18.9 copy-start.40
  67.2 18.9 copy-start.42
  74.9 11.2 copy-start.7
  78.3 12.8 all-to-all-start.2
  89.3 10.0 copy-start.85
  89.3 10.0 copy-start.86
  89.3 10.0 copy-start.87
  89.3 10.0 copy-start.88
  89.3 10.0 copy-start.89
  89.4 10.1 copy-start.90
  89.4 10.1 copy-start.80
  91.1 75.1 %all-to-all-start = ((bf16[96,128,128]{1,2,0:T(8,128)(2,1)}), bf16[96,128,128]{1,2,0:T(8,128)(2,1)S(1)}, u32[]{:S(2)}, u32[]{:S(2)}) async-start(bf16[96,128,128]{1,2,0:T(8,128)(2,1)} %pad_maximum_fusion.5), calls=%async_computation | async-start | bytes 6291456 | tf_op jit(solution)/shard_map/all_to_all | solution.py:189
  95.5 22.0 all-gather.15.cloned.1.call-start
  97.4 39.8 %all-gather.13.cloned.1.call-start = ((), (), s32[]{:S(2)}) async-start(), calls=%async_computation.16 | async-start | bytes 1474560 | tf_op jit(solution)/shard_map/all_gather | solution.py:93
  166.2 200.5 %all-to-all-start.1 = ((bf16[96,256,128]{1,2,0:T(8,128)(2,1)}), bf16[96,256,128]{1,2,0:T(8,128)(2,1)}, u32[]{:S(2)}, u32[]{:S(2)}) async-start(bf16[96,256,128]{1,2,0:T(8,128)(2,1)} %pad_maximum_fusion.3), calls=%async_computation.1 | async-start | bytes 12582912 | tf_op jit(solution)/shard_map/all_to_all | solution.py:191
  171.0 380.7 %all-gather.17.cloned.1.call-start = ((), (), s32[]{:S(2)}) async-start(), calls=%async_computation.18 | async-start | bytes 1474560 | tf_op jit(solution)/shard_map/all_gather | solution.py:95
  172.8 384.5 %all-gather.19.cloned.1.call-start = ((), (), s32[]{:S(2)}) async-start(), calls=%async_computation.19 | async-start | bytes 5898240 | tf_op jit(solution)/shard_map/all_gather | solution.py:96
  175.8 153.7 %copy-start.57 = (s32[8,256]{1,0:T(8,128)S(1)}, s32[8,256]{1,0:T(8,128)}, u32[]{:S(2)}) copy-start(s32[8,256]{1,0:T(8,128)} %param.28) | copy-start | bytes 24580
  175.8 392.6 %all-gather.21.cloned.1.call-start = ((), (), s32[]{:S(2)}) async-start(), calls=%async_computation.20 | async-start | bytes 5898240 | tf_op jit(solution)/shard_map/all_gather | solution.py:97
  366.7 8.8 copy-start.24
  366.7 8.8 copy-start.32
  504.3 40.7 %all-to-all-start.3 = ((bf16[12,512,128]{2,0,1:T(8,128)(2,1)}), bf16[12,512,128]{2,0,1:T(8,128)(2,1)S(1)}, u32[]{:S(2)}, u32[]{:S(2)}) async-start(bf16[12,512,128]{2,0,1:T(8,128)(2,1)} %copy.266), calls=%async_computation.3 | async-start | bytes 4194304 | tf_op jit(solution)/shard_map/all_to_all | solution.py:221
  507.9 106.9 %copy-start.34 = (f32[768]{0:T(1024)}, f32[768]{0:T(1024)S(1)}, u32[]{:S(2)}) copy-start(f32[768]{0:T(1024)S(1)} %convert_element_type.369) | copy-start | bytes 9220
  507.9 95.3 %copy-start.47 = (f32[768]{0:T(1024)}, f32[768]{0:T(1024)S(1)}, u32[]{:S(2)}) copy-start(f32[768]{0:T(1024)S(1)} %convert_element_type.381) | copy-start | bytes 9220
  508.0 60.5 %copy-start.38 = (f32[768]{0:T(1024)}, f32[768]{0:T(1024)S(1)}, u32[]{:S(2)}) copy-start(f32[768]{0:T(1024)S(1)} %convert_element_type.371) | copy-start | bytes 9220
  513.3 73.5 %copy-start.59 = (f32[4,1,768]{2,1,0:T(1,128)}, f32[4,1,768]{2,1,0:T(1,128)S(1)}, u32[]{:S(2)}) copy-start(f32[4,1,768]{2,1,0:T(1,128)S(1)} %convert_element_type.445) | copy-start | bytes 36868
  556.8 58.0 %copy-start.2 = (f32[8,128,768]{2,1,0:T(8,128)}, f32[8,128,768]{2,1,0:T(8,128)S(1)}, u32[]{:S(2)}) copy-start(f32[8,128,768]{2,1,0:T(8,128)S(1)} %get-tuple-element.286) | copy-start | bytes 9437188
  556.8 58.0 %copy-start.30 = (f32[8,128]{1,0:T(8,128)}, f32[8,128]{1,0:T(8,128)S(1)}, u32[]{:S(2)}) copy-start(f32[8,128]{1,0:T(8,128)S(1)} %broadcast_multiply_fusion.5) | copy-start | bytes 12292
  557.3 57.5 %copy-start.36 = (f32[8,128]{1,0:T(8,128)}, f32[8,128]{1,0:T(8,128)S(1)}, u32[]{:S(2)}) copy-start(f32[8,128]{1,0:T(8,128)S(1)} %add_rsqrt_fusion.1) | copy-start | bytes 12292
  580.4 22.8 copy-start
  580.4 22.8 copy-start.44
  582.9 20.3 copy-start.49
  586.8 16.4 copy-start.21
  603.2 11.6 copy-start.12
  625.9 37.0 %all-to-all-start.4 = ((bf16[96,64,128]{2,1,0:T(8,128)(2,1)}), bf16[96,64,128]{2,1,0:T(8,128)(2,1)S(1)}, u32[]{:S(2)}, u32[]{:S(2)}) async-start(bf16[96,64,128]{2,1,0:T(8,128)(2,1)} %reshape.372), calls=%async_computation.4 | async-start | bytes 3145728 | tf_op jit(solution)/shard_map/all_to_all | solution.py:309
  889.8 10.4 all-to-all-start.7
  900.1 96.9 %all-to-all-start.6 = ((bf16[12,1024,128]{2,0,1:T(8,128)(2,1)}), bf16[12,1024,128]{2,0,1:T(8,128)(2,1)}, u32[]{:S(2)}, u32[]{:S(2)}) async-start(bf16[12,1024,128]{2,0,1:T(8,128)(2,1)} %copy.275), calls=%async_computation.6 | async-start | bytes 8388608 | tf_op jit(solution)/shard_map/all_to_all | solution.py:373
  918.1 83.9 %copy-start.9 = (bf16[8,12,128,64]{3,2,1,0:T(8,128)(2,1)S(1)}, bf16[8,12,128,64]{3,2,1,0:T(8,128)(2,1)}, u32[]{:S(2)}) copy-start(bf16[8,12,128,64]{3,2,1,0:T(8,128)(2,1)} %reshape.370) | copy-start | bytes 4718596
  997.0 187.0 %all-to-all-start.5 = ((bf16[12,2048,128]{2,0,1:T(8,128)(2,1)}), bf16[12,2048,128]{2,0,1:T(8,128)(2,1)}, u32[]{:S(2)}, u32[]{:S(2)}) async-start(bf16[12,2048,128]{2,0,1:T(8,128)(2,1)} %copy.272), calls=%async_computation.5 | async-start | bytes 16777216 | tf_op jit(solution)/shard_map/all_to_all | solution.py:375
  1002.0 1365.1 %reduce-scatter.20.cloned.1.call-start = ((), (), s32[]{:S(2)}) async-start(), calls=%async_computation.27 | async-start | bytes 245760 | tf_op jit(solution)/shard_map/reduce_scatter | solution.py:518
  1004.5 13.5 copy-start.23
  1004.5 13.5 copy-start.27
  1196.2 9.2 slice-start
  2318.1 50.6 %reduce-scatter.14.cloned.1.call-start = ((), (), s32[]{:S(2)}) async-start(), calls=%async_computation.24 | async-start | bytes 1474560 | tf_op jit(solution)/shard_map/reduce_scatter | solution.py:476
  2318.8 73.4 %reduce-scatter.12.cloned.1.call-start = ((), (), s32[]{:S(2)}) async-start(), calls=%async_computation.23 | async-start | bytes 1474560 | tf_op jit(solution)/shard_map/reduce_scatter | solution.py:473
  2319.5 100.8 %reduce-scatter.10.cloned.1.call-start = ((), (), s32[]{:S(2)}) async-start(), calls=%async_computation.22 | async-start | bytes 1474560 | tf_op jit(solution)/shard_map/reduce_scatter | solution.py:470
  2320.1 129.3 %reduce-scatter.8.cloned.1.call-start = ((), (), s32[]{:S(2)}) async-start(), calls=%async_computation.21 | async-start | bytes 1474560 | tf_op jit(solution)/shard_map/reduce_scatter | solution.py:467
  2320.9 178.8 %reduce-scatter.18.cloned.1.call-start = ((), (), s32[]{:S(2)}) async-start(), calls=%async_computation.26 | async-start | bytes 5898240 | tf_op jit(solution)/shard_map/reduce_scatter | solution.py:482
  2321.5 228.7 %reduce-scatter.16.cloned.1.call-start = ((), (), s32[]{:S(2)}) async-start(), calls=%async_computation.25 | async-start | bytes 5898240 | tf_op jit(solution)/shard_map/reduce_scatter | solution.py:479
  2330.0 24.6 copy-start.1
  2330.0 24.6 copy-start.45
  2330.0 24.5 copy-start.48
  2330.0 24.5 copy-start.50
  2347.1 9.2 copy-start.29
  (66 other events, 229.5 us)
Sparse Core Ops, SparseCore 0:
  10.2 20.1 all-gather.10
  98.5 19.0 all-gather.14
  119.7 17.4 all-gather.12
  173.6 18.7 all-gather.16
  193.9 37.4 all-gather.18
  232.8 37.4 all-gather.20
  2318.2 17.1 reduce-scatter.19
  2337.9 25.7 reduce-scatter.13
  2366.4 25.7 reduce-scatter.11
  2394.6 25.7 reduce-scatter.9
  2423.7 25.6 reduce-scatter.7
  2451.8 47.8 reduce-scatter.17
  2502.4 47.8 reduce-scatter.15
where the time goes:
time: 2580 us; the launch traced here: 2560 us
  blocking collectives  1340 us (52%)
  waiting for transfers between devices  466 us (18%)
  matrix products  323 us (13%)
  local copies, waits for them, and re-layouts  248 us (10%)
  other arithmetic  129 us (5%)
  starting transfers between devices  37.2 us (1%)
    psum x1, blocking collectives, body(): lax.psum((grad_query_weight, grad_key_weight, grad_value_weight, grad_out...  1100 us
    all_gather x1, blocking collectives, body(): lax.all_gather(token_types, 'seq', axis=1, tiled=True)  149 us
    all_to_all x1, waiting for transfers between devices, body(): lax.all_to_all(grad_pair_heads, 'seq', split_axis=1, concat_axis=0, tiled...  114 us
    dot_general x24, matrix products, score_block(): lax.dot_general(query_row, key_join, (((1,), (1,)), ((), ())), preferred_...  90.1 us
    all_to_all x1, waiting for transfers between devices, body(): lax.all_to_all(grad_query_heads, 'seq', split_axis=1, concat_axis=0, tile...  78.9 us
  transfers between devices with their start and end apart: 21, of which 14 were waited for; matrix products, arithmetic and copies ran while one was open for 14% of the time, Pallas kernels for 0%

commit v1 on v0

--- a/solution.py
+++ b/solution.py
@@ -4,6 +4,8 @@
 import jax
 import jax.numpy as jnp
 from jax import lax
+from jax.experimental import pallas as pl
+from jax.experimental.pallas import tpu as pltpu
 from jax.sharding import PartitionSpec as P
 
 MODEL_WIDTH = 768
@@ -547,9 +549,657 @@
     )
 
 
+BF16 = jnp.bfloat16
+F32 = jnp.float32
+PAIRS = HEAD_COUNT // 2
+LANES = 2 * HEAD_SIZE
+ROWS = 256
+FAR = -(2.0**100)
+FF = 3072
+NN = (((1,), (0,)), ((), ()))
+NT = (((1,), (1,)), ((), ()))
+TN = (((0,), (0,)), ((), ()))
+
+
+def mm(left, right, dims=NN):
+    return lax.dot_general(left, right, dims, preferred_element_type=F32)
+
+
+def split(value):
+    high = value.astype(BF16)
+    return high, (value - high.astype(F32)).astype(BF16)
+
+
+def lane_ids(rows):
+    return lax.broadcasted_iota(jnp.int32, (rows, LANES), 1)
+
+
+def attend_kernel(
+    query_ref,
+    key_ref,
+    value_ref,
+    map_ref,
+    map_add_ref,
+    content_ref,
+    query_side_ref,
+    key_side_ref,
+    phase_ref,
+    cos_ref,
+    sin_ref,
+    mixture_ref,
+    join_ref,
+    key_join,
+    value_join,
+):
+    query = query_ref[...]
+    high, low = split(query)
+    terms = mm(jnp.concatenate([high, low], axis=1), map_ref[0]) + map_add_ref[0]
+    lane = lane_ids(PQ)
+    left = lane < HEAD_SIZE
+    content = query + content_ref[...]
+    position = terms[:, :LANES] * cos_ref[...] + terms[:, LANES : 2 * LANES] * sin_ref[...]
+    side = query_side_ref[...]
+    typed = (lane >= 3) & (lane < 6)
+    scale = HEAD_SIZE ** (-0.5)
+    for h in range(2):
+        first, second = (content, position) if h == 0 else (position, content)
+        join_ref[h, :, :LANES] = (jnp.where(left, first, second) * scale).astype(BF16)
+        base = 2 * LANES * (h + 1)
+        same = terms[:, base : base + LANES]
+        other = terms[:, base + LANES : base + 2 * LANES]
+        kind = jnp.where(side > 0.5, same, other) * scale
+        join_ref[h, :, LANES:] = jnp.where(typed, kind, side).astype(BF16)
+    key_left = lane_ids(LEN) < HEAD_SIZE
+    key_join[:, LANES:] = key_side_ref[...]
+    value_join[:, :LANES] = value_ref[...]
+    value_join[:, LANES:] = key_side_ref[...]
+    tile_lane = lane_ids(ROWS)
+    for h in range(2):
+        pieces = (key_ref[...], phase_ref[...]) if h == 0 else (phase_ref[...], key_ref[...])
+        key_join[:, :LANES] = jnp.where(key_left, *pieces)
+        for i in range(PQ // ROWS):
+            rows = slice(i * ROWS, (i + 1) * ROWS)
+            scores = mm(join_ref[h, rows, :], key_join[...], NT)
+            top = jnp.max(scores, axis=1, keepdims=True)
+            weights = jnp.exp(scores - top).astype(BF16)
+            mixed = mm(weights, value_join[...])
+            total = mixed[:, LANES + 6 : LANES + 7]
+            result = (mixed[:, :LANES] / total).astype(BF16)
+            if h == 0:
+                mixture_ref[rows, :] = result
+            else:
+                mixture_ref[rows, :] = jnp.where(
+                    tile_lane < HEAD_SIZE, mixture_ref[rows, :], result
+                )
+            shift = -(top + jnp.log(total))
+            one = shift.astype(BF16).astype(F32)
+            two = (shift - one).astype(BF16).astype(F32)
+            three = shift - one - two
+            extra = jnp.where(tile_lane == 6, one, jnp.where(tile_lane == 7, two, three))
+            kept = join_ref[h, rows, LANES:].astype(F32)
+            inside = (tile_lane >= 6) & (tile_lane < 9)
+            join_ref[h, rows, LANES:] = jnp.where(inside, extra, kept).astype(BF16)
+
+
+def attend_forward(query, pairs, maps, map_add, content, query_side, key_side, phase, cosm, sinm):
+    whole = lambda shape: pl.BlockSpec(shape, lambda i: (0, 0))
+    return pl.pallas_call(
+        attend_kernel,
+        grid=(PAIRS,),
+        in_specs=[
+            pl.BlockSpec((PQ, LANES), lambda i: (0, i)),
+            pl.BlockSpec((LEN, LANES), lambda i: (0, i)),
+            pl.BlockSpec((LEN, LANES), lambda i: (0, i + PAIRS)),
+            pl.BlockSpec((1, 2 * LANES, 6 * LANES), lambda i: (i, 0, 0)),
+            pl.BlockSpec((1, 1, 6 * LANES), lambda i: (i, 0, 0)),
+            pl.BlockSpec((1, LANES), lambda i: (0, i)),
+            whole((PQ, LANES)),
+            whole((LEN, LANES)),
+            whole((LEN, LANES)),
+            whole((PQ, LANES)),
+            whole((PQ, LANES)),
+        ],
+        out_specs=[
+            pl.BlockSpec((PQ, LANES), lambda i: (0, i)),
+            pl.BlockSpec((2, PQ, 2 * LANES), lambda i: (i, 0, 0)),
+        ],
+        out_shape=[
+            jax.ShapeDtypeStruct((PQ, MODEL_WIDTH), BF16),
+            jax.ShapeDtypeStruct((HEAD_COUNT, PQ, 2 * LANES), BF16),
+        ],
+        scratch_shapes=[
+            pltpu.VMEM((LEN, 2 * LANES), BF16),
+            pltpu.VMEM((LEN, 2 * LANES), BF16),
+        ],
+        cost_estimate=pl.CostEstimate(
+            flops=4 * HEAD_COUNT * PQ * LEN * 256,
+            bytes_accessed=20_000_000,
+            transcendentals=HEAD_COUNT * PQ * LEN,
+        ),
+        compiler_params=pltpu.CompilerParams(vmem_limit_bytes=56 * 2**20),
+        name="attend_forward",
+    )(query, pairs, pairs, maps, map_add, content, query_side, key_side, phase, cosm, sinm)
+
+
+def attend_back_kernel(
+    join_ref,
+    key_ref,
+    value_ref,
+    query_ref,
+    mixture_ref,
+    grad_ref,
+    map_back_ref,
+    rows_ref,
+    query_side_ref,
+    key_side_ref,
+    phase_ref,
+    cos_ref,
+    sin_ref,
+    grad_query_ref,
+    grad_key_ref,
+    grad_value_ref,
+    sums_ref,
+    grad_map_ref,
+    key_join,
+    value_join,
+    key_total,
+    value_total,
+    join_grads,
+):
+    scale = HEAD_SIZE ** (-0.5)
+    key_left = lane_ids(LEN) < HEAD_SIZE
+    tile_lane = lane_ids(ROWS)
+    key_join[:, LANES:] = key_side_ref[...]
+    value_join[:, :LANES] = value_ref[...]
+    value_join[:, LANES:] = key_side_ref[...]
+    for h in range(2):
+        pieces = (key_ref[...], phase_ref[...]) if h == 0 else (phase_ref[...], key_ref[...])
+        key_join[:, :LANES] = jnp.where(key_left, *pieces)
+        mine = (tile_lane < HEAD_SIZE) if h == 0 else (tile_lane >= HEAD_SIZE)
+        part = slice(h * HEAD_SIZE, (h + 1) * HEAD_SIZE)
+        for i in range(PQ // ROWS):
+            rows = slice(i * ROWS, (i + 1) * ROWS)
+            join = join_ref[h, rows, :]
+            grad = jnp.where(mine, grad_ref[rows, :].astype(F32), 0.0)
+            dot = -jnp.sum(grad * mixture_ref[rows, :].astype(F32), axis=1, keepdims=True)
+            one = dot.astype(BF16).astype(F32)
+            two = (dot - one).astype(BF16).astype(F32)
+            three = dot - one - two
+            extra = jnp.where(tile_lane == 6, one, jnp.where(tile_lane == 7, two, three))
+            inside = (tile_lane >= 6) & (tile_lane < 9)
+            extra = jnp.where(inside, extra, 0.0)
+            grad_low = grad.astype(BF16)
+            weights = jnp.exp(mm(join, key_join[...], NT))
+            slope = mm(
+                jnp.concatenate([grad_low, extra.astype(BF16)], axis=1), value_join[...], NT
+            )
+            low_slope = (weights * slope).astype(BF16)
+            low_weights = weights.astype(BF16)
+            join_grads[h, rows, :] = mm(low_slope, key_join[...])
+            to_key = mm(join_ref[h, rows, part], low_slope, TN)
+            to_value = mm(grad_ref[rows, part], low_weights, TN)
+            if i == 0:
+                key_total[part, :] = to_key
+                value_total[part, :] = to_value
+            else:
+                key_total[part, :] += to_key
+                value_total[part, :] += to_value
+    grad_key_ref[...] = key_total[...].T.astype(BF16)
+    grad_value_ref[...] = value_total[...].T.astype(BF16)
+    lane = lane_ids(PQ)
+    left = lane < HEAD_SIZE
+    typed = (lane >= 3) & (lane < 6)
+    rounded = [(join_grads[h, :, :LANES] * scale).astype(BF16).astype(F32) for h in range(2)]
+    content = jnp.where(left, rounded[0], rounded[1])
+    position = jnp.where(left, rounded[1], rounded[0])
+    turned = jnp.concatenate([position * cos_ref[...], position * sin_ref[...]], axis=1)
+    turned_high, turned_low = split(turned)
+    shifted_grad = mm(turned_high, map_back_ref[0]) + mm(turned_low, map_back_ref[0])
+    side = query_side_ref[...]
+    sames, others = [], []
+    for h in range(2):
+        kinds = jnp.where(typed, join_grads[h, :, LANES:], 0.0)
+        same = jnp.sum(jnp.where(side > 0.5, kinds, 0.0), axis=1, keepdims=True)
+        other = jnp.sum(jnp.where(side > 0.5, 0.0, kinds), axis=1, keepdims=True)
+        sames.append((same * scale).astype(BF16).astype(F32))
+        others.append((other * scale).astype(BF16).astype(F32))
+    same = jnp.where(left, sames[0], sames[1])
+    other = jnp.where(left, others[0], others[1])
+    position_add = rows_ref[0, 0:1, :]
+    type_add = rows_ref[0, 1:2, :]
+    type_other = rows_ref[0, 2:3, :]
+    type_same = rows_ref[0, 3:4, :]
+    typed_grad = same * type_same + other * type_other
+    grad_query_ref[...] = (content + shifted_grad + typed_grad).astype(BF16)
+    query = query_ref[...]
+    shifted_high, shifted_low = split(query + position_add)
+    grad_map_ref[0] = (
+        mm(shifted_high, turned_high, TN)
+        + mm(shifted_low, turned_high, TN)
+        + mm(shifted_high, turned_low, TN)
+    )
+    kinds = query + type_add
+    row = lambda v: jnp.sum(v, axis=0, keepdims=True)
+    sums_ref[0, 0:1, :] = row(content)
+    sums_ref[0, 1:2, :] = row(shifted_grad)
+    sums_ref[0, 2:3, :] = row(typed_grad)
+    sums_ref[0, 3:4, :] = row(kinds * other)
+    sums_ref[0, 4:5, :] = row(kinds * same)
+    sums_ref[0, 5:6, :] = row(grad_value_ref[...].astype(F32))
+
+
+def attend_backward(
+    join, pairs, query, mixture, grad, map_back, rows, query_side, key_side, phase, cosm, sinm
+):
+    whole = lambda shape: pl.BlockSpec(shape, lambda i: (0, 0))
+    return pl.pallas_call(
+        attend_back_kernel,
+        grid=(PAIRS,),
+        in_specs=[
+            pl.BlockSpec((2, PQ, 2 * LANES), lambda i: (i, 0, 0)),
+            pl.BlockSpec((LEN, LANES), lambda i: (0, i)),
+            pl.BlockSpec((LEN, LANES), lambda i: (0, i + PAIRS)),
+            pl.BlockSpec((PQ, LANES), lambda i: (0, i)),
+            pl.BlockSpec((PQ, LANES), lambda i: (0, i)),
+            pl.BlockSpec((PQ, LANES), lambda i: (0, i)),
+            pl.BlockSpec((1, 2 * LANES, LANES), lambda i: (i, 0, 0)),
+            pl.BlockSpec((1, 8, LANES), lambda i: (i, 0, 0)),
+            whole((PQ, LANES)),
+            whole((LEN, LANES)),
+            whole((LEN, LANES)),
+            whole((PQ, LANES)),
+            whole((PQ, LANES)),
+        ],
+        out_specs=[
+            pl.BlockSpec((PQ, LANES), lambda i: (0, i)),
+            pl.BlockSpec((LEN, LANES), lambda i: (0, i)),
+            pl.BlockSpec((LEN, LANES), lambda i: (0, i)),
+            pl.BlockSpec((1, 8, LANES), lambda i: (i, 0, 0)),
+            pl.BlockSpec((1, LANES, 2 * LANES), lambda i: (i, 0, 0)),
+        ],
+        out_shape=[
+            jax.ShapeDtypeStruct((PQ, MODEL_WIDTH), BF16),
+            jax.ShapeDtypeStruct((LEN, MODEL_WIDTH), BF16),
+            jax.ShapeDtypeStruct((LEN, MODEL_WIDTH), BF16),
+            jax.ShapeDtypeStruct((PAIRS, 8, LANES), F32),
+            jax.ShapeDtypeStruct((PAIRS, LANES, 2 * LANES), F32),
+        ],
+        scratch_shapes=[
+            pltpu.VMEM((LEN, 2 * LANES), BF16),
+            pltpu.VMEM((LEN, 2 * LANES), BF16),
+            pltpu.VMEM((LANES, LEN), F32),
+            pltpu.VMEM((LANES, LEN), F32),
+            pltpu.VMEM((2, PQ, 2 * LANES), F32),
+        ],
+        cost_estimate=pl.CostEstimate(
+            flops=10 * HEAD_COUNT * PQ * LEN * 256,
+            bytes_accessed=32_000_000,
+            transcendentals=HEAD_COUNT * PQ * LEN,
+        ),
+        compiler_params=pltpu.CompilerParams(vmem_limit_bytes=58 * 2**20),
+        name="attend_backward",
+    )(
+        join,
+        pairs,
+        pairs,
+        query,
+        mixture,
+        grad,
+        map_back,
+        rows,
+        query_side,
+        key_side,
+        phase,
+        cosm,
+        sinm,
+    )
+
+
+def swap_halves(value, axis):
+    first, second = jnp.split(value, 2, axis=axis)
+    return jnp.concatenate([second, first], axis=axis)
+
+
+def pair_maps(relative, table):
+    relative = relative.reshape(PAIRS, 2, HEAD_SIZE, HEAD_SIZE)
+    nothing = jnp.zeros((PAIRS, HEAD_SIZE, HEAD_SIZE), F32)
+    turned = swap_halves(relative, 3)
+
+    def crossed(value):
+        top = jnp.concatenate([nothing, value[:, 0]], axis=2)
+        bottom = jnp.concatenate([value[:, 1], nothing], axis=2)
+        return jnp.concatenate([top, bottom], axis=1)
+
+    plain, swapped = crossed(relative), crossed(turned)
+    table = table.reshape(PAIRS, 2, 2, HEAD_SIZE)
+    columns = jnp.arange(LANES)
+    wanted = ((columns >= 3) & (columns < 6)).astype(F32)
+    kinds = []
+    for h in range(2):
+        for b in (1, 0):
+            vector = table[:, h, b]
+            zero = jnp.zeros_like(vector)
+            full = jnp.concatenate([vector, zero] if h == 0 else [zero, vector], axis=1)
+            kinds.append(full[:, :, None] * wanted[None, None, :])
+    return plain, swapped, kinds
+
+
+def sequence_body(
+    tokens,
+    segments,
+    token_types,
+    cotangent,
+    query_weight,
+    key_weight,
+    value_weight,
+    output_weight,
+    inner_weight,
+    outer_weight,
+    value_bias,
+    output_bias,
+    inner_bias,
+    outer_bias,
+    attention_norm_gain,
+    first_shift,
+    second_gain,
+    second_shift,
+    content_bias,
+    position_bias,
+    type_bias,
+    relative_kernel,
+    type_embed,
+):
+    owners = lax.axis_size("dp")
+    part = MODEL_WIDTH // owners
+    low = lambda value: value.astype(BF16)
+    even_segments, odd_segments = segments[:, 0::2], segments[:, 1::2]
+    labels = jnp.stack(
+        [
+            segments[:, :128],
+            segments[:, 128:],
+            token_types[:, :128],
+            token_types[:, 128:],
+            even_segments,
+            token_types[:, 0::2],
+            (even_segments == odd_segments).astype(jnp.int32),
+        ],
+        axis=1,
+    )
+    labels = lax.all_to_all(labels, "seq", split_axis=0, concat_axis=0, tiled=True)
+    rows = lax.all_to_all(tokens, "seq", split_axis=0, concat_axis=0, tiled=True)
+    small = jnp.concatenate(
+        [
+            low(value).reshape(-1)
+            for value in (
+                value_bias,
+                output_bias,
+                outer_bias,
+                attention_norm_gain,
+                first_shift,
+                second_gain,
+                second_shift,
+                content_bias,
+                position_bias,
+                type_bias,
+                inner_bias,
+                relative_kernel,
+                type_embed,
+            )
+        ]
+    )
+    small = lax.all_gather(small.reshape(1, -1), "dp", axis=0, tiled=True)
+    first = jnp.concatenate([low(query_weight), low(key_weight), low(value_weight)], axis=1)
+    first = lax.all_gather(first, "dp", axis=0, tiled=True)
+    next_weights = jnp.concatenate([low(output_weight), low(inner_weight)], axis=1)
+    next_weights = lax.all_gather(next_weights, "dp", axis=0, tiled=True)
+    outer_low = lax.all_gather(low(outer_weight), "dp", axis=0, tiled=True)
+
+    def take(start, size):
+        return small[:, start : start + size].astype(F32)
+
+    vectors = [take(part * j, part).reshape(1, MODEL_WIDTH) for j in range(10)]
+    (
+        value_add,
+        output_add,
+        outer_add,
+        gain_one,
+        shift_one,
+        gain_two,
+        shift_two,
+        content_add,
+        position_add,
+        type_add,
+    ) = vectors
+    place = 10 * part
+    inner_add = take(place, FF // owners).reshape(1, FF)
+    place += FF // owners
+    kernel_size = HEAD_COUNT * HEAD_SIZE * HEAD_SIZE // owners
+    relative = take(place, kernel_size).reshape(HEAD_COUNT, HEAD_SIZE, HEAD_SIZE)
+    place += kernel_size
+    table = take(place, HEAD_COUNT * 2 * HEAD_SIZE // owners).reshape(HEAD_COUNT, 2, HEAD_SIZE)
+
+    segment_row = labels[:, 0:2].reshape(LEN)
+    type_row = labels[:, 2:4].reshape(LEN)
+    query_segments = labels[:, 4].reshape(PQ)
+    query_types = labels[:, 5].reshape(PQ)
+    pair_same = labels[:, 6] > 0
+
+    first_doc, last_doc = segment_row[0], segment_row[LEN - 1]
+    first_type = type_row[0]
+    last_type = jnp.max(jnp.where(type_row == first_type, -1, type_row))
+
+    def classes(values, start, end):
+        return jnp.where(values == start, 0, jnp.where(values == end, 2, 1))[:, None]
+
+    columns = jnp.arange(LANES, dtype=jnp.int32)[None, :]
+    key_side = (
+        (columns == classes(segment_row, first_doc, last_doc))
+        | (columns == 3 + classes(type_row, first_type, last_type))
+        | ((columns >= 6) & (columns < 9))
+    ).astype(BF16)
+    query_docs = classes(query_segments, first_doc, last_doc)
+    query_side = jnp.where(
+        columns < 3,
+        jnp.where(columns == query_docs, 0.0, FAR),
+        (columns == 3 + classes(query_types, first_type, last_type)).astype(F32),
+    )
+    frequency = frequencies()
+    key_angle = jnp.arange(LEN, dtype=F32)[:, None] * frequency[None, :]
+    phase = jnp.concatenate([jnp.cos(key_angle), jnp.sin(key_angle)], axis=1).astype(BF16)
+    phase = jnp.concatenate([phase, phase], axis=1)
+    query_angle = (2.0 * jnp.arange(PQ, dtype=F32))[:, None] * frequency[None, :]
+    cos, sin = jnp.cos(query_angle), jnp.sin(query_angle)
+    cosm = jnp.concatenate([cos, -cos, cos, -cos], axis=1)
+    sinm = jnp.concatenate([sin, sin, sin, sin], axis=1)
+
+    plain, swapped, kinds = pair_maps(relative, table)
+    stacked = jnp.concatenate([plain, swapped, *kinds], axis=2)
+    maps = low(jnp.concatenate([stacked, stacked], axis=1))
+    pair_vector = lambda vector: vector.reshape(PAIRS, 1, LANES)
+    position_pairs, type_pairs = pair_vector(position_add), pair_vector(type_add)
+    product = partial(jnp.einsum, "pke,pef->pkf", precision=highest)
+    map_add = jnp.concatenate(
+        [
+            product(position_pairs, stacked[:, :, : 2 * LANES]),
+            product(type_pairs, stacked[:, :, 2 * LANES :]),
+        ],
+        axis=2,
+    )
+    map_back = low(
+        jnp.concatenate([plain.transpose(0, 2, 1), swapped.transpose(0, 2, 1)], axis=1)
+    )
+    table_pairs = table.reshape(PAIRS, 2, 2, HEAD_SIZE).transpose(0, 2, 1, 3)
+    table_pairs = table_pairs.reshape(PAIRS, 2, LANES)
+    row_terms = jnp.concatenate(
+        [position_pairs, type_pairs, table_pairs, jnp.zeros((PAIRS, 4, LANES), F32)], axis=1
+    )
+
+    block = 2 * rows.shape[1] // 2
+    pooled_block = block // 2
+    at = jnp.arange(block, dtype=jnp.int32)[None, None, :]
+    want = 2 * jnp.arange(pooled_block, dtype=jnp.int32)[None, :, None]
+    half = jnp.where(pair_same, 0.5, 1.0)[:, :, None]
+    pool = jnp.where(at == want, half, jnp.where(at == want + 1, 1.0 - half, 0.0)).astype(BF16)
+    pool = jnp.where(at == want + 1, jnp.where(pair_same, 0.5, 0.0)[:, :, None].astype(BF16), pool)
+
+    pooled = jnp.einsum("cpt,ctd->cpd", pool, rows, preferred_element_type=F32)
+    pooled = pooled.reshape(PQ, MODEL_WIDTH)
+    pooled_low = low(pooled)
+    token_rows = rows.reshape(LEN, MODEL_WIDTH)
+    query = mm(pooled_low, first[:, :MODEL_WIDTH])
+    pair_add = jnp.concatenate([jnp.zeros_like(value_add), value_add], axis=1)
+    pairs = low(mm(token_rows, first[:, MODEL_WIDTH:]) + pair_add)
+    mixture, join = attend_forward(
+        query, pairs, maps, map_add, content_add, query_side, key_side, phase, cosm, sinm
+    )
+
+    cotangent, _ = lax.optimization_barrier((cotangent, pairs))
+    cotangent = lax.all_to_all(cotangent, "seq", split_axis=0, concat_axis=0, tiled=True)
+    upstream = cotangent.reshape(PQ, MODEL_WIDTH).astype(F32)
+
+    output_low, inner_low = next_weights[:, :MODEL_WIDTH], next_weights[:, MODEL_WIDTH:]
+    attention = mm(mixture, output_low) + output_add
+    hidden, normed_one, inverse_one = norm_forward(pooled + attention, gain_one, shift_one)
+    hidden_low = low(hidden)
+    expanded = mm(hidden_low, inner_low) + inner_add
+    active = low(jax.nn.gelu(expanded, approximate=True))
+    branch = mm(active, outer_low) + outer_add
+    result, normed_two, inverse_two = norm_forward(hidden + branch, gain_two, shift_two)
+    output = low(result).reshape(SG, PQ // SG, MODEL_WIDTH)
+    output = lax.all_to_all(output, "seq", split_axis=0, concat_axis=0, tiled=True)
+
+    total = lambda value: jnp.sum(value, axis=0)
+    grad_gain_two = total(upstream * normed_two)
+    grad_shift_two = total(upstream)
+    grad_second = norm_backward(upstream, normed_two, inverse_two, gain_two)
+    grad_branch = low(grad_second)
+    grad_outer_weight = mm(active, grad_branch, TN)
+    grad_outer_bias = total(grad_branch.astype(F32))
+    grad_active = mm(grad_branch, outer_low, NT)
+    _, gelu_pull = jax.vjp(partial(jax.nn.gelu, approximate=True), expanded)
+    grad_expanded = low(gelu_pull(grad_active)[0])
+    grad_inner_weight = mm(hidden_low, grad_expanded, TN)
+    grad_inner_bias = total(grad_expanded.astype(F32))
+
+    def shared(value):
+        value = lax.psum_scatter(low(value), "dp", scatter_dimension=0, tiled=True)
+        return lax.psum(value, "seq").astype(F32)
+
+    owned_outer = shared(grad_outer_weight)
+    owned_inner = shared(grad_inner_weight)
+    grad_hidden = grad_second + mm(grad_expanded, inner_low, NT)
+    grad_gain_one = total(grad_hidden * normed_one)
+    grad_shift_one = total(grad_hidden)
+    grad_first = norm_backward(grad_hidden, normed_one, inverse_one, gain_one)
+    grad_attention = low(grad_first)
+    grad_output_weight = mm(mixture, grad_attention, TN)
+    grad_output_bias = total(grad_attention.astype(F32))
+    grad_mixture = low(mm(grad_attention, output_low, NT))
+
+    grad_query, grad_key, grad_value, sums, grad_map = attend_backward(
+        join,
+        pairs,
+        query,
+        mixture,
+        grad_mixture,
+        map_back,
+        row_terms,
+        query_side,
+        key_side,
+        phase,
+        cosm,
+        sinm,
+    )
+    grad_query_weight = mm(pooled_low, grad_query, TN)
+    grad_key_weight = mm(token_rows, grad_key, TN)
+    grad_value_weight = mm(token_rows, grad_value, TN)
+    grad_pooled = grad_first + mm(grad_query, first[:, :MODEL_WIDTH], NT)
+    grad_direct = mm(grad_key, first[:, MODEL_WIDTH : 2 * MODEL_WIDTH], NT)
+    grad_direct = grad_direct + mm(grad_value, first[:, 2 * MODEL_WIDTH :], NT)
+    high_pooled, low_pooled = split(grad_pooled.reshape(SG, pooled_block, MODEL_WIDTH))
+    spread = partial(jnp.einsum, "cpt,cpd->ctd", preferred_element_type=F32)
+    spread_sum = spread(pool, high_pooled) + spread(pool, low_pooled)
+    grad_tokens = low(grad_direct.reshape(SG, block, MODEL_WIDTH) + spread_sum)
+    grad_tokens = lax.all_to_all(grad_tokens, "seq", split_axis=0, concat_axis=0, tiled=True)
+
+    crossed = grad_map.reshape(PAIRS, 2, HEAD_SIZE, 2, 2, HEAD_SIZE)
+    grad_relative = jnp.stack(
+        [
+            crossed[:, h, :, 0, 1 - h] + swap_halves(crossed[:, h, :, 1, 1 - h], 2)
+            for h in range(2)
+        ],
+        axis=1,
+    ).reshape(HEAD_COUNT, HEAD_SIZE, HEAD_SIZE)
+    grad_table = sums[:, 3:5].reshape(PAIRS, 2, 2, HEAD_SIZE).transpose(0, 2, 1, 3)
+    sum_row = lambda j: sums[:, j].reshape(owners, -1)
+    small_grads = jnp.concatenate(
+        [
+            value.reshape(owners, -1)
+            for value in (
+                sum_row(5),
+                grad_output_bias,
+                grad_outer_bias,
+                grad_gain_one,
+                grad_shift_one,
+                grad_gain_two,
+                grad_shift_two,
+                sum_row(0),
+                sum_row(1),
+                sum_row(2),
+                grad_inner_bias,
+                grad_relative,
+                grad_table,
+            )
+        ],
+        axis=1,
+    )
+    wide = 4 * MODEL_WIDTH
+    small_rows = small_grads.shape[1] // wide
+    late = jnp.concatenate(
+        [grad_query_weight, grad_key_weight, grad_value_weight, grad_output_weight], axis=1
+    ).reshape(owners, part, wide)
+    spare = jnp.zeros((owners, -small_rows % 8, wide), F32)
+    late = jnp.concatenate(
+        [late, small_grads.reshape(owners, small_rows, wide), spare], axis=1
+    ).reshape(-1, wide)
+    owned_late = shared(late)
+    squares = [owned_late[:part, j * MODEL_WIDTH : (j + 1) * MODEL_WIDTH] for j in range(4)]
+    small_owned = owned_late[part : part + small_rows].reshape(-1)
+    place = 0
+    pieces = []
+    for size in [part] * 10 + [FF // owners, kernel_size, HEAD_COUNT * 2 * HEAD_SIZE // owners]:
+        pieces.append(small_owned[place : place + size])
+        place += size
+    heads = HEAD_COUNT // owners
+    return (
+        output.reshape(SG, PQ // SG, MODEL_WIDTH),
+        grad_tokens,
+        squares[0],
+        squares[1],
+        squares[2],
+        squares[3],
+        owned_inner,
+        owned_outer,
+        pieces[0],
+        pieces[1],
+        pieces[10],
+        pieces[2],
+        pieces[3],
+        pieces[4],
+        pieces[5],
+        pieces[6],
+        pieces[7].reshape(heads, HEAD_SIZE),
+        pieces[8].reshape(heads, HEAD_SIZE),
+        pieces[9].reshape(heads, HEAD_SIZE),
+        pieces[11].reshape(heads, HEAD_SIZE, HEAD_SIZE),
+        pieces[12].reshape(heads, 2, HEAD_SIZE),
+    )
+
+
 def solution(mesh):
+    whole = mesh.shape["seq"] == SG and mesh.shape["dp"] == 4
     return jax.shard_map(
-        body,
+        sequence_body if whole else body,
         mesh=mesh,
         in_specs=(
             P("dp", "seq", None),

time: 2580 us -> 661 us (0.26)
  blocking collectives: 1340 us -> 6.1 us
  waiting for transfers between devices: 466 us -> 244 us
  matrix products: 323 us -> 126 us
  local copies, waits for them, and re-layouts: 248 us -> 57.3 us
  Pallas kernels: 0 us -> 119 us
  other arithmetic: 129 us -> 60.8 us
    psum x1 -> x0, blocking collectives: 1100 us -> none  [body(): lax.psum((grad_query_weight, grad_key_weight, grad_value_weight, grad_out...]
    all_gather x8 -> x1, blocking collectives: 213 us -> 6.1 us  [sequence_body(): small = lax.all_gather(small.reshape(1, -1), 'dp', axis=0, tiled=True)]
    dot_general x108 -> x22, matrix products: 323 us -> 126 us  [the longest x17 115 us: mm(): return lax.dot_general(left, right, dims, preferred_element_type=F32)]
    reduce_scatter x7 -> x3, waiting for transfers between devices: 172 us -> 4.23 us  [shared(): value = lax.psum_scatter(low(value), 'dp', scatter_dimension=0, tiled=True)]
    all_to_all x8 -> x5, waiting for transfers between devices: 277 us -> 152 us  [the longest x1 105 us: sequence_body(): lax.all_to_all(grad_tokens, 'seq', split_axis=0, concat_axis=0, tiled=True)]
    pallas_call x0 -> x2, Pallas kernels: none -> 119 us  [the longest x1 73.7 us: attend_backward(): pl.pallas_call(attend_back_kernel, grid=(PAIRS,), in_specs=[pl.BlockSpec(...]
    psum x0 -> x1, waiting for transfers between devices: none -> 87.4 us  [shared(): return lax.psum(value, 'seq').astype(F32)]
    reduce_sum x28 -> x5, other arithmetic: 70.2 us -> 7.97 us  [the longest x4 7.6 us: sequence_body(): total = lambda value: jnp.sum(value, axis=0)]
  transfers between devices with their start and end apart: 21 -> 12, of which waited for: 14 -> 5; matrix products, arithmetic and copies ran while one was open for 14% -> 28% of each run, Pallas kernels for 0% -> 18%
where the time goes in v1:
time: 661 us; the launch traced here: 656 us
  waiting for transfers between devices  244 us (37%)
  matrix products  126 us (19%)
  Pallas kernels  119 us (18%)
  other arithmetic  60.8 us (9%)
  local copies, waits for them, and re-layouts  57.3 us (9%)
  starting transfers between devices  27.4 us (4%)
  between operations  15.8 us (2%)
    dot_general x17, matrix products, mm(): return lax.dot_general(left, right, dims, preferred_element_type=F32)  115 us
    all_to_all x1, waiting for transfers between devices, sequence_body(): lax.all_to_all(grad_tokens, 'seq', split_axis=0, concat_axis=0, tiled=True)  105 us
    psum x1, waiting for transfers between devices, shared(): return lax.psum(value, 'seq').astype(F32)  87.4 us
    pallas_call x1, Pallas kernels, attend_backward(): pl.pallas_call(attend_back_kernel, grid=(PAIRS,), in_specs=[pl.BlockSpec(...  73.7 us
    pallas_call x1, Pallas kernels, attend_forward(): pl.pallas_call(attend_kernel, grid=(PAIRS,), in_specs=[pl.BlockSpec((PQ,...  45.1 us
    all_to_all x1, waiting for transfers between devices, sequence_body(): lax.all_to_all(tokens, 'seq', split_axis=0, concat_axis=0, tiled=True)  26.6 us
    all_to_all x1, waiting for transfers between devices, sequence_body(): lax.all_to_all(output, 'seq', split_axis=0, concat_axis=0, tiled=True)  20.6 us
    unnamed x120, local copies, waits for them, and re-layouts  14.2 us
  transfers between devices with their start and end apart: 12, of which 5 were waited for; matrix products, arithmetic and copies ran while one was open for 28% of the time, Pallas kernels for 18%

profile of v1, /device:TPU:0, one launch (start us, length us, event | category | flops | bytes accessed | tf_op | source)
XLA Modules:
  0.0 656.3 jit_solution(6619417256846553199)
XLA Ops:
  7.3 1.2 convert_element_type.190
  12.0 1.2 pad_maximum_fusion.2
  14.7 7.3 %all-to-all-start = ((s32[8,7,128]{2,1,0:T(8,128)}), s32[8,7,128]{2,1,0:T(8,128)S(1)}, u32[]{:S(2)}, u32[]{:S(2)}) async-start(s32[8,7,128]{2,1,0:T(8,128)} %stack.41), calls=%async_computation | async-start | bytes 65536 | tf_op jit(solution)/shard_map/all_to_all | solution.py:928
  24.0 6.1 all-gather
  38.3 6.4 all-to-all-start.1
  44.8 2.5 fusion.45
  49.5 1.3 reshape.533.content_ref
  57.6 1.5 broadcast_multiply_fusion.1
  59.1 1.5 broadcast_multiply_fusion
  60.5 2.0 fusion.24
  62.6 1.6 pad_maximum_fusion.1
  64.2 4.3 copy.118.map_ref
  69.2 1.9 multiply_sine_fusion
  71.1 1.8 pad_maximum_fusion.5
  73.0 4.0 cosine_convert_fusion
  77.0 1.4 pad_maximum_fusion.4.phase_ref
  78.9 1.3 fusion.111
  80.9 2.6 add_bitcast_fusion
  83.5 2.6 select_add_fusion
  87.3 2.1 fusion.39.key_side_ref
  89.4 26.6 %all-to-all-done.1 = bf16[8,256,768]{2,1,0:T(8,128)(2,1)S(1)} async-done(((bf16[8,256,768]{2,1,0:T(8,128)(2,1)}), bf16[8,256,768]{2,1,0:T(8,128)(2,1)S(1)}, u32[]{:S(2)}, u32[]{:S(2)}) %all-to-all-start.1) | async-done | bytes 3145760 | tf_op jit(solution)/shard_map/all_to_all | solution.py:929
  116.0 9.7 %fusion.7.key_ref.value_ref = bf16[2048,1536]{1,0:T(8,128)(2,1)} fusion(bf16[2048,768]{1,0:T(8,128)(2,1)S(1)} %bitcast.138, f32[1536]{0:T(1024)S(1)} %convert_reduce_fusion, bf16[768,2304]{1,0:T(8,128)(2,1)} %all-gather.5.cloned.1.call-done), kind=kOutput, calls=%fused_computation.11 | convolution fusion | flops 4838129664 | bytes 11802624 | tf_op jit(solution)/shard_map/dot_general | solution.py:565
  125.6 3.6 all-to-all-start.3
  129.4 2.6 fusion.59
  132.2 5.3 fusion.43.query_ref
  137.5 45.1 %attend_forward.1 = (bf16[1024,768]{1,0:T(8,128)(2,1)}, bf16[12,1024,256]{2,1,0:T(8,128)(2,1)}) custom-call(f32[1024,768]{1,0:T(8,128)} %fusion.43.query_ref, bf16[2048,1536]{1,0:T(8,128)(2,1)} %fusion.7.key_ref.value_ref, bf16[2048,1536]{1,0:T(8,128)(2,1)} %fusion.7.key_ref.value_ref, bf16[6,256,768]{2,1,0:T(8,128)(2,1)} %copy.118.map_ref, ...), custom_call_target="tpu_custom_call" | custom-call | flops 25769803776 | bytes 20000000 | tf_op jit(solution)/shard_map/attend_forward/pallas_call | solution.py:646
  183.1 4.4 fusion.117
  189.1 8.3 %fusion.10 = f32[1024,3072]{1,0:T(8,128)} fusion(bf16[768,3840]{1,0:T(8,128)(2,1)S(1)} %bitcast.168, f32[1024,768]{1,0:T(8,128)S(1)} %get-tuple-element.130, f32[768]{0:T(1024)S(1)} %reshape.536, f32[768]{0:T(1024)S(1)} %reshape.535, f32[1024]{0:T(1024)S(1)} %add_rsqrt_fusion.1, f32[1024]{0:T(1024)S(1)} %broadcast_multiply_fusion.8), kind=kOutput, calls=%fused_computation.19 | convolution fusion | flops 4835770368 | bytes 20463616 | tf_op jit(solution)/shard_map/dot_general | solution.py:565
  197.4 13.1 %fusion.118 = (f32[1024]{0:T(1024)S(1)}, f32[1024,768]{1,0:T(8,128)S(1)}) fusion(f32[768]{0:T(1024)S(1)} %reshape.538, bf16[3072,768]{1,0:T(8,128)(2,1)} %all-gather.9.cloned.1.call-done, f32[1024,3072]{1,0:T(8,128)} %fusion.10, f32[3072]{0:T(1024)S(1)} %reshape.537, f32[768]{0:T(1024)S(1)} %reshape.536, f32[768]{0:T(1024)S(1)} %reshape.535, ...), kind=kOutput, calls=%fused_computation.234 | convolution fusion | flops 4868799488 | bytes 23626752 | tf_op jit(solution)/shard_map/dot_general | solution.py:565
  211.0 2.7 fusion.18
  214.9 1.6 copy-done.8
  216.7 9.4 %convolution_convert_fusion = bf16[3072,768]{1,0:T(8,128)(2,1)} fusion(f32[1024,768]{1,0:T(8,128)S(1)} %get-tuple-element.51, f32[1024,3072]{1,0:T(8,128)S(1)} %copy-done.53, f32[3072]{0:T(1024)S(1)} %reshape.537), kind=kOutput, calls=%fused_computation.13 | convolution fusion | flops 4866441216 | bytes 20459520 | tf_op jit(solution)/shard_map/dot_general | solution.py:565
  229.6 19.8 %fusion.119 = (bf16[3072]{0:T(1024)(128)(2,1)S(1)}, bf16[1024,3072]{1,0:T(8,128)(2,1)}) fusion(f32[1024,3072]{1,0:T(8,128)} %fusion.10, f32[3072]{0:T(1024)S(1)} %reshape.537, bf16[3072,768]{1,0:T(8,128)(2,1)} %all-gather.9.cloned.1.call-done, f32[1024,768]{1,0:T(8,128)} %copy-done.8), kind=kOutput, calls=%fused_computation.235 | convolution fusion | flops 4901827584 | bytes 26757120 | tf_op jit(solution)/shard_map/dot_general | solution.py:565
  249.4 10.9 %multiply_reduce_fusion = (bf16[768]{0:T(1024)(128)(2,1)S(1)}, f32[1024]{0:T(1024)S(1)}, f32[1024]{0:T(1024)S(1)}, bf16[768]{0:T(1024)(128)(2,1)S(1)}, f32[1024,768]{1,0:T(8,128)}) fusion(f32[1024,768]{1,0:T(8,128)S(1)} %copy-done.4, f32[1024]{0:T(1024)S(1)} %add_rsqrt_fusion.1, f32[1024]{0:T(1024)S(1)} %broadcast_multiply_fusion.8, f32[768]{0:T(1024)S(1)} %reshape.535, ...), kind=kOutput, calls=%fused_computation.34 | convolution fusion | flops 4839698432 | bytes 20469760 | tf_op jit(solution)/shard_map/dot_general | solution.py:565
  260.6 3.4 convert_reduce_fusion.1
  264.1 10.4 %convolution_convert_fusion.1 = bf16[768,3072]{1,0:T(8,128)(2,1)} fusion(bf16[1024,3072]{1,0:T(8,128)(2,1)} %get-tuple-element.135, f32[1024,768]{1,0:T(8,128)} %copy-done.3, f32[768]{0:T(1024)S(1)} %reshape.536, f32[768]{0:T(1024)S(1)} %reshape.535, f32[1024]{0:T(1024)S(1)} %add_rsqrt_fusion.1, f32[1024]{0:T(1024)S(1)} %broadcast_multiply_fusion.8), kind=kOutput, calls=%fused_computation.14 | convolution fusion | flops 4838129664 | bytes 14170112 | tf_op jit(solution)/shard_map/dot_general | solution.py:565
  274.8 3.9 convolution_convert_fusion.2.grad_ref
  278.6 73.7 %attend_backward.1 = (bf16[1024,768]{1,0:T(8,128)(2,1)}, bf16[2048,768]{1,0:T(8,128)(2,1)}, bf16[2048,768]{1,0:T(8,128)(2,1)}, f32[6,8,128]{2,1,0:T(8,128)}, f32[6,128,256]{2,1,0:T(8,128)}) custom-call(bf16[12,1024,256]{2,1,0:T(8,128)(2,1)} %get-tuple-element.30.join_ref, bf16[2048,1536]{1,0:T(8,128)(2,1)} %fusion.7.key_ref.value_ref, ...), custom_call_target="tpu_custom_call" | custom-call | flops 64424509440 | bytes 32000000 | tf_op jit(solution)/shard_map/attend_backward/pallas_call | solution.py:795
  353.7 3.4 convolution_convert_fusion.6
  357.1 1.5 convolution_convert_fusion.3
  360.0 2.8 fusion.32
  362.8 2.8 fusion.33
  365.6 2.5 pad_maximum_fusion
  368.0 6.6 %copy.120 = bf16[768,3072]{1,0:T(8,128)(2,1)} copy(bf16[768,3072]{0,1:T(8,128)(2,1)} %pad_maximum_fusion) | data formatting | bytes 9437184 | tf_op jit(solution)/shard_map/concatenate | solution.py:1158
  374.6 3.4 reshape.522
  378.1 2.2 fusion.105
  382.7 6.0 maximum_maximum_fusion
  388.7 5.9 all-to-all-start.2
  394.7 3.9 convolution_add_fusion.1
  399.7 1.6 copy-done.22
  402.4 2.7 fusion.35
  405.1 2.9 convolution_add_fusion
  408.0 2.8 add_convert_fusion.1
  410.8 20.6 %all-to-all-done.2 = bf16[8,128,768]{2,1,0:T(8,128)(2,1)} async-done(((bf16[8,128,768]{2,1,0:T(8,128)(2,1)}), bf16[8,128,768]{2,1,0:T(8,128)(2,1)}, u32[]{:S(2)}, u32[]{:S(2)}) %all-to-all-start.2) | async-done | bytes 1572896 | tf_op jit(solution)/shard_map/all_to_all | solution.py:1069
  431.4 3.7 all-to-all-start.4
  435.2 4.2 reduce-scatter.4.cloned.1.call-done
  439.4 105.2 %all-to-all-done.4 = bf16[8,256,768]{2,1,0:T(8,128)(2,1)S(1)} async-done(((bf16[8,256,768]{2,1,0:T(8,128)(2,1)}), bf16[8,256,768]{2,1,0:T(8,128)(2,1)S(1)}, u32[]{:S(2)}, u32[]{:S(2)}) %all-to-all-start.4) | async-done | bytes 3145760 | tf_op jit(solution)/shard_map/all_to_all | solution.py:1123
  544.6 87.4 %all-reduce.12.cloned.1.call-done = (bf16[200,3072]{1,0:T(8,128)(2,1)}, bf16[192,3072]{1,0:T(8,128)(2,1)}, bf16[768,768]{1,0:T(8,128)(2,1)}) async-done(((bf16[200,3072]{1,0:T(8,128)(2,1)}, bf16[192,3072]{1,0:T(8,128)(2,1)}, bf16[768,768]{1,0:T(8,128)(2,1)}), (bf16[200,3072]{1,0:T(8,128)(2,1)}, bf16[192,3072]{1,0:T(8,128)(2,1)}, bf16[768,768]{1,0:T(8,128)(2,1)})) %all-reduce.12.cloned.1.call-update) | async-done | bytes 3588112 | tf_op jit(solution)/shard_map/psum | solution.py:1086
  634.9 2.7 fusion.106
  638.3 1.4 slice.357
  640.2 2.9 convert_element_type.234
  643.2 1.6 convert_element_type.236
  644.7 2.7 copy.169
  647.4 1.7 copy.170
  (284 shorter events, 46.4 us)
Async XLA Ops:
  7.2 4.6 copy-start.17
  7.2 4.6 copy-start.9
  7.2 82.2 %all-gather.5.cloned.1.call-start = ((), (), s32[]{:S(2)}) async-start(), calls=%async_computation.8 | async-start | bytes 4423680 | tf_op jit(solution)/shard_map/all_gather | solution.py:952
  11.7 171.3 %all-gather.7.cloned.1.call-start = ((), (), s32[]{:S(2)}) async-start(), calls=%async_computation.9 | async-start | bytes 7372800 | tf_op jit(solution)/shard_map/all_gather | solution.py:954
  11.8 1.6 copy-start.32
  11.8 2.0 copy-start.33
  12.0 10.0 %copy-start.10 = (f32[768,768]{1,0:T(8,128)S(1)}, f32[768,768]{1,0:T(8,128)}, u32[]{:S(2)}) copy-start(f32[768,768]{1,0:T(8,128)} %param.32) | copy-start | bytes 7077892
  13.3 10.0 %copy-start.41 = (f32[192]{0:T(256)S(1)}, f32[192]{0:T(256)}, u32[]{:S(2)}) copy-start(f32[192]{0:T(256)} %param.33) | copy-start | bytes 2308
  13.3 10.0 %copy-start.42 = (f32[192]{0:T(256)S(1)}, f32[192]{0:T(256)}, u32[]{:S(2)}) copy-start(f32[192]{0:T(256)} %param.34) | copy-start | bytes 2308
  13.3 10.0 %copy-start.43 = (f32[192]{0:T(256)S(1)}, f32[192]{0:T(256)}, u32[]{:S(2)}) copy-start(f32[192]{0:T(256)} %param.36) | copy-start | bytes 2308
  13.3 10.0 %copy-start.44 = (f32[192]{0:T(256)S(1)}, f32[192]{0:T(256)}, u32[]{:S(2)}) copy-start(f32[192]{0:T(256)} %param.37) | copy-start | bytes 2308
  13.3 10.1 %copy-start.45 = (f32[192]{0:T(256)S(1)}, f32[192]{0:T(256)}, u32[]{:S(2)}) copy-start(f32[192]{0:T(256)} %param.38) | copy-start | bytes 2308
  13.3 10.1 %copy-start.46 = (f32[192]{0:T(256)S(1)}, f32[192]{0:T(256)}, u32[]{:S(2)}) copy-start(f32[192]{0:T(256)} %param.39) | copy-start | bytes 2308
  13.3 10.1 %copy-start.47 = (f32[192]{0:T(256)S(1)}, f32[192]{0:T(256)}, u32[]{:S(2)}) copy-start(f32[192]{0:T(256)} %param.40) | copy-start | bytes 2308
  13.3 10.1 %copy-start.38 = (f32[3,64]{1,0:T(4,128)S(1)}, f32[3,64]{1,0:T(4,128)}, u32[]{:S(2)}) copy-start(f32[3,64]{1,0:T(4,128)} %param.41) | copy-start | bytes 2308
  13.3 10.2 %copy-start.39 = (f32[3,64]{1,0:T(4,128)S(1)}, f32[3,64]{1,0:T(4,128)}, u32[]{:S(2)}) copy-start(f32[3,64]{1,0:T(4,128)} %param.42) | copy-start | bytes 2308
  13.3 10.3 %copy-start.40 = (f32[3,64]{1,0:T(4,128)S(1)}, f32[3,64]{1,0:T(4,128)}, u32[]{:S(2)}) copy-start(f32[3,64]{1,0:T(4,128)} %param.43) | copy-start | bytes 2308
  13.3 10.3 %copy-start.37 = (f32[3,2,64]{2,1,0:T(2,128)S(1)}, f32[3,2,64]{2,1,0:T(2,128)}, u32[]{:S(2)}) copy-start(f32[3,2,64]{2,1,0:T(2,128)} %param.45) | copy-start | bytes 4612
  13.3 10.4 %copy-start.36 = (f32[768]{0:T(1024)S(1)}, f32[768]{0:T(1024)}, u32[]{:S(2)}) copy-start(f32[768]{0:T(1024)} %param.35) | copy-start | bytes 9220
  13.4 10.4 %copy-start.25 = (f32[3,64,64]{2,1,0:T(8,128)S(1)}, f32[3,64,64]{2,1,0:T(8,128)}, u32[]{:S(2)}) copy-start(f32[3,64,64]{2,1,0:T(8,128)} %param.44) | copy-start | bytes 147460
  14.7 23.0 %all-to-all-start = ((s32[8,7,128]{2,1,0:T(8,128)}), s32[8,7,128]{2,1,0:T(8,128)S(1)}, u32[]{:S(2)}, u32[]{:S(2)}) async-start(s32[8,7,128]{2,1,0:T(8,128)} %stack.41), calls=%async_computation | async-start | bytes 65536 | tf_op jit(solution)/shard_map/all_to_all | solution.py:928
  22.0 175.4 %all-gather.9.cloned.1.call-start = ((), (), s32[]{:S(2)}) async-start(), calls=%async_computation.10 | async-start | bytes 5898240 | tf_op jit(solution)/shard_map/all_gather | solution.py:955
  23.2 12.3 %copy-start.35 = (f32[128]{0:T(128)}, f32[128]{0:T(128)S(1)}, u32[]{:S(2)}) copy-start(f32[128]{0:T(128)S(1)} %and_convert_fusion) | copy-start | bytes 1540
  32.4 3.1 copy-start.5
  32.8 4.9 copy-start.6
  32.8 4.9 copy-start.7
  38.3 77.6 %all-to-all-start.1 = ((bf16[8,256,768]{2,1,0:T(8,128)(2,1)}), bf16[8,256,768]{2,1,0:T(8,128)(2,1)S(1)}, u32[]{:S(2)}, u32[]{:S(2)}) async-start(bf16[8,256,768]{2,1,0:T(8,128)(2,1)} %param.23), calls=%async_computation.1 | async-start | bytes 6291456 | tf_op jit(solution)/shard_map/all_to_all | solution.py:929
  60.5 2.1 copy-start.12
  69.2 9.3 %copy-start.24 = (s32[8,7,128]{2,1,0:T(8,128)S(1)}, s32[8,7,128]{2,1,0:T(8,128)}, u32[]{:S(2)}) copy-start(s32[8,7,128]{2,1,0:T(8,128)} %copy-done.23) | copy-start | bytes 86020
  72.9 56.4 %copy-start.18 = (pred[128,256]{0,1:T(8,128)(4,1)}, pred[128,256]{0,1:T(8,128)(4,1)S(1)}, u32[]{:S(2)}) copy-start(pred[128,256]{0,1:T(8,128)(4,1)S(1)} %get-tuple-element.136) | copy-start | bytes 98308
  73.0 56.4 %copy-start.20 = (pred[128,256]{0,1:T(8,128)(4,1)}, pred[128,256]{0,1:T(8,128)(4,1)S(1)}, u32[]{:S(2)}) copy-start(pred[128,256]{0,1:T(8,128)(4,1)S(1)} %get-tuple-element.137) | copy-start | bytes 98308
  80.9 48.5 %copy-start.26 = (bf16[8,128]{1,0:T(8,128)(2,1)}, bf16[8,128]{1,0:T(8,128)(2,1)S(1)}, u32[]{:S(2)}) copy-start(bf16[8,128]{1,0:T(8,128)(2,1)S(1)} %get-tuple-element.54) | copy-start | bytes 6148
  80.9 48.5 %copy-start.28 = (bf16[8,128]{1,0:T(8,128)(2,1)}, bf16[8,128]{1,0:T(8,128)(2,1)S(1)}, u32[]{:S(2)}) copy-start(bf16[8,128]{1,0:T(8,128)(2,1)S(1)} %select_bitcast_fusion.1) | copy-start | bytes 6148
  80.9 48.5 %copy-start.30 = (bf16[8,128]{1,0:T(8,128)(2,1)}, bf16[8,128]{1,0:T(8,128)(2,1)S(1)}, u32[]{:S(2)}) copy-start(bf16[8,128]{1,0:T(8,128)(2,1)S(1)} %broadcast_subtract_fusion) | copy-start | bytes 6148
  116.0 9.7 %copy-start = (bf16[8,256,768]{2,1,0:T(8,128)(2,1)}, bf16[8,256,768]{2,1,0:T(8,128)(2,1)S(1)}, u32[]{:S(2)}) copy-start(bf16[8,256,768]{2,1,0:T(8,128)(2,1)S(1)} %all-to-all-done.1) | copy-start | bytes 9437188
  125.6 57.0 %all-to-all-start.3 = ((bf16[8,128,768]{2,1,0:T(8,128)(2,1)}), bf16[8,128,768]{2,1,0:T(8,128)(2,1)S(1)}, u32[]{:S(2)}, u32[]{:S(2)}) async-start(bf16[8,128,768]{2,1,0:T(8,128)(2,1)} %param.26), calls=%async_computation.3 | async-start | bytes 3145728 | tf_op jit(solution)/shard_map/all_to_all | solution.py:1057
  129.3 305.8 %reduce-scatter.8.cloned.1.call-start = ((), (), s32[]{:S(2)}) async-start(), calls=%async_computation.13 | async-start | bytes 5898240 | tf_op jit(solution)/shard_map/reduce_scatter | solution.py:1085
  132.0 5.5 copy-start.2
  132.2 5.3 copy-start.13
  183.0 6.1 slice-start
  183.1 6.0 slice-start.1
  187.5 1.6 copy-start.3
  211.0 5.7 copy-start.53
  214.9 1.7 copy-start.8
  226.2 1.9 copy-start.34
  226.2 209.0 %reduce-scatter.6.cloned.1.call-start = ((), (), s32[]{:S(2)}) async-start(), calls=%async_computation.12 | async-start | bytes 5898240 | tf_op jit(solution)/shard_map/reduce_scatter | solution.py:1085
  229.6 19.8 %copy-start.4 = (f32[1024,768]{1,0:T(8,128)S(1)}, f32[1024,768]{1,0:T(8,128)}, u32[]{:S(2)}) copy-start(f32[1024,768]{1,0:T(8,128)} %copy-done.3) | copy-start | bytes 9437188
  274.5 164.8 %reduce-scatter.4.cloned.1.call-start = ((), (), s32[]{:S(2)}) async-start(), calls=%async_computation.11 | async-start | bytes 6144000 | tf_op jit(solution)/shard_map/reduce_scatter | solution.py:1085
  353.7 3.4 copy-start.52
  357.1 1.9 copy-start.1
  357.1 2.8 copy-start.50
  360.0 2.8 copy-start.48
  388.7 42.7 %all-to-all-start.2 = ((bf16[8,128,768]{2,1,0:T(8,128)(2,1)}), bf16[8,128,768]{2,1,0:T(8,128)(2,1)}, u32[]{:S(2)}, u32[]{:S(2)}) async-start(bf16[8,128,768]{2,1,0:T(8,128)(2,1)} %bitcast.141), calls=%async_computation.2 | async-start | bytes 3145728 | tf_op jit(solution)/shard_map/all_to_all | solution.py:1069
  394.6 4.0 copy-start.19
  394.6 4.0 copy-start.21
  394.7 4.0 copy-start.27
  394.7 4.0 copy-start.29
  394.7 4.0 copy-start.31
  398.7 2.6 copy-start.22
  398.7 3.7 copy-start.51
  402.4 2.7 copy-start.49
  431.4 113.2 %all-to-all-start.4 = ((bf16[8,256,768]{2,1,0:T(8,128)(2,1)}), bf16[8,256,768]{2,1,0:T(8,128)(2,1)S(1)}, u32[]{:S(2)}, u32[]{:S(2)}) async-start(bf16[8,256,768]{2,1,0:T(8,128)(2,1)} %add_convert_fusion.1), calls=%async_computation.4 | async-start | bytes 6291456 | tf_op jit(solution)/shard_map/all_to_all | solution.py:1123
  435.1 196.9 %all-reduce.12.cloned.1.call-start = ((), (), s32[]{:S(2)}) async-start(), calls=%async_computation.14 | async-start | bytes 7176192 | tf_op jit(solution)/shard_map/psum | solution.py:1086
  638.3 4.9 copy-start.14
  (4 other events, 3.9 us)
Sparse Core Ops, SparseCore 0:
  11.8 34.1 all-gather.4
  47.5 44.1 all-gather.6
  93.3 37.4 all-gather.8
  226.3 49.0 reduce-scatter.7
  278.0 47.8 reduce-scatter.5
  388.8 50.4 reduce-scatter.3
  443.8 188.0 all-reduce.11

commit v2 on v1

--- a/solution.py
+++ b/solution.py
@@ -855,6 +855,546 @@
     )
 
 
+FF_STEP = 512
+FF_TILES = FF // FF_STEP
+ROW_TILES = PQ // ROWS
+
+
+def row_norm(value):
+    centred = value - jnp.mean(value, axis=1, keepdims=True)
+    inverse = lax.rsqrt(jnp.mean(centred * centred, axis=1, keepdims=True) + norm_eps)
+    return centred * inverse, inverse
+
+
+def row_norm_back(scaled, normed, inverse):
+    along = jnp.mean(scaled * normed, axis=1, keepdims=True)
+    return inverse * (scaled - jnp.mean(scaled, axis=1, keepdims=True) - normed * along)
+
+
+def gelu_pieces(value):
+    rate = math.sqrt(2.0 / math.pi)
+    square = value * value
+    bend = jnp.tanh(rate * value * (1.0 + 0.044715 * square))
+    half = 0.5 * (1.0 + bend)
+    slope = half + (0.5 * rate) * value * (1.0 - bend * bend) * (1.0 + 0.134145 * square)
+    return value * half, slope
+
+
+def mlp_kernel(
+    mixture_ref,
+    pooled_ref,
+    upstream_ref,
+    output_weight_ref,
+    inner_weight_ref,
+    outer_weight_ref,
+    vectors_ref,
+    inner_add_ref,
+    output_ref,
+    grad_mixture_ref,
+    grad_first_ref,
+    grad_outer_ref,
+    grad_inner_ref,
+    grad_output_ref,
+    sums_ref,
+    inner_sums_ref,
+    active,
+    slopes,
+    grad_expanded,
+    hidden_low,
+    grad_branch,
+    grad_attention,
+):
+    step = pl.program_id(0)
+
+    @pl.when(step < ROW_TILES)
+    def _():
+        rows = pl.ds(pl.multiple_of(step * ROWS, ROWS), ROWS)
+        vector = lambda j: vectors_ref[j : j + 1, :]
+        output_add, outer_add, gain_one, shift_one, gain_two, shift_two = map(vector, range(6))
+        attention = mm(mixture_ref[rows, :], output_weight_ref[...]) + output_add
+        normed_one, inverse_one = row_norm(pooled_ref[...] + attention)
+        hidden = normed_one * gain_one + shift_one
+        low_hidden = hidden.astype(BF16)
+        hidden_low[rows, :] = low_hidden
+        branch = jnp.zeros((ROWS, MODEL_WIDTH), F32)
+        for j in range(FF_TILES):
+            part = slice(j * FF_STEP, (j + 1) * FF_STEP)
+            expanded = mm(low_hidden, inner_weight_ref[:, part]) + inner_add_ref[:, part]
+            value, slope = gelu_pieces(expanded)
+            low_value = value.astype(BF16)
+            active[rows, part] = low_value
+            slopes[:, part] = slope
+            branch += mm(low_value, outer_weight_ref[part, :])
+        normed_two, inverse_two = row_norm(hidden + (branch + outer_add))
+        output_ref[...] = (normed_two * gain_two + shift_two).astype(BF16)
+        upstream = upstream_ref[...].astype(F32)
+        grad_second = row_norm_back(upstream * gain_two, normed_two, inverse_two)
+        low_branch = grad_second.astype(BF16)
+        grad_branch[rows, :] = low_branch
+        grad_hidden = grad_second
+        inner_sums = []
+        for j in range(FF_TILES):
+            part = slice(j * FF_STEP, (j + 1) * FF_STEP)
+            grad_active = mm(low_branch, outer_weight_ref[part, :], NT)
+            low_grad = (slopes[:, part] * grad_active).astype(BF16)
+            grad_expanded[rows, part] = low_grad
+            inner_sums.append(jnp.sum(low_grad.astype(F32), axis=0, keepdims=True))
+            grad_hidden += mm(low_grad, inner_weight_ref[:, part], NT)
+        grad_first = row_norm_back(grad_hidden * gain_one, normed_one, inverse_one)
+        grad_first_ref[...] = grad_first
+        low_attention = grad_first.astype(BF16)
+        grad_attention[rows, :] = low_attention
+        grad_mixture_ref[...] = mm(low_attention, output_weight_ref[...], NT).astype(BF16)
+        row = lambda v: jnp.sum(v, axis=0, keepdims=True)
+        sums = jnp.concatenate(
+            [
+                row(low_attention.astype(F32)),
+                row(low_branch.astype(F32)),
+                row(grad_hidden * normed_one),
+                row(grad_hidden),
+                row(upstream * normed_two),
+                row(upstream),
+                jnp.zeros((2, MODEL_WIDTH), F32),
+            ],
+            axis=0,
+        )
+        inner_sum = jnp.concatenate(inner_sums, axis=1)
+
+        @pl.when(step == 0)
+        def _():
+            sums_ref[...] = sums
+            inner_sums_ref[...] = inner_sum
+
+        @pl.when(step > 0)
+        def _():
+            sums_ref[...] += sums
+            inner_sums_ref[...] += inner_sum
+
+    for j in range(FF_TILES):
+
+        @pl.when(step == ROW_TILES + j)
+        def _():
+            part = slice(j * FF_STEP, (j + 1) * FF_STEP)
+            grad_outer_ref[...] = mm(active[:, part], grad_branch[...], TN).astype(BF16)
+            grad_inner_ref[...] = mm(hidden_low[...], grad_expanded[:, part], TN).astype(BF16)
+            if j == 0:
+                grad_output_ref[...] = mm(mixture_ref[...], grad_attention[...], TN).astype(BF16)
+
+
+def mlp(mixture, pooled, upstream, output_weight, inner_weight, outer_weight, vectors, inner_add):
+    fixed = lambda shape: pl.BlockSpec(shape, lambda i: (0, 0), pipeline_mode=pl.Buffered(1))
+    still = lambda shape: pl.BlockSpec(shape, lambda i: (0, 0))
+    tile = pl.BlockSpec((ROWS, MODEL_WIDTH), lambda i: (jnp.minimum(i, ROW_TILES - 1), 0))
+    late = lambda i: jnp.maximum(i - ROW_TILES, 0)
+    whole = (PQ, MODEL_WIDTH)
+    square = (MODEL_WIDTH, MODEL_WIDTH)
+    return pl.pallas_call(
+        mlp_kernel,
+        grid=(ROW_TILES + FF_TILES,),
+        in_specs=[
+            fixed(whole),
+            tile,
+            tile,
+            fixed(square),
+            fixed((MODEL_WIDTH, FF)),
+            fixed((FF, MODEL_WIDTH)),
+            fixed((8, MODEL_WIDTH)),
+            fixed((1, FF)),
+        ],
+        out_specs=[
+            tile,
+            tile,
+            tile,
+            pl.BlockSpec((FF_STEP, MODEL_WIDTH), lambda i: (late(i), 0)),
+            pl.BlockSpec((MODEL_WIDTH, FF_STEP), lambda i: (0, late(i))),
+            still(square),
+            still((8, MODEL_WIDTH)),
+            still((1, FF)),
+        ],
+        out_shape=[
+            jax.ShapeDtypeStruct(whole, BF16),
+            jax.ShapeDtypeStruct(whole, BF16),
+            jax.ShapeDtypeStruct(whole, F32),
+            jax.ShapeDtypeStruct((FF, MODEL_WIDTH), BF16),
+            jax.ShapeDtypeStruct((MODEL_WIDTH, FF), BF16),
+            jax.ShapeDtypeStruct(square, BF16),
+            jax.ShapeDtypeStruct((8, MODEL_WIDTH), F32),
+            jax.ShapeDtypeStruct((1, FF), F32),
+        ],
+        scratch_shapes=[
+            pltpu.VMEM((PQ, FF), BF16),
+            pltpu.VMEM((ROWS, FF), F32),
+            pltpu.VMEM((PQ, FF), BF16),
+            pltpu.VMEM(whole, BF16),
+            pltpu.VMEM(whole, BF16),
+            pltpu.VMEM(whole, BF16),
+        ],
+        cost_estimate=pl.CostEstimate(
+            flops=2 * PQ * MODEL_WIDTH * (3 * MODEL_WIDTH + 6 * FF),
+            bytes_accessed=40_000_000,
+            transcendentals=PQ * FF,
+        ),
+        compiler_params=pltpu.CompilerParams(vmem_limit_bytes=58 * 2**20),
+        name="mlp",
+    )(mixture, pooled, upstream, output_weight, inner_weight, outer_weight, vectors, inner_add)
+
+
+MESH = pl.DeviceIdType.MESH
+SUM_ROWS = 48
+STAGES = ("core", "y", "x", "near", "far", "far_back", "near_back", "x_back")
+SMALL_ROWS = 16
+SMALL_COLUMNS = 1024
+
+
+class Place:
+    def __init__(self):
+        self.seq, self.dp = lax.axis_index("seq"), lax.axis_index("dp")
+        self.core, self.y = self.dp % 2, self.dp // 2
+        self.x, self.near, self.far = self.seq % 2, (self.seq // 2) % 2, self.seq // 4
+        self.partner = {
+            "core": (self.seq, self.dp + 1 - 2 * self.core),
+            "y": (self.seq, self.dp + 2 - 4 * self.y),
+            "x": (self.seq + 1 - 2 * self.x, self.dp),
+            "near": (self.seq + 2 - 4 * self.near, self.dp),
+            "far": (self.seq + 4 - 8 * self.far, self.dp),
+        }
+
+    def peers(self):
+        return [((self.seq + k) % SG, self.dp) for k in range(1, SG)]
+
+    def greet(self):
+        barrier = pltpu.get_barrier_semaphore()
+        others = [self.partner["core"], self.partner["y"], *self.peers()]
+        for device in others:
+            pl.semaphore_signal(barrier, inc=1, device_id=device, device_id_type=MESH)
+        pl.semaphore_wait(barrier, len(others))
+
+
+def add_rows(target, addend, rows):
+    def step(i, carry):
+        at = pl.ds(pl.multiple_of(i * SUM_ROWS, 16), SUM_ROWS)
+        left, right = target(at), addend(at)
+        left[...] = (left[...].astype(F32) + right[...].astype(F32)).astype(BF16)
+        return carry
+
+    lax.fori_loop(0, rows // SUM_ROWS, step, 0)
+
+
+class Chunk:
+    def __init__(self, place, index, source, rows, columns, buffers, send, receive, local):
+        self.place, self.source, self.rows, self.columns = place, source, rows, columns
+        self.own, self.from_core, self.from_y, self.from_x, self.from_near, self.from_far, self.full = buffers
+        self.send_at = lambda stage, k=0: send.at[index, STAGES.index(stage) + (8 if k else 0)]
+        self.receive_at = lambda stage, k=0: receive.at[index, STAGES.index(stage) + (8 if k else 0)]
+        self.local = lambda k: local.at[index, k]
+        half, quarter = rows // 2, rows // 4
+        self.my_columns = pl.ds(pl.multiple_of(place.x * (columns // 2), 128), columns // 2)
+        self.other_columns = pl.ds(
+            pl.multiple_of((1 - place.x) * (columns // 2), 128), columns // 2
+        )
+        self.my_half = pl.multiple_of(place.near * half, 16)
+        self.my_quarter = pl.multiple_of(place.near * half + place.far * quarter, 16)
+
+    def remote(self, stage, source, target, k=0):
+        return pltpu.make_async_remote_copy(
+            src_ref=source,
+            dst_ref=target,
+            send_sem=self.send_at(stage, k),
+            recv_sem=self.receive_at(stage, k),
+            device_id=self.place.partner[stage.split("_")[0]],
+            device_id_type=MESH,
+        )
+
+    def locals(self):
+        return [
+            pltpu.make_async_copy(
+                self.source(2 * k + self.place.core), self.own.at[k], self.local(k)
+            )
+            for k in range(2)
+        ]
+
+    def copies(self, stage):
+        place, rows = self.place, self.rows
+        half, quarter = rows // 2, rows // 4
+        if stage == "core":
+            return [
+                self.remote(
+                    stage, self.source(2 * k + 1 - place.core), self.from_core.at[k], k
+                )
+                for k in range(2)
+            ]
+        if stage == "y":
+            return [self.remote(stage, self.from_core.at[1 - place.y], self.from_y)]
+        if stage == "x":
+            return [self.remote(stage, self.from_y.at[:, self.other_columns], self.from_x)]
+        if stage == "near":
+            other = pl.ds(pl.multiple_of((1 - place.near) * half, 16), half)
+            return [self.remote(stage, self.from_x.at[other, :], self.from_near)]
+        if stage == "far":
+            other = pl.ds(pl.multiple_of((1 - place.far) * quarter, 16), quarter)
+            return [self.remote(stage, self.from_near.at[other, :], self.from_far)]
+        if stage == "far_back":
+            mine = self.full.at[pl.ds(self.my_quarter, quarter), self.my_columns]
+            return [self.remote(stage, self.from_far, mine)]
+        if stage == "near_back":
+            mine = self.full.at[pl.ds(self.my_half, half), self.my_columns]
+            return [self.remote(stage, mine, mine)]
+        mine = self.full.at[:, self.my_columns]
+        return [self.remote(stage, mine, mine)]
+
+    def start(self, stage):
+        if stage == "core":
+            for copy in self.locals():
+                copy.start()
+        for copy in self.copies(stage):
+            copy.start()
+
+    def finish(self, stage):
+        place, rows = self.place, self.rows
+        half, quarter = rows // 2, rows // 4
+        for copy in self.copies(stage):
+            copy.wait_recv()
+        if stage == "core":
+            for copy in self.locals():
+                copy.wait()
+            for k in range(2):
+                add_rows(
+                    lambda at: self.from_core.at[k, at, :], lambda at: self.own.at[k, at, :], rows
+                )
+        elif stage == "y":
+            add_rows(
+                lambda at: self.from_y.at[at, :],
+                lambda at: self.from_core.at[place.y, at, :],
+                rows,
+            )
+        elif stage == "x":
+            add_rows(
+                lambda at: self.from_x.at[at, :],
+                lambda at: self.from_y.at[at, self.my_columns],
+                rows,
+            )
+        elif stage == "near":
+            add_rows(
+                lambda at: self.from_near.at[at, :],
+                lambda at: self.from_x.at[
+                    pl.ds(pl.multiple_of(at.start + self.my_half, 16), SUM_ROWS), :
+                ],
+                half,
+            )
+        elif stage == "far":
+            begin = place.far * quarter
+            add_rows(
+                lambda at: self.from_far.at[at, :],
+                lambda at: self.from_near.at[
+                    pl.ds(pl.multiple_of(at.start + begin, 16), SUM_ROWS), :
+                ],
+                quarter,
+            )
+
+            def step(i, carry):
+                at = pl.ds(pl.multiple_of(i * SUM_ROWS, 16), SUM_ROWS)
+                to = pl.ds(pl.multiple_of(i * SUM_ROWS + self.my_quarter, 16), SUM_ROWS)
+                self.full[to, self.my_columns] = self.from_far[at, :]
+                return carry
+
+            lax.fori_loop(0, quarter // SUM_ROWS, step, 0)
+
+    def close(self, stages):
+        for stage in stages:
+            for copy in self.copies(stage):
+                copy.wait_send()
+
+
+def chunk_buffers(rows, columns):
+    buffer = lambda *shape: pltpu.VMEM(shape, BF16)
+    return [
+        buffer(2, rows, columns),
+        buffer(2, rows, columns),
+        buffer(rows, columns),
+        buffer(rows, columns // 2),
+        buffer(rows // 2, columns // 2),
+        buffer(rows // 4, columns // 2),
+        buffer(rows, columns),
+    ]
+
+
+def grad_chunks():
+    quarter = MODEL_WIDTH // 4
+    return [
+        (0, MODEL_WIDTH, 0, 0, MODEL_WIDTH // 2, MODEL_WIDTH),
+        (0, MODEL_WIDTH, MODEL_WIDTH // 2, 0, MODEL_WIDTH // 2, MODEL_WIDTH),
+        (1, quarter, 0, 0, quarter, FF // 2),
+        (1, quarter, 0, FF // 2, quarter, FF // 2),
+        (2, quarter, 0, 0, quarter, MODEL_WIDTH),
+        (3, quarter, 0, 0, quarter, MODEL_WIDTH),
+        (4, quarter, 0, 0, quarter, MODEL_WIDTH),
+        (5, quarter, 0, 0, quarter, MODEL_WIDTH),
+    ]
+
+
+def finish_kernel(tokens_ref, small_ref, *refs):
+    chunks = grad_chunks()
+    grads, refs = refs[:6], refs[6:]
+    tokens_out, small_out, refs = refs[0], refs[1], refs[2:]
+    outs, refs = refs[:6], refs[6:]
+    buffers, refs = refs[: 7 * len(chunks)], refs[7 * len(chunks) :]
+    (
+        send,
+        receive,
+        local,
+        token_send,
+        token_receive,
+        token_local,
+        small_core,
+        small_y,
+        small_all,
+        small_send,
+        small_receive,
+    ) = refs
+    place = Place()
+    place.greet()
+    kept = pltpu.make_async_copy(
+        tokens_ref.at[place.seq], tokens_out.at[place.seq], token_local
+    )
+    kept.start()
+    moved = []
+    for k in range(1, SG):
+        to = (place.seq + k) % SG
+        copy = pltpu.make_async_remote_copy(
+            src_ref=tokens_ref.at[to],
+            dst_ref=tokens_out.at[place.seq],
+            send_sem=token_send.at[k - 1],
+            recv_sem=token_receive.at[k - 1],
+            device_id=(to, place.dp),
+            device_id_type=MESH,
+        )
+        copy.start()
+        moved.append(copy)
+
+    def small_copy(source, target, slot, device):
+        return pltpu.make_async_remote_copy(
+            src_ref=source,
+            dst_ref=target,
+            send_sem=small_send.at[slot],
+            recv_sem=small_receive.at[slot],
+            device_id=device,
+            device_id_type=MESH,
+        )
+
+    core_copies = [
+        small_copy(
+            small_ref.at[2 * k + 1 - place.core], small_core.at[k], k, place.partner["core"]
+        )
+        for k in range(2)
+    ]
+    for copy in core_copies:
+        copy.start()
+
+    def chunk_of(index):
+        which, owner_rows, row, column, rows, columns = chunks[index]
+
+        def source(owner):
+            begin = pl.multiple_of(owner * owner_rows + row, 16)
+            return grads[which].at[pl.ds(begin, rows), pl.ds(column, columns)]
+
+        return Chunk(
+            place,
+            index,
+            source,
+            rows,
+            columns,
+            buffers[7 * index : 7 * index + 7],
+            send,
+            receive,
+            local,
+        )
+
+    work = [chunk_of(i) for i in range(len(chunks))]
+    small_copies = []
+    for tick in range(len(work) + len(STAGES)):
+        for s in reversed(range(len(STAGES) + 1)):
+            i = tick - s
+            if 0 <= i < len(work):
+                if s > 0:
+                    work[i].finish(STAGES[s - 1])
+                if s < len(STAGES):
+                    work[i].start(STAGES[s])
+        if tick == 0:
+            for k, copy in enumerate(core_copies):
+                copy.wait_recv()
+                small_core[k] += small_ref[2 * k + place.core]
+            y_copy = small_copy(
+                small_core.at[1 - place.y], small_y, 2, place.partner["y"]
+            )
+            y_copy.start()
+        if tick == 1:
+            y_copy.wait_recv()
+            small_all[place.seq] = small_core[place.y] + small_y[...]
+            for k, device in enumerate(place.peers()):
+                copy = small_copy(
+                    small_all.at[place.seq], small_all.at[place.seq], 3 + k, device
+                )
+                copy.start()
+                small_copies.append(copy)
+    for copy in small_copies:
+        copy.wait_recv()
+    total = small_all[0]
+    for k in range(1, SG):
+        total = total + small_all[k]
+    small_out[...] = total
+    for i, item in enumerate(work):
+        which, _, row, column, rows, columns = chunks[i]
+        outs[which][row : row + rows, column : column + columns] = item.full[...]
+        item.close(STAGES)
+    for copy in [*core_copies, y_copy, *small_copies]:
+        copy.wait_send()
+    for copy in moved:
+        copy.wait()
+    kept.wait()
+
+
+def finish(tokens, small, grads):
+    anywhere = pl.BlockSpec(memory_space=pl.ANY)
+    chunks = grad_chunks()
+    quarter = MODEL_WIDTH // 4
+    shapes = [
+        (MODEL_WIDTH, MODEL_WIDTH),
+        (quarter, FF),
+        *[(quarter, MODEL_WIDTH)] * 4,
+    ]
+    count = len(chunks)
+    small_shape = (SMALL_ROWS, SMALL_COLUMNS)
+    inside = pl.BlockSpec(memory_space=pltpu.VMEM)
+    return pl.pallas_call(
+        finish_kernel,
+        in_specs=[anywhere, inside, *[anywhere] * 6],
+        out_specs=[anywhere, inside, *[inside] * 6],
+        out_shape=[
+            jax.ShapeDtypeStruct(tokens.shape, BF16),
+            jax.ShapeDtypeStruct(small_shape, F32),
+            *[jax.ShapeDtypeStruct(shape, BF16) for shape in shapes],
+        ],
+        scratch_shapes=[
+            *[buffer for chunk in chunks for buffer in chunk_buffers(*chunk[4:])],
+            pltpu.SemaphoreType.DMA((count, 16)),
+            pltpu.SemaphoreType.DMA((count, 16)),
+            pltpu.SemaphoreType.DMA((count, 2)),
+            pltpu.SemaphoreType.DMA((SG - 1,)),
+            pltpu.SemaphoreType.DMA((SG - 1,)),
+            pltpu.SemaphoreType.DMA,
+            pltpu.VMEM((2, *small_shape), F32),
+            pltpu.VMEM(small_shape, F32),
+            pltpu.VMEM((SG, *small_shape), F32),
+            pltpu.SemaphoreType.DMA((SG + 2,)),
+            pltpu.SemaphoreType.DMA((SG + 2,)),
+        ],
+        compiler_params=pltpu.CompilerParams(
+            collective_id=3, has_side_effects=True, vmem_limit_bytes=56 * 2**20
+        ),
+        name="finish",
+    )(tokens, small, *grads)
+
+
 def swap_halves(value, axis):
     first, second = jnp.split(value, 2, axis=axis)
     return jnp.concatenate([second, first], axis=axis)
@@ -925,8 +1465,9 @@
         ],
         axis=1,
     )
+    rows = lax.all_to_all(tokens, "seq", split_axis=0, concat_axis=0, tiled=True)
+    labels, _ = lax.optimization_barrier((labels, rows))
     labels = lax.all_to_all(labels, "seq", split_axis=0, concat_axis=0, tiled=True)
-    rows = lax.all_to_all(tokens, "seq", split_axis=0, concat_axis=0, tiled=True)
     small = jnp.concatenate(
         [
             low(value).reshape(-1)
@@ -1034,13 +1575,13 @@
         [position_pairs, type_pairs, table_pairs, jnp.zeros((PAIRS, 4, LANES), F32)], axis=1
     )
 
-    block = 2 * rows.shape[1] // 2
+    block = rows.shape[1]
     pooled_block = block // 2
     at = jnp.arange(block, dtype=jnp.int32)[None, None, :]
     want = 2 * jnp.arange(pooled_block, dtype=jnp.int32)[None, :, None]
     half = jnp.where(pair_same, 0.5, 1.0)[:, :, None]
-    pool = jnp.where(at == want, half, jnp.where(at == want + 1, 1.0 - half, 0.0)).astype(BF16)
-    pool = jnp.where(at == want + 1, jnp.where(pair_same, 0.5, 0.0)[:, :, None].astype(BF16), pool)
+    other_half = jnp.where(pair_same, 0.5, 0.0)[:, :, None]
+    pool = jnp.where(at == want, half, jnp.where(at == want + 1, other_half, 0.0)).astype(BF16)
 
     pooled = jnp.einsum("cpt,ctd->cpd", pool, rows, preferred_element_type=F32)
     pooled = pooled.reshape(PQ, MODEL_WIDTH)
@@ -1053,48 +1594,45 @@
         query, pairs, maps, map_add, content_add, query_side, key_side, phase, cosm, sinm
     )
 
-    cotangent, _ = lax.optimization_barrier((cotangent, pairs))
+    cotangent, _ = lax.optimization_barrier((cotangent, labels))
     cotangent = lax.all_to_all(cotangent, "seq", split_axis=0, concat_axis=0, tiled=True)
-    upstream = cotangent.reshape(PQ, MODEL_WIDTH).astype(F32)
+    upstream = cotangent.reshape(PQ, MODEL_WIDTH)
 
     output_low, inner_low = next_weights[:, :MODEL_WIDTH], next_weights[:, MODEL_WIDTH:]
-    attention = mm(mixture, output_low) + output_add
-    hidden, normed_one, inverse_one = norm_forward(pooled + attention, gain_one, shift_one)
-    hidden_low = low(hidden)
-    expanded = mm(hidden_low, inner_low) + inner_add
-    active = low(jax.nn.gelu(expanded, approximate=True))
-    branch = mm(active, outer_low) + outer_add
-    result, normed_two, inverse_two = norm_forward(hidden + branch, gain_two, shift_two)
-    output = low(result).reshape(SG, PQ // SG, MODEL_WIDTH)
+    vectors = jnp.concatenate(
+        [
+            output_add,
+            outer_add,
+            gain_one,
+            shift_one,
+            gain_two,
+            shift_two,
+            jnp.zeros((2, MODEL_WIDTH), F32),
+        ],
+        axis=0,
+    )
+    (
+        output,
+        grad_mixture,
+        grad_first,
+        grad_outer_weight,
+        grad_inner_weight,
+        grad_output_weight,
+        row_sums,
+        grad_inner_bias,
+    ) = mlp(
+        mixture, pooled, upstream, output_low, inner_low, outer_low, vectors, inner_add
+    )
+    (
+        grad_output_bias,
+        grad_outer_bias,
+        grad_gain_one,
+        grad_shift_one,
+        grad_gain_two,
+        grad_shift_two,
+    ) = [row_sums[j] for j in range(6)]
+    output = output.reshape(SG, PQ // SG, MODEL_WIDTH)
     output = lax.all_to_all(output, "seq", split_axis=0, concat_axis=0, tiled=True)
-
-    total = lambda value: jnp.sum(value, axis=0)
-    grad_gain_two = total(upstream * normed_two)
-    grad_shift_two = total(upstream)
-    grad_second = norm_backward(upstream, normed_two, inverse_two, gain_two)
-    grad_branch = low(grad_second)
-    grad_outer_weight = mm(active, grad_branch, TN)
-    grad_outer_bias = total(grad_branch.astype(F32))
-    grad_active = mm(grad_branch, outer_low, NT)
-    _, gelu_pull = jax.vjp(partial(jax.nn.gelu, approximate=True), expanded)
-    grad_expanded = low(gelu_pull(grad_active)[0])
-    grad_inner_weight = mm(hidden_low, grad_expanded, TN)
-    grad_inner_bias = total(grad_expanded.astype(F32))
-
-    def shared(value):
-        value = lax.psum_scatter(low(value), "dp", scatter_dimension=0, tiled=True)
-        return lax.psum(value, "seq").astype(F32)
-
-    owned_outer = shared(grad_outer_weight)
-    owned_inner = shared(grad_inner_weight)
-    grad_hidden = grad_second + mm(grad_expanded, inner_low, NT)
-    grad_gain_one = total(grad_hidden * normed_one)
-    grad_shift_one = total(grad_hidden)
-    grad_first = norm_backward(grad_hidden, normed_one, inverse_one, gain_one)
-    grad_attention = low(grad_first)
-    grad_output_weight = mm(mixture, grad_attention, TN)
-    grad_output_bias = total(grad_attention.astype(F32))
-    grad_mixture = low(mm(grad_attention, output_low, NT))
 
     grad_query, grad_key, grad_value, sums, grad_map = attend_backward(
         join,
@@ -1110,9 +1648,6 @@
         cosm,
         sinm,
     )
-    grad_query_weight = mm(pooled_low, grad_query, TN)
-    grad_key_weight = mm(token_rows, grad_key, TN)
-    grad_value_weight = mm(token_rows, grad_value, TN)
     grad_pooled = grad_first + mm(grad_query, first[:, :MODEL_WIDTH], NT)
     grad_direct = mm(grad_key, first[:, MODEL_WIDTH : 2 * MODEL_WIDTH], NT)
     grad_direct = grad_direct + mm(grad_value, first[:, 2 * MODEL_WIDTH :], NT)
@@ -1120,7 +1655,9 @@
     spread = partial(jnp.einsum, "cpt,cpd->ctd", preferred_element_type=F32)
     spread_sum = spread(pool, high_pooled) + spread(pool, low_pooled)
     grad_tokens = low(grad_direct.reshape(SG, block, MODEL_WIDTH) + spread_sum)
-    grad_tokens = lax.all_to_all(grad_tokens, "seq", split_axis=0, concat_axis=0, tiled=True)
+    grad_query_weight = low(mm(pooled_low, grad_query, TN))
+    grad_key_weight = low(mm(token_rows, grad_key, TN))
+    grad_value_weight = low(mm(token_rows, grad_value, TN))
 
     crossed = grad_map.reshape(PAIRS, 2, HEAD_SIZE, 2, 2, HEAD_SIZE)
     grad_relative = jnp.stack(
@@ -1153,18 +1690,24 @@
         ],
         axis=1,
     )
-    wide = 4 * MODEL_WIDTH
-    small_rows = small_grads.shape[1] // wide
-    late = jnp.concatenate(
-        [grad_query_weight, grad_key_weight, grad_value_weight, grad_output_weight], axis=1
-    ).reshape(owners, part, wide)
-    spare = jnp.zeros((owners, -small_rows % 8, wide), F32)
-    late = jnp.concatenate(
-        [late, small_grads.reshape(owners, small_rows, wide), spare], axis=1
-    ).reshape(-1, wide)
-    owned_late = shared(late)
-    squares = [owned_late[:part, j * MODEL_WIDTH : (j + 1) * MODEL_WIDTH] for j in range(4)]
-    small_owned = owned_late[part : part + small_rows].reshape(-1)
+    count = small_grads.shape[1]
+    room = SMALL_ROWS * SMALL_COLUMNS
+    small_grads = jnp.pad(small_grads, ((0, 0), (0, room - count)))
+    grad_tokens, small_owned, *owned = finish(
+        grad_tokens,
+        small_grads.reshape(owners, SMALL_ROWS, SMALL_COLUMNS),
+        [
+            grad_outer_weight,
+            grad_inner_weight,
+            grad_output_weight,
+            grad_query_weight,
+            grad_key_weight,
+            grad_value_weight,
+        ],
+    )
+    owned_outer, owned_inner, owned_output, *squares = [value.astype(F32) for value in owned]
+    squares.append(owned_output)
+    small_owned = small_owned.reshape(-1)
     place = 0
     pieces = []
     for size in [part] * 10 + [FF // owners, kernel_size, HEAD_COUNT * 2 * HEAD_SIZE // owners]:

time: 661 us -> 580 us (0.88)
  waiting for transfers between devices: 244 us -> 0.09 us
  Pallas kernels: 119 us -> 354 us
  matrix products: 126 us -> 53 us
  local copies, waits for them, and re-layouts: 57.3 us -> 65.8 us
    pallas_call x0 -> x2, Pallas kernels: none -> 236 us  [the longest x1 165 us: finish(): pl.pallas_call(finish_kernel, in_specs=[anywhere, inside, *[anywhere] * 6...]
    all_to_all x1 -> x0, waiting for transfers between devices: 105 us -> none  [sequence_body(): lax.all_to_all(grad_tokens, 'seq', split_axis=0, concat_axis=0, tiled=True)]
    psum x1 -> x0, waiting for transfers between devices: 87.4 us -> none  [shared(): return lax.psum(value, 'seq').astype(F32)]
    dot_general x17 -> x8, matrix products: 115 us -> 42.7 us  [mm(): return lax.dot_general(left, right, dims, preferred_element_type=F32)]
    all_to_all x1, waiting for transfers between devices: 26.6 us -> 0.01 us  [sequence_body(): lax.all_to_all(tokens, 'seq', split_axis=0, concat_axis=0, tiled=True)]
    all_to_all x1, waiting for transfers between devices: 20.6 us -> 0.01 us  [sequence_body(): lax.all_to_all(output, 'seq', split_axis=0, concat_axis=0, tiled=True)]
    reduce_sum x7 -> x0, other arithmetic: 8.97 us -> none  [the longest x4 7.6 us: sequence_body(): total = lambda value: jnp.sum(value, axis=0)]
    concatenate x2 -> x0, other arithmetic: 8.45 us -> none  [the longest x1 5.97 us: sequence_body(): jnp.concatenate([late, small_grads.reshape(owners, small_rows, wide), spa...]
  transfers between devices with their start and end apart: 12 -> 7, of which waited for: 5 -> 0; matrix products, arithmetic and copies ran while one was open for 28% -> 24% of each run, Pallas kernels for 18% -> 36%
where the time goes in v2:
time: 580 us; the launch traced here: 577 us
  Pallas kernels  354 us (61%)
  local copies, waits for them, and re-layouts  65.8 us (11%)
  other arithmetic  57 us (10%)
  matrix products  53 us (9%)
  starting transfers between devices  25.8 us (4%)
  between operations  14.9 us (3%)
  blocking collectives  6.11 us (1%)
    pallas_call x1, Pallas kernels, finish(): pl.pallas_call(finish_kernel, in_specs=[anywhere, inside, *[anywhere] * 6...  165 us
    pallas_call x1, Pallas kernels, attend_backward(): pl.pallas_call(attend_back_kernel, grid=(PAIRS,), in_specs=[pl.BlockSpec(...  73.4 us
    pallas_call x1, Pallas kernels, mlp(): pl.pallas_call(mlp_kernel, grid=(ROW_TILES + FF_TILES,), in_specs=[fixed(...  70.7 us
    pallas_call x1, Pallas kernels, attend_forward(): pl.pallas_call(attend_kernel, grid=(PAIRS,), in_specs=[pl.BlockSpec((PQ,...  44.9 us
    dot_general x8, matrix products, mm(): return lax.dot_general(left, right, dims, preferred_element_type=F32)  42.7 us
    unnamed x125, local copies, waits for them, and re-layouts  16.3 us
  transfers between devices with their start and end apart: 7, of which 0 were waited for; matrix products, arithmetic and copies ran while one was open for 24% of the time, Pallas kernels for 36%

profile of v2, /device:TPU:0, one launch (start us, length us, event | category | flops | bytes accessed | tf_op | source)
XLA Modules:
  0.0 576.7 jit_solution(6894084031438961579)
XLA Ops:
  7.2 1.1 convert_element_type.151
  8.3 1.2 convert_element_type.152
  9.6 1.1 convert_element_type.153
  10.7 1.0 pad_maximum_fusion.2
  12.8 1.2 pad_maximum_fusion.1
  14.0 7.3 %all-to-all-start = ((bf16[8,256,768]{2,1,0:T(8,128)(2,1)}), bf16[8,256,768]{2,1,0:T(8,128)(2,1)S(1)}, u32[]{:S(2)}, u32[]{:S(2)}) async-start(bf16[8,256,768]{2,1,0:T(8,128)(2,1)} %param.23), calls=%async_computation | async-start | bytes 6291456 | tf_op jit(solution)/shard_map/all_to_all | solution.py:1468
  21.5 3.1 convert_element_type.174
  25.3 6.1 %all-gather = bf16[61440]{0:T(1024)(128)(2,1)S(1)} all-gather(bf16[15360]{0:T(1024)(128)(2,1)S(1)} %concatenate.115), channel_id=2, replica_groups=mesh['seq'=8,'dp'=4] {'dp'}, dimensions={0}, use_global_device_ids=true | all-gather | bytes 153600 | tf_op jit(solution)/shard_map/all_gather | solution.py:1491
  32.8 1.2 reshape.472
  34.8 1.0 fusion.68
  35.7 1.3 slice_convert_fusion.1
  38.0 1.7 copy.117
  39.8 1.7 copy.118
  42.4 1.7 concatenate.118
  44.1 1.8 copy.119
  46.0 1.8 copy.120
  47.8 1.1 fusion.51
  53.7 1.6 slice_convert_fusion.10
  55.3 1.3 reshape.500
  56.7 2.0 convert_bitcast_fusion.1
  58.7 2.0 convert_bitcast_fusion
  65.4 1.3 reshape.498
  66.7 1.9 fusion.23
  70.4 1.3 pad_maximum_fusion.11.map_add_ref
  71.7 1.8 pad_maximum_fusion.8.map_back_ref
  73.6 1.9 multiply_sine_fusion
  75.5 1.9 pad_maximum_fusion.4
  77.4 3.3 pad_maximum_fusion
  82.4 4.3 copy.96.map_ref
  90.0 4.0 cosine_convert_fusion
  94.1 1.4 pad_maximum_fusion.3.phase_ref
  95.5 6.3 %all-to-all-start.1 = ((s32[8,7,128]{2,1,0:T(8,128)}), s32[8,7,128]{2,1,0:T(8,128)S(1)}, u32[]{:S(2)}, u32[]{:S(2)}) async-start(s32[8,7,128]{2,1,0:T(8,128)} %stack.40), calls=%async_computation.1 | async-start | bytes 65536 | tf_op jit(solution)/shard_map/all_to_all | solution.py:1470
  101.8 9.1 %fusion.key_ref.value_ref = bf16[2048,1536]{1,0:T(8,128)(2,1)} fusion(bf16[2048,768]{1,0:T(8,128)(2,1)S(1)} %bitcast.102, f32[1536]{0:T(1024)S(1)} %convert_reduce_fusion, bf16[768,2304]{1,0:T(8,128)(2,1)} %all-gather.5.cloned.1.call-done), kind=kOutput, calls=%fused_computation.1 | convolution fusion | flops 4838129664 | bytes 11802624 | tf_op jit(solution)/shard_map/dot_general | solution.py:565
  111.4 5.9 %all-to-all-start.2 = ((bf16[8,128,768]{2,1,0:T(8,128)(2,1)}), bf16[8,128,768]{2,1,0:T(8,128)(2,1)}, u32[]{:S(2)}, u32[]{:S(2)}) async-start(bf16[8,128,768]{2,1,0:T(8,128)(2,1)} %param.26), calls=%async_computation.2 | async-start | bytes 3145728 | tf_op jit(solution)/shard_map/all_to_all | solution.py:1598
  117.3 1.3 fusion.72
  119.2 2.6 select_add_fusion
  121.8 2.6 compare_select_fusion.4
  124.4 1.1 convert_select_fusion.query_side_ref
  126.3 2.5 fusion.17.key_side_ref
  128.7 4.4 fusion.19.query_ref
  133.1 44.9 %attend_forward.1 = (bf16[1024,768]{1,0:T(8,128)(2,1)}, bf16[12,1024,256]{2,1,0:T(8,128)(2,1)}) custom-call(f32[1024,768]{1,0:T(8,128)} %fusion.19.query_ref, bf16[2048,1536]{1,0:T(8,128)(2,1)} %fusion.key_ref.value_ref, bf16[2048,1536]{1,0:T(8,128)(2,1)} %fusion.key_ref.value_ref, bf16[6,256,768]{2,1,0:T(8,128)(2,1)} %copy.96.map_ref, ...), custom_call_target="tpu_custom_call" | custom-call | flops 25769803776 | bytes 20000000 | tf_op jit(solution)/shard_map/attend_forward/pallas_call | solution.py:646
  178.0 4.8 slice.320.inner_weight_ref
  182.8 2.4 slice.319.output_weight_ref
  185.1 70.7 %mlp.1 = (bf16[1024,768]{1,0:T(8,128)(2,1)}, bf16[1024,768]{1,0:T(8,128)(2,1)}, f32[1024,768]{1,0:T(8,128)}, bf16[3072,768]{1,0:T(8,128)(2,1)}, bf16[768,3072]{1...) custom-call(bf16[1024,768]{1,0:T(8,128)(2,1)} %get-tuple-element.47.mixture_ref, ...), custom_call_target="tpu_custom_call" | custom-call | flops 32614907904 | bytes 40000000 | tf_op jit(solution)/shard_map/mlp/pallas_call | solution.py:991
  255.9 73.4 %attend_backward.1 = (bf16[1024,768]{1,0:T(8,128)(2,1)}, bf16[2048,768]{1,0:T(8,128)(2,1)}, bf16[2048,768]{1,0:T(8,128)(2,1)}, f32[6,8,128]{2,1,0:T(8,128)}, f32[6,128,256]{2,1,0:T(8,128)}) custom-call(bf16[12,1024,256]{2,1,0:T(8,128)(2,1)} %get-tuple-element.50.join_ref, bf16[2048,1536]{1,0:T(8,128)(2,1)} %fusion.key_ref.value_ref, ...), custom_call_target="tpu_custom_call" | custom-call | flops 64424509440 | bytes 32000000 | tf_op jit(solution)/shard_map/attend_backward/pallas_call | solution.py:795
  330.0 1.5 slice_reduce_fusion
  331.6 2.4 reshape.464
  339.5 4.0 convolution_convert_fusion.2.refs_3_
  343.5 2.7 convolution_add_fusion.1
  346.3 4.1 fusion.21
  351.2 3.7 fusion.10.refs_4_
  354.9 6.3 %all-to-all-start.3 = ((bf16[8,128,768]{2,1,0:T(8,128)(2,1)}), bf16[8,128,768]{2,1,0:T(8,128)(2,1)}, u32[]{:S(2)}, u32[]{:S(2)}) async-start(bf16[8,128,768]{2,1,0:T(8,128)(2,1)} %bitcast.111), calls=%async_computation.3 | async-start | bytes 3145728 | tf_op jit(solution)/shard_map/all_to_all | solution.py:1635
  361.2 7.5 %fusion.13 = f32[2048,768]{1,0:T(8,128)} fusion(bf16[2048,768]{1,0:T(8,128)(2,1)} %get-tuple-element.52, bf16[768,2304]{1,0:T(8,128)(2,1)} %all-gather.5.cloned.1.call-done), kind=kOutput, calls=%fused_computation.23 | convolution fusion | flops 2415919104 | bytes 10616832 | tf_op jit(solution)/shard_map/dot_general | solution.py:565
  370.4 1.1 concatenate.146
  372.4 7.0 %fusion.11.refs_5_ = bf16[768,768]{1,0:T(8,128)(2,1)} fusion(bf16[2048,768]{1,0:T(8,128)(2,1)} %get-tuple-element.53, bf16[2048,768]{1,0:T(8,128)(2,1)} %bitcast.103), kind=kOutput, calls=%fused_computation.21 | convolution fusion | flops 2416508928 | bytes 7471104 | tf_op jit(solution)/shard_map/dot_general | solution.py:565
  379.4 4.3 convolution_add_fusion
  383.8 2.9 add_convert_fusion.1.tokens_ref
  386.6 165.1 %finish.1 = (bf16[8,256,768]{2,1,0:T(8,128)(2,1)}, f32[16,1024]{1,0:T(8,128)}, bf16[768,768]{1,0:T(8,128)(2,1)}, bf16[192,3072]{1,0:T(8,128)(2,1)}, bf16[192,768...) custom-call(bf16[8,256,768]{2,1,0:T(8,128)(2,1)} %add_convert_fusion.1.tokens_ref,, ...), custom_call_target="tpu_custom_call" | custom-call | tf_op jit(solution)/shard_map/finish/pallas_call | solution.py:1368
  551.7 1.0 slice.288
  552.7 1.0 slice.293
  555.2 2.9 convert_element_type.188
  558.1 1.6 convert_element_type.189
  565.7 2.7 copy.144
  568.3 1.7 copy.145
  (252 shorter events, 41.1 us)
Async XLA Ops:
  7.2 94.6 %all-gather.5.cloned.1.call-start = ((), (), s32[]{:S(2)}) async-start(), calls=%async_computation.4 | async-start | bytes 4423680 | tf_op jit(solution)/shard_map/all_gather | solution.py:1493
  8.3 3.4 copy-start.6
  11.7 1.1 copy-start.9
  11.7 166.3 %all-gather.7.cloned.1.call-start = ((), (), s32[]{:S(2)}) async-start(), calls=%async_computation.5 | async-start | bytes 7372800 | tf_op jit(solution)/shard_map/all_gather | solution.py:1495
  14.0 81.5 %all-to-all-start = ((bf16[8,256,768]{2,1,0:T(8,128)(2,1)}), bf16[8,256,768]{2,1,0:T(8,128)(2,1)S(1)}, u32[]{:S(2)}, u32[]{:S(2)}) async-start(bf16[8,256,768]{2,1,0:T(8,128)(2,1)} %param.23), calls=%async_computation | async-start | bytes 6291456 | tf_op jit(solution)/shard_map/all_to_all | solution.py:1468
  21.3 3.3 copy-start.19
  21.3 3.4 copy-start.39
  21.3 3.5 copy-start.38
  21.3 3.5 copy-start.41
  21.3 3.6 copy-start.42
  21.3 3.7 copy-start.43
  21.3 3.8 copy-start.44
  21.3 3.8 copy-start.45
  21.4 3.8 copy-start.46
  21.4 3.8 copy-start.47
  21.4 3.8 copy-start.48
  21.4 3.8 copy-start.49
  21.4 3.8 copy-start.50
  21.4 163.7 %all-gather.9.cloned.1.call-start = ((), (), s32[]{:S(2)}) async-start(), calls=%async_computation.6 | async-start | bytes 5898240 | tf_op jit(solution)/shard_map/all_gather | solution.py:1496
  24.5 12.5 %copy-start.20 = (s32[8,256]{1,0:T(8,128)S(1)}, s32[8,256]{1,0:T(8,128)}, u32[]{:S(2)}) copy-start(s32[8,256]{1,0:T(8,128)} %param.24) | copy-start | bytes 24580
  31.5 0.7 copy-start.14
  56.7 4.1 copy-start.25
  56.7 4.9 copy-start.23
  56.7 5.7 copy-start.26
  56.7 6.5 %copy-start.24 = (f32[6,128]{1,0:T(8,128)S(1)}, f32[6,128]{1,0:T(8,128)}, u32[]{:S(2)}) copy-start(f32[6,128]{1,0:T(8,128)} %concatenate.127) | copy-start | bytes 9220
  58.7 5.2 copy-start.40
  77.4 3.3 copy-start.21
  77.4 3.3 copy-start.22
  77.4 3.4 copy-start.34
  82.4 4.4 copy-start.37
  82.4 4.4 copy-start.33
  82.4 5.1 copy-start.32
  82.4 5.2 copy-start.31
  82.4 5.2 copy-start.30
  82.4 5.3 copy-start.29
  82.4 5.4 copy-start.28
  82.4 5.5 copy-start.27
  90.0 35.6 %copy-start.10 = (pred[128,256]{0,1:T(8,128)(4,1)}, pred[128,256]{0,1:T(8,128)(4,1)S(1)}, u32[]{:S(2)}) copy-start(pred[128,256]{0,1:T(8,128)(4,1)S(1)} %get-tuple-element.150) | copy-start | bytes 98308
  90.0 35.6 %copy-start.12 = (pred[128,256]{0,1:T(8,128)(4,1)}, pred[128,256]{0,1:T(8,128)(4,1)S(1)}, u32[]{:S(2)}) copy-start(pred[128,256]{0,1:T(8,128)(4,1)S(1)} %get-tuple-element.151) | copy-start | bytes 98308
  95.5 30.1 %copy-start = (bf16[8,256,768]{2,1,0:T(8,128)(2,1)}, bf16[8,256,768]{2,1,0:T(8,128)(2,1)S(1)}, u32[]{:S(2)}) copy-start(bf16[8,256,768]{2,1,0:T(8,128)(2,1)S(1)} %all-to-all-done) | copy-start | bytes 9437188
  95.5 15.5 %all-to-all-start.1 = ((s32[8,7,128]{2,1,0:T(8,128)}), s32[8,7,128]{2,1,0:T(8,128)S(1)}, u32[]{:S(2)}, u32[]{:S(2)}) async-start(s32[8,7,128]{2,1,0:T(8,128)} %stack.40), calls=%async_computation.1 | async-start | bytes 65536 | tf_op jit(solution)/shard_map/all_to_all | solution.py:1470
  111.4 73.7 %all-to-all-start.2 = ((bf16[8,128,768]{2,1,0:T(8,128)(2,1)}), bf16[8,128,768]{2,1,0:T(8,128)(2,1)}, u32[]{:S(2)}, u32[]{:S(2)}) async-start(bf16[8,128,768]{2,1,0:T(8,128)(2,1)} %param.26), calls=%async_computation.2 | async-start | bytes 3145728 | tf_op jit(solution)/shard_map/all_to_all | solution.py:1598
  126.2 6.9 %copy-start.2 = (f32[8,128,768]{2,1,0:T(8,128)}, f32[8,128,768]{2,1,0:T(8,128)S(1)}, u32[]{:S(2)}) copy-start(f32[8,128,768]{2,1,0:T(8,128)S(1)} %fusion.22) | copy-start | bytes 9437188
  335.0 4.6 copy-start.3
  339.5 4.0 copy-start.4
  339.5 4.0 copy-start.7
  343.5 2.7 copy-start.11
  343.5 2.8 copy-start.13
  346.3 4.1 copy-start.1
  346.3 4.9 copy-start.52
  354.9 210.8 %all-to-all-start.3 = ((bf16[8,128,768]{2,1,0:T(8,128)(2,1)}), bf16[8,128,768]{2,1,0:T(8,128)(2,1)}, u32[]{:S(2)}, u32[]{:S(2)}) async-start(bf16[8,128,768]{2,1,0:T(8,128)(2,1)} %bitcast.111), calls=%async_computation.3 | async-start | bytes 3145728 | tf_op jit(solution)/shard_map/all_to_all | solution.py:1635
  361.2 7.5 %copy-start.35 = (f32[8,768]{1,0:T(8,128)S(1)}, f32[8,768]{1,0:T(8,128)}, u32[]{:S(2)}) copy-start(f32[8,768]{1,0:T(8,128)} %get-tuple-element.57) | copy-start | bytes 73732
  361.2 8.5 %copy-start.36 = (f32[1,3072]{1,0:T(1,128)S(1)}, f32[1,3072]{1,0:T(1,128)}, u32[]{:S(2)}) copy-start(f32[1,3072]{1,0:T(1,128)} %get-tuple-element.58) | copy-start | bytes 36868
  371.5 7.9 %slice-start.2 = ((s8[6291456]{0:T(1024)(128)(4,1)}), s8[4194304]{0:T(1024)(128)(4,1)S(1)}, s32[]{:S(2)}) async-start(s8[6291456]{0:T(1024)(128)(4,1)} %bitcast.146), calls=%async_computation.9 | async-start | bytes 8388608
  372.4 7.0 %slice-start.3 = ((s8[6291456]{0:T(1024)(128)(4,1)}), s8[2097152]{0:T(1024)(128)(4,1)S(1)}, s32[]{:S(2)}) async-start(s8[6291456]{0:T(1024)(128)(4,1)} %bitcast.146), calls=%async_computation.10 | async-start | bytes 4194304
  372.4 7.0 %copy-start.51 = (bf16[2048,768]{1,0:T(8,128)(2,1)S(1)}, bf16[2048,768]{1,0:T(8,128)(2,1)}, u32[]{:S(2)}) copy-start(bf16[2048,768]{1,0:T(8,128)(2,1)} %get-tuple-element.53) | copy-start | bytes 9437188
  372.4 11.3 %slice-start = ((s8[6291456]{0:T(1024)(128)(4,1)}), s8[4194304]{0:T(1024)(128)(4,1)S(1)}, s32[]{:S(2)}) async-start(s8[6291456]{0:T(1024)(128)(4,1)} %bitcast.100), calls=%async_computation.7 | async-start | bytes 8388608
  379.4 4.3 slice-start.1
  551.7 6.4 %copy-start.8 = (bf16[768,768]{1,0:T(8,128)(2,1)S(1)}, bf16[768,768]{1,0:T(8,128)(2,1)}, u32[]{:S(2)}) copy-start(bf16[768,768]{1,0:T(8,128)(2,1)} %get-tuple-element.69) | copy-start | bytes 3538948
  558.1 1.6 copy-start.18
  558.1 2.5 copy-start.17
  558.1 3.3 copy-start.16
  558.1 4.2 copy-start.15
  561.4 6.9 %copy-start.5 = (bf16[8,256,768]{2,1,0:T(8,128)(2,1)S(1)}, bf16[8,256,768]{2,1,0:T(8,128)(2,1)}, u32[]{:S(2)}) copy-start(bf16[8,256,768]{2,1,0:T(8,128)(2,1)} %get-tuple-element.182) | copy-start | bytes 9437188
Sparse Core Ops, SparseCore 0:
  11.8 34.1 all-gather.4
  47.5 44.1 all-gather.6
  93.3 37.4 all-gather.8

commit v3 on v1

--- a/solution.py
+++ b/solution.py
@@ -3,6 +3,7 @@
 
 import jax
 import jax.numpy as jnp
+import numpy as np
 from jax import lax
 from jax.experimental import pallas as pl
 from jax.experimental.pallas import tpu as pltpu
@@ -574,13 +575,39 @@
     return lax.broadcasted_iota(jnp.int32, (rows, LANES), 1)
 
 
+VECTORS = 16
+
+
+def pair_maps(relative):
+    row = lax.broadcasted_iota(jnp.int32, (HEAD_SIZE, LANES), 0)
+    twice = (lane_ids(HEAD_SIZE) % HEAD_SIZE == row).astype(BF16)
+    lane = lane_ids(LANES)
+    row = lax.broadcasted_iota(jnp.int32, (LANES, LANES), 0)
+    crossed = (row < HEAD_SIZE) != (lane < HEAD_SIZE)
+    plain = jnp.where(crossed, mm(relative, twice), 0.0).astype(BF16)
+    half = HEAD_SIZE // 2
+    partner = jnp.where(lane % HEAD_SIZE < half, lane + half, lane - half)
+    swapped = mm(plain, (row == partner).astype(BF16)).astype(BF16)
+    return plain, swapped
+
+
+def kind_maps(vectors):
+    row = lax.broadcasted_iota(jnp.int32, (VECTORS, 4 * LANES), 0)
+    column = lax.broadcasted_iota(jnp.int32, (VECTORS, 4 * LANES), 1)
+    lane = column % LANES
+    wanted = (lane >= 3) & (lane < 6) & (row == 11 - (column // LANES) % 2)
+    both = mm(vectors.astype(BF16), wanted.astype(BF16), TN)
+    row = lax.broadcasted_iota(jnp.int32, (LANES, 4 * LANES), 0)
+    column = lax.broadcasted_iota(jnp.int32, (LANES, 4 * LANES), 1)
+    return jnp.where((row < HEAD_SIZE) == (column < 2 * LANES), both, 0.0).astype(BF16)
+
+
 def attend_kernel(
     query_ref,
     key_ref,
     value_ref,
-    map_ref,
-    map_add_ref,
-    content_ref,
+    relative_ref,
+    vectors_ref,
     query_side_ref,
     key_side_ref,
     phase_ref,
@@ -593,10 +620,18 @@
 ):
     query = query_ref[...]
     high, low = split(query)
-    terms = mm(jnp.concatenate([high, low], axis=1), map_ref[0]) + map_add_ref[0]
+    plain, swapped = pair_maps(relative_ref[...])
+    kinds = kind_maps(vectors_ref[...])
+    maps = jnp.concatenate([plain, swapped, kinds], axis=1)
+    position_add, type_add = vectors_ref[8:9, :].astype(BF16), vectors_ref[9:10, :].astype(BF16)
+    map_add = jnp.concatenate(
+        [mm(position_add, plain), mm(position_add, swapped), mm(type_add, kinds)], axis=1
+    )
+    terms = mm(jnp.concatenate([high, low], axis=1), jnp.concatenate([maps, maps], axis=0))
+    terms = terms + map_add
     lane = lane_ids(PQ)
     left = lane < HEAD_SIZE
-    content = query + content_ref[...]
+    content = query + vectors_ref[7:8, :]
     position = terms[:, :LANES] * cos_ref[...] + terms[:, LANES : 2 * LANES] * sin_ref[...]
     side = query_side_ref[...]
     typed = (lane >= 3) & (lane < 6)
@@ -641,7 +676,7 @@
             join_ref[h, rows, LANES:] = jnp.where(inside, extra, kept).astype(BF16)
 
 
-def attend_forward(query, pairs, maps, map_add, content, query_side, key_side, phase, cosm, sinm):
+def attend_forward(query, pairs, relative, vectors, query_side, key_side, phase, cosm, sinm):
     whole = lambda shape: pl.BlockSpec(shape, lambda i: (0, 0))
     return pl.pallas_call(
         attend_kernel,
@@ -650,9 +685,8 @@
             pl.BlockSpec((PQ, LANES), lambda i: (0, i)),
             pl.BlockSpec((LEN, LANES), lambda i: (0, i)),
             pl.BlockSpec((LEN, LANES), lambda i: (0, i + PAIRS)),
-            pl.BlockSpec((1, 2 * LANES, 6 * LANES), lambda i: (i, 0, 0)),
-            pl.BlockSpec((1, 1, 6 * LANES), lambda i: (i, 0, 0)),
-            pl.BlockSpec((1, LANES), lambda i: (0, i)),
+            pl.BlockSpec((LANES, HEAD_SIZE), lambda i: (i, 0)),
+            pl.BlockSpec((VECTORS, LANES), lambda i: (0, i)),
             whole((PQ, LANES)),
             whole((LEN, LANES)),
             whole((LEN, LANES)),
@@ -678,7 +712,727 @@
         ),
         compiler_params=pltpu.CompilerParams(vmem_limit_bytes=56 * 2**20),
         name="attend_forward",
-    )(query, pairs, pairs, maps, map_add, content, query_side, key_side, phase, cosm, sinm)
+    )(query, pairs, pairs, relative, vectors, query_side, key_side, phase, cosm, sinm)
+
+
+MESH = pl.DeviceIdType.MESH
+SUM_ROWS = 48
+STAGES = ("core", "y", "x", "near", "far", "far_back", "near_back", "x_back")
+SMALL_ROWS = 16
+SMALL_COLUMNS = 1024
+
+
+class Place:
+    def __init__(self):
+        self.seq, self.dp = lax.axis_index("seq"), lax.axis_index("dp")
+        self.core, self.y = self.dp % 2, self.dp // 2
+        self.x, self.near, self.far = self.seq % 2, (self.seq // 2) % 2, self.seq // 4
+        self.partner = {
+            "core": (self.seq, self.dp + 1 - 2 * self.core),
+            "y": (self.seq, self.dp + 2 - 4 * self.y),
+            "x": (self.seq + 1 - 2 * self.x, self.dp),
+            "near": (self.seq + 2 - 4 * self.near, self.dp),
+            "far": (self.seq + 4 - 8 * self.far, self.dp),
+        }
+
+    def peers(self):
+        return [((self.seq + k) % SG, self.dp) for k in range(1, SG)]
+
+    def greet(self):
+        barrier = pltpu.get_barrier_semaphore()
+        others = [self.partner["core"], self.partner["y"], *self.peers()]
+        for device in others:
+            pl.semaphore_signal(barrier, inc=1, device_id=device, device_id_type=MESH)
+        pl.semaphore_wait(barrier, len(others))
+
+
+def add_rows(target, addend, rows):
+    def step(i, carry):
+        at = pl.ds(pl.multiple_of(i * SUM_ROWS, 16), SUM_ROWS)
+        left, right = target(at), addend(at)
+        left[...] = left[...] + right[...]
+        return carry
+
+    lax.fori_loop(0, rows // SUM_ROWS, step, 0)
+
+
+class Chunk:
+    def __init__(self, place, index, source, rows, columns, buffers, send, receive, local):
+        self.place, self.source, self.rows, self.columns = place, source, rows, columns
+        self.own, self.from_core, self.from_y, self.from_x, self.from_near, self.from_far, self.full = buffers
+        self.send_at = lambda stage, k=0: send.at[index, STAGES.index(stage) + (8 if k else 0)]
+        self.receive_at = lambda stage, k=0: receive.at[index, STAGES.index(stage) + (8 if k else 0)]
+        self.local = lambda k: local.at[index, k]
+        half, quarter = rows // 2, rows // 4
+        self.my_columns = pl.ds(pl.multiple_of(place.x * (columns // 2), 128), columns // 2)
+        self.other_columns = pl.ds(
+            pl.multiple_of((1 - place.x) * (columns // 2), 128), columns // 2
+        )
+        self.my_half = pl.multiple_of(place.near * half, 16)
+        self.my_quarter = pl.multiple_of(place.near * half + place.far * quarter, 16)
+
+    def remote(self, stage, source, target, k=0):
+        return pltpu.make_async_remote_copy(
+            src_ref=source,
+            dst_ref=target,
+            send_sem=self.send_at(stage, k),
+            recv_sem=self.receive_at(stage, k),
+            device_id=self.place.partner[stage.split("_")[0]],
+            device_id_type=MESH,
+        )
+
+    def locals(self):
+        if self.own is None:
+            return []
+        return [
+            pltpu.make_async_copy(
+                self.source(2 * k + self.place.core), self.own.at[k], self.local(k)
+            )
+            for k in range(2)
+        ]
+
+    def copies(self, stage):
+        place, rows = self.place, self.rows
+        half, quarter = rows // 2, rows // 4
+        if stage == "core":
+            return [
+                self.remote(
+                    stage, self.source(2 * k + 1 - place.core), self.from_core.at[k], k
+                )
+                for k in range(2)
+            ]
+        if stage == "y":
+            return [self.remote(stage, self.from_core.at[1 - place.y], self.from_y)]
+        if stage == "x":
+            return [self.remote(stage, self.from_y.at[:, self.other_columns], self.from_x)]
+        if stage == "near":
+            other = pl.ds(pl.multiple_of((1 - place.near) * half, 16), half)
+            return [self.remote(stage, self.from_x.at[other, :], self.from_near)]
+        if stage == "far":
+            other = pl.ds(pl.multiple_of((1 - place.far) * quarter, 16), quarter)
+            return [self.remote(stage, self.from_near.at[other, :], self.from_far)]
+        if stage == "far_back":
+            mine = self.full.at[pl.ds(self.my_quarter, quarter), self.my_columns]
+            return [self.remote(stage, self.from_far, mine)]
+        if stage == "near_back":
+            mine = self.full.at[pl.ds(self.my_half, half), self.my_columns]
+            return [self.remote(stage, mine, mine)]
+        mine = self.full.at[:, self.my_columns]
+        return [self.remote(stage, mine, mine)]
+
+    def start(self, stage):
+        if stage == "core":
+            for copy in self.locals():
+                copy.start()
+        for copy in self.copies(stage):
+            copy.start()
+
+    def finish(self, stage):
+        place, rows = self.place, self.rows
+        half, quarter = rows // 2, rows // 4
+        for copy in self.copies(stage):
+            copy.wait_recv()
+        if stage == "core":
+            for copy in self.locals():
+                copy.wait()
+            for k in range(2):
+                kept = (
+                    self.source(2 * k + place.core) if self.own is None else self.own.at[k]
+                )
+                add_rows(
+                    lambda at: self.from_core.at[k, at, :], lambda at: kept.at[at, :], rows
+                )
+        elif stage == "y":
+            add_rows(
+                lambda at: self.from_y.at[at, :],
+                lambda at: self.from_core.at[place.y, at, :],
+                rows,
+            )
+        elif stage == "x":
+            add_rows(
+                lambda at: self.from_x.at[at, :],
+                lambda at: self.from_y.at[at, self.my_columns],
+                rows,
+            )
+        elif stage == "near":
+            add_rows(
+                lambda at: self.from_near.at[at, :],
+                lambda at: self.from_x.at[
+                    pl.ds(pl.multiple_of(at.start + self.my_half, 16), SUM_ROWS), :
+                ],
+                half,
+            )
+        elif stage == "far":
+            begin = place.far * quarter
+            add_rows(
+                lambda at: self.from_far.at[at, :],
+                lambda at: self.from_near.at[
+                    pl.ds(pl.multiple_of(at.start + begin, 16), SUM_ROWS), :
+                ],
+                quarter,
+            )
+
+    def place_piece(self):
+        def step(i, carry):
+            at = pl.ds(pl.multiple_of(i * SUM_ROWS, 16), SUM_ROWS)
+            to = pl.ds(pl.multiple_of(i * SUM_ROWS + self.my_quarter, 16), SUM_ROWS)
+            self.full[to, self.my_columns] = self.from_far[at, :]
+            return carry
+
+        lax.fori_loop(0, self.rows // 4 // SUM_ROWS, step, 0)
+
+    def step(self, stage):
+        at = STAGES.index(stage)
+        if at > 0:
+            self.finish(STAGES[at - 1])
+        if stage == "far_back":
+            self.place_piece()
+        self.start(stage)
+
+    def close(self, stages):
+        for stage in stages:
+            for copy in self.copies(stage):
+                copy.wait_send()
+
+
+DOWN, UP = STAGES[:5], STAGES[5:]
+WHOLE = 3
+
+
+def down_buffers(rows, columns, own):
+    buffer = lambda *shape: pltpu.VMEM(shape, BF16)
+    return [
+        *([buffer(2, rows, columns)] if own else []),
+        buffer(2, rows, columns),
+        buffer(rows, columns),
+        buffer(rows, columns // 2),
+        buffer(rows // 2, columns // 2),
+        buffer(rows // 4, columns // 2),
+    ]
+
+
+def grad_chunks():
+    quarter = MODEL_WIDTH // 4
+    half = MODEL_WIDTH // 2
+    early = [
+        (0, MODEL_WIDTH, 0, 0, half, MODEL_WIDTH),
+        (0, MODEL_WIDTH, half, 0, half, MODEL_WIDTH),
+        (1, quarter, 0, 0, quarter, FF // 2),
+        (1, quarter, 0, FF // 2, quarter, FF // 2),
+        (2, quarter, 0, 0, quarter, MODEL_WIDTH),
+    ]
+    late = [(j, quarter, 0, 0, quarter, MODEL_WIDTH) for j in (3, 4, 5)]
+    return early, late
+
+
+def chunk_source(grad, chunk):
+    _, owner_rows, row, column, rows, columns = chunk
+
+    def source(owner):
+        begin = pl.multiple_of(owner * owner_rows + row, 16)
+        return grad.at[pl.ds(begin, rows), pl.ds(column, columns)]
+
+    return source
+
+
+SEND_ORDER = (4, 3, 5, 2, 6, 1, 7, 0)
+
+
+def finish_kernel(
+    grad_query_ref,
+    grad_key_ref,
+    grad_value_ref,
+    tokens_ref,
+    pooled_ref,
+    grad_first_ref,
+    pool_ref,
+    weights_ref,
+    small_ref,
+    *refs,
+):
+    early, late = grad_chunks()
+    early = early[WHOLE:]
+    pieces, refs = refs[: len(early)], refs[len(early) :]
+    tokens_out, small_out, refs = refs[0], refs[1], refs[2:]
+    count = len(early) + len(late)
+    outs, refs = refs[:count], refs[count:]
+    fulls, refs = refs[:count], refs[count:]
+    buffers, refs = refs[: 5 * len(late)], refs[5 * len(late) :]
+    (
+        tokens_stage,
+        late_grads,
+        send,
+        receive,
+        token_send,
+        token_receive,
+        token_local,
+        small_core,
+        small_y,
+        small_all,
+        small_send,
+        small_receive,
+    ) = refs
+    place = Place()
+    place.greet()
+    first = []
+    for i, chunk in enumerate(early):
+        kept = [None, None, None, None, None, pieces[i], fulls[i]]
+        first.append(Chunk(place, i, None, *chunk[4:], kept, send, receive, None))
+    second = []
+    for j, chunk in enumerate(late):
+        i = len(early) + j
+        kept = [None, *buffers[5 * j : 5 * j + 5], fulls[i]]
+        source = chunk_source(late_grads.at[j], chunk)
+        second.append(Chunk(place, i, source, *chunk[4:], kept, send, receive, None))
+    for item in first:
+        item.place_piece()
+        item.start("far_back")
+
+    moved = []
+
+    def send_tokens(k):
+        to = (place.seq + k) % SG
+        block = LEN // SG
+        rows = pl.ds(pl.multiple_of(to * block, block), block)
+        pooled_rows = pl.ds(pl.multiple_of(to * (block // 2), block // 2), block // 2)
+        weight = lambda j: weights_ref[:, j * MODEL_WIDTH : (j + 1) * MODEL_WIDTH]
+        grad_pooled = grad_first_ref[pooled_rows, :] + mm(
+            grad_query_ref[pooled_rows, :], weight(0), NT
+        )
+        high, low = split(grad_pooled)
+        total = mm(grad_key_ref[rows, :], weight(1), NT)
+        total += mm(grad_value_ref[rows, :], weight(2), NT)
+        total += mm(pool_ref[to], high, TN) + mm(pool_ref[to], low, TN)
+        tokens_stage[to] = total.astype(BF16)
+        if k == 0:
+            copy = pltpu.make_async_copy(
+                tokens_stage.at[to], tokens_out.at[place.seq], token_local
+            )
+        else:
+            copy = pltpu.make_async_remote_copy(
+                src_ref=tokens_stage.at[to],
+                dst_ref=tokens_out.at[place.seq],
+                send_sem=token_send.at[k - 1],
+                recv_sem=token_receive.at[k - 1],
+                device_id=(to, place.dp),
+                device_id_type=MESH,
+            )
+        copy.start()
+        moved.append(copy)
+
+    for k in SEND_ORDER[:3]:
+        send_tokens(k)
+    for item in first:
+        item.step("near_back")
+    for k in SEND_ORDER[3:6]:
+        send_tokens(k)
+    for item in first:
+        item.step("x_back")
+    for k in SEND_ORDER[6:]:
+        send_tokens(k)
+
+    def small_copy(source, target, slot, device):
+        return pltpu.make_async_remote_copy(
+            src_ref=source,
+            dst_ref=target,
+            send_sem=small_send.at[slot],
+            recv_sem=small_receive.at[slot],
+            device_id=device,
+            device_id_type=MESH,
+        )
+
+    core_copies = [
+        small_copy(
+            small_ref.at[2 * k + 1 - place.core], small_core.at[k], k, place.partner["core"]
+        )
+        for k in range(2)
+    ]
+    for copy in core_copies:
+        copy.start()
+    operands = [
+        (pooled_ref, grad_query_ref),
+        (tokens_ref, grad_key_ref),
+        (tokens_ref, grad_value_ref),
+    ]
+    for j, (left, right) in enumerate(operands):
+        for r in range(0, MODEL_WIDTH, 256):
+            late_grads[j, r : r + 256, :] = mm(left[:, r : r + 256], right[...], TN).astype(BF16)
+        second[j].start("core")
+    for k, copy in enumerate(core_copies):
+        copy.wait_recv()
+        small_core[k] += small_ref[2 * k + place.core]
+    y_copy = small_copy(small_core.at[1 - place.y], small_y, 2, place.partner["y"])
+    y_copy.start()
+    for item in second:
+        item.step("y")
+    y_copy.wait_recv()
+    small_all[place.seq] = small_core[place.y] + small_y[...]
+    small_copies = []
+    for k, device in enumerate(place.peers()):
+        copy = small_copy(small_all.at[place.seq], small_all.at[place.seq], 3 + k, device)
+        copy.start()
+        small_copies.append(copy)
+    for stage in STAGES[2:]:
+        for item in second:
+            item.step(stage)
+
+    for item, out in zip(first, outs):
+        item.finish(STAGES[-1])
+        out[...] = item.full[...]
+        item.close(UP)
+    for copy in small_copies:
+        copy.wait_recv()
+    total = small_all[0]
+    for k in range(1, SG):
+        total = total + small_all[k]
+    small_out[...] = total
+    for item, out in zip(second, outs[len(first) :]):
+        item.finish(STAGES[-1])
+        out[...] = item.full[...]
+        item.close(STAGES)
+    for copy in [*core_copies, y_copy, *small_copies]:
+        copy.wait_send()
+    for copy in moved:
+        copy.wait()
+
+
+def finish(
+    grad_query, grad_key, grad_value, tokens, pooled, grad_first, pool, weights, small, pieces
+):
+    anywhere = pl.BlockSpec(memory_space=pl.ANY)
+    early, late = grad_chunks()
+    early = early[WHOLE:]
+    chunks = early + late
+    count = len(chunks)
+    small_shape = (SMALL_ROWS, SMALL_COLUMNS)
+    inside = pl.BlockSpec(memory_space=pltpu.VMEM)
+    out_tokens = (SG, LEN // SG, MODEL_WIDTH)
+    return pl.pallas_call(
+        finish_kernel,
+        in_specs=[inside] * (9 + len(early)),
+        out_specs=[anywhere, inside, *[inside] * count],
+        out_shape=[
+            jax.ShapeDtypeStruct(out_tokens, BF16),
+            jax.ShapeDtypeStruct(small_shape, F32),
+            *[jax.ShapeDtypeStruct(chunk[4:], BF16) for chunk in chunks],
+        ],
+        scratch_shapes=[
+            *[pltpu.VMEM(chunk[4:], BF16) for chunk in chunks],
+            *[buffer for chunk in late for buffer in down_buffers(*chunk[4:], False)],
+            pltpu.VMEM(out_tokens, BF16),
+            pltpu.VMEM((3, MODEL_WIDTH, MODEL_WIDTH), BF16),
+            pltpu.SemaphoreType.DMA((count, 16)),
+            pltpu.SemaphoreType.DMA((count, 16)),
+            pltpu.SemaphoreType.DMA((SG - 1,)),
+            pltpu.SemaphoreType.DMA((SG - 1,)),
+            pltpu.SemaphoreType.DMA,
+            pltpu.VMEM((2, *small_shape), F32),
+            pltpu.VMEM(small_shape, F32),
+            pltpu.VMEM((SG, *small_shape), F32),
+            pltpu.SemaphoreType.DMA((SG + 2,)),
+            pltpu.SemaphoreType.DMA((SG + 2,)),
+        ],
+        compiler_params=pltpu.CompilerParams(
+            collective_id=3, has_side_effects=True, vmem_limit_bytes=58 * 2**20
+        ),
+        name="finish",
+    )(
+        grad_query,
+        grad_key,
+        grad_value,
+        tokens,
+        pooled,
+        grad_first,
+        pool,
+        weights,
+        small,
+        *pieces,
+    )
+
+
+FF_STEP = 512
+FF_TILES = FF // FF_STEP
+ROW_TILES = PQ // ROWS
+
+
+def row_norm(value):
+    centred = value - jnp.mean(value, axis=1, keepdims=True)
+    inverse = lax.rsqrt(jnp.mean(centred * centred, axis=1, keepdims=True) + norm_eps)
+    return centred * inverse, inverse
+
+
+def row_norm_back(scaled, normed, inverse):
+    along = jnp.mean(scaled * normed, axis=1, keepdims=True)
+    return inverse * (scaled - jnp.mean(scaled, axis=1, keepdims=True) - normed * along)
+
+
+def gelu_pieces(value):
+    rate = math.sqrt(2.0 / math.pi)
+    square = value * value
+    bend = jnp.tanh(rate * value * (1.0 + 0.044715 * square))
+    half = 0.5 * (1.0 + bend)
+    slope = half + (0.5 * rate) * value * (1.0 - bend * bend) * (1.0 + 0.134145 * square)
+    return value * half, slope
+
+
+def mlp_kernel(
+    mixture_ref,
+    pooled_ref,
+    upstream_ref,
+    output_weight_ref,
+    inner_weight_ref,
+    outer_weight_ref,
+    vectors_ref,
+    inner_add_ref,
+    output_ref,
+    grad_mixture_ref,
+    grad_first_ref,
+    grad_outer_ref,
+    grad_inner_ref,
+    grad_output_ref,
+    sums_ref,
+    inner_sums_ref,
+    active,
+    slopes,
+    grad_expanded,
+    hidden_low,
+    grad_branch,
+    grad_attention,
+    output_stage,
+    mixture_stage,
+    first_stage,
+    send,
+    receive,
+    local,
+):
+    step = pl.program_id(0)
+    place = Place()
+    block = PQ // SG
+    tile = (step + place.seq // 2 + 1) % ROW_TILES
+    begin = pl.multiple_of(tile * ROWS, ROWS)
+
+    def output_copy(to):
+        return pltpu.make_async_remote_copy(
+            src_ref=output_stage.at[to],
+            dst_ref=output_ref.at[place.seq],
+            send_sem=send.at[to],
+            recv_sem=receive.at[place.seq],
+            device_id=(to, place.dp),
+            device_id_type=MESH,
+        )
+
+    def kept_copy():
+        return pltpu.make_async_copy(
+            output_stage.at[place.seq], output_ref.at[place.seq], local.at[0]
+        )
+
+    def row_copies():
+        rows = pl.ds(begin, ROWS)
+        return [
+            pltpu.make_async_copy(
+                mixture_stage.at[rows, :], grad_mixture_ref.at[rows, :], local.at[1 + 2 * tile]
+            ),
+            pltpu.make_async_copy(
+                first_stage.at[rows, :], grad_first_ref.at[rows, :], local.at[2 + 2 * tile]
+            ),
+        ]
+
+    @pl.when(step == 0)
+    def _():
+        place.greet()
+
+    @pl.when(step < ROW_TILES)
+    def _():
+        rows = pl.ds(begin, ROWS)
+        vector = lambda j: vectors_ref[j : j + 1, :]
+        output_add, outer_add, gain_one, shift_one, gain_two, shift_two = map(vector, range(1, 7))
+        attention = mm(mixture_ref[rows, :], output_weight_ref[...]) + output_add
+        normed_one, inverse_one = row_norm(pooled_ref[rows, :] + attention)
+        hidden = normed_one * gain_one + shift_one
+        low_hidden = hidden.astype(BF16)
+        hidden_low[rows, :] = low_hidden
+        branch = jnp.zeros((ROWS, MODEL_WIDTH), F32)
+        for j in range(FF_TILES):
+            part = slice(j * FF_STEP, (j + 1) * FF_STEP)
+            expanded = mm(low_hidden, inner_weight_ref[:, part]) + inner_add_ref[:, part]
+            value, slope = gelu_pieces(expanded)
+            low_value = value.astype(BF16)
+            active[rows, part] = low_value
+            slopes[:, part] = slope
+            branch += mm(low_value, outer_weight_ref[part, :])
+        normed_two, inverse_two = row_norm(hidden + (branch + outer_add))
+        result = (normed_two * gain_two + shift_two).astype(BF16)
+        for k in range(ROWS // block):
+            to = tile * (ROWS // block) + k
+            output_stage[to] = result[k * block : (k + 1) * block]
+
+            @pl.when(to == place.seq)
+            def _():
+                kept_copy().start()
+
+            @pl.when(to != place.seq)
+            def _():
+                output_copy(to).start()
+
+        upstream = upstream_ref[rows, :].astype(F32)
+        grad_second = row_norm_back(upstream * gain_two, normed_two, inverse_two)
+        low_branch = grad_second.astype(BF16)
+        grad_branch[rows, :] = low_branch
+        grad_hidden = grad_second
+        inner_sums = []
+        for j in range(FF_TILES):
+            part = slice(j * FF_STEP, (j + 1) * FF_STEP)
+            grad_active = mm(low_branch, outer_weight_ref[part, :], NT)
+            low_grad = (slopes[:, part] * grad_active).astype(BF16)
+            grad_expanded[rows, part] = low_grad
+            inner_sums.append(jnp.sum(low_grad.astype(F32), axis=0, keepdims=True))
+            grad_hidden += mm(low_grad, inner_weight_ref[:, part], NT)
+        grad_first = row_norm_back(grad_hidden * gain_one, normed_one, inverse_one)
+        first_stage[rows, :] = grad_first
+        low_attention = grad_first.astype(BF16)
+        grad_attention[rows, :] = low_attention
+        mixture_stage[rows, :] = mm(low_attention, output_weight_ref[...], NT).astype(BF16)
+        for copy in row_copies():
+            copy.start()
+        row = lambda v: jnp.sum(v, axis=0, keepdims=True)
+        sums = jnp.concatenate(
+            [
+                row(low_attention.astype(F32)),
+                row(low_branch.astype(F32)),
+                row(grad_hidden * normed_one),
+                row(grad_hidden),
+                row(upstream * normed_two),
+                row(upstream),
+                jnp.zeros((2, MODEL_WIDTH), F32),
+            ],
+            axis=0,
+        )
+        inner_sum = jnp.concatenate(inner_sums, axis=1)
+
+        @pl.when(step == 0)
+        def _():
+            sums_ref[...] = sums
+            inner_sums_ref[...] = inner_sum
+
+        @pl.when(step > 0)
+        def _():
+            sums_ref[...] += sums
+            inner_sums_ref[...] += inner_sum
+
+    for j in range(FF_TILES):
+
+        @pl.when(step == ROW_TILES + j)
+        def _():
+            part = slice(j * FF_STEP, (j + 1) * FF_STEP)
+            grad_outer_ref[...] = mm(active[:, part], grad_branch[...], TN).astype(BF16)
+            grad_inner_ref[...] = mm(hidden_low[...], grad_expanded[:, part], TN).astype(BF16)
+            if j == 0:
+                grad_output_ref[...] = mm(mixture_ref[...], grad_attention[...], TN).astype(BF16)
+
+    @pl.when(step == ROW_TILES + FF_TILES - 1)
+    def _():
+        for t in range(ROW_TILES):
+            rows = pl.ds(t * ROWS, ROWS)
+            pltpu.make_async_copy(
+                mixture_stage.at[rows, :], grad_mixture_ref.at[rows, :], local.at[1 + 2 * t]
+            ).wait()
+            pltpu.make_async_copy(
+                first_stage.at[rows, :], grad_first_ref.at[rows, :], local.at[2 + 2 * t]
+            ).wait()
+        kept_copy().wait()
+        for k in range(1, SG):
+            other = (place.seq + k) % SG
+            output_copy(other).wait_send()
+            pltpu.make_async_remote_copy(
+                src_ref=output_stage.at[other],
+                dst_ref=output_ref.at[other],
+                send_sem=send.at[other],
+                recv_sem=receive.at[other],
+                device_id=(other, place.dp),
+                device_id_type=MESH,
+            ).wait_recv()
+
+
+def mlp(mixture, pooled, upstream, output_weight, inner_weight, outer_weight, vectors, inner_add):
+    fixed = lambda shape: pl.BlockSpec(shape, lambda i: (0, 0), pipeline_mode=pl.Buffered(1))
+    still = lambda shape: pl.BlockSpec(shape, lambda i: (0, 0))
+    anywhere = pl.BlockSpec(memory_space=pl.ANY)
+    out_shape = (SG, PQ // SG, MODEL_WIDTH)
+    late = lambda i: jnp.maximum(i - ROW_TILES, 0)
+    whole = (PQ, MODEL_WIDTH)
+    square = (MODEL_WIDTH, MODEL_WIDTH)
+    return pl.pallas_call(
+        mlp_kernel,
+        grid=(ROW_TILES + FF_TILES,),
+        in_specs=[
+            fixed(whole),
+            fixed(whole),
+            fixed(whole),
+            fixed(square),
+            fixed((MODEL_WIDTH, FF)),
+            fixed((FF, MODEL_WIDTH)),
+            fixed((VECTORS, MODEL_WIDTH)),
+            fixed((1, FF)),
+        ],
+        out_specs=[
+            anywhere,
+            anywhere,
+            anywhere,
+            pl.BlockSpec((FF_STEP, MODEL_WIDTH), lambda i: (late(i), 0)),
+            pl.BlockSpec((MODEL_WIDTH, FF_STEP), lambda i: (0, late(i))),
+            still(square),
+            still((8, MODEL_WIDTH)),
+            still((1, FF)),
+        ],
+        out_shape=[
+            jax.ShapeDtypeStruct(out_shape, BF16),
+            jax.ShapeDtypeStruct(whole, BF16),
+            jax.ShapeDtypeStruct(whole, F32),
+            jax.ShapeDtypeStruct((FF, MODEL_WIDTH), BF16),
+            jax.ShapeDtypeStruct((MODEL_WIDTH, FF), BF16),
+            jax.ShapeDtypeStruct(square, BF16),
+            jax.ShapeDtypeStruct((8, MODEL_WIDTH), F32),
+            jax.ShapeDtypeStruct((1, FF), F32),
+        ],
+        scratch_shapes=[
+            pltpu.VMEM((PQ, FF), BF16),
+            pltpu.VMEM((ROWS, FF), F32),
+            pltpu.VMEM((PQ, FF), BF16),
+            pltpu.VMEM(whole, BF16),
+            pltpu.VMEM(whole, BF16),
+            pltpu.VMEM(whole, BF16),
+            pltpu.VMEM(out_shape, BF16),
+            pltpu.VMEM(whole, BF16),
+            pltpu.VMEM(whole, F32),
+            pltpu.SemaphoreType.DMA((SG,)),
+            pltpu.SemaphoreType.DMA((SG,)),
+            pltpu.SemaphoreType.DMA((1 + 2 * ROW_TILES,)),
+        ],
+        cost_estimate=pl.CostEstimate(
+            flops=2 * PQ * MODEL_WIDTH * (3 * MODEL_WIDTH + 6 * FF),
+            bytes_accessed=40_000_000,
+            transcendentals=PQ * FF,
+        ),
+        compiler_params=pltpu.CompilerParams(
+            collective_id=1, has_side_effects=True, vmem_limit_bytes=60 * 2**20
+        ),
+        name="mlp",
+    )(mixture, pooled, upstream, output_weight, inner_weight, outer_weight, vectors, inner_add)
+
+
+SLOTS = 2 * (PQ // ROWS)
+EARLY_SLOTS = {}
+for _i, _steps in enumerate(
+    (
+        (3, 12, 17, 20, 23, 26, 29, 34),
+        (6, 20, 25, 28, 31, 34, 37, 42),
+        (9, 28, 33, 36, 39, 42, 45, 48),
+        (12, 36, 41, 44, 48),
+        (14, 41, 45, 47, 48),
+    )
+):
+    for _stage, _slot in zip((*STAGES[1 : len(_steps)], None), _steps):
+        EARLY_SLOTS.setdefault(_slot, []).append((_i, _stage))
 
 
 def attend_back_kernel(
@@ -688,24 +1442,56 @@
     query_ref,
     mixture_ref,
     grad_ref,
-    map_back_ref,
-    rows_ref,
+    relative_ref,
+    vectors_ref,
     query_side_ref,
     key_side_ref,
     phase_ref,
     cos_ref,
     sin_ref,
+    grad_outer_ref,
+    grad_inner_ref,
+    grad_output_ref,
     grad_query_ref,
     grad_key_ref,
     grad_value_ref,
     sums_ref,
     grad_map_ref,
-    key_join,
-    value_join,
-    key_total,
-    value_total,
-    join_grads,
+    *refs,
 ):
+    early, _ = grad_chunks()
+    sent, refs = refs[: len(early)], refs[len(early) :]
+    key_join, value_join, key_total, value_total, join_grads, *refs = refs
+    fulls, refs = refs[:WHOLE], refs[WHOLE:]
+    buffers, (send, receive, local) = refs[: 6 * len(early)], refs[6 * len(early) :]
+    pair = pl.program_id(0)
+    place = Place()
+    grads = (grad_outer_ref, grad_inner_ref, grad_output_ref)
+    work = []
+    for i, chunk in enumerate(early):
+        kept = [*buffers[6 * i : 6 * i + 6], fulls[i] if i < WHOLE else None]
+        source = chunk_source(grads[chunk[0]], chunk)
+        work.append(Chunk(place, i, source, *chunk[4:], kept, send, receive, local))
+
+    def exchange(slot):
+        for i, stage in EARLY_SLOTS.get(slot, ()):
+            if stage is not None:
+                work[i].step(stage)
+            elif i < WHOLE:
+                work[i].finish(STAGES[-1])
+                sent[i][...] = work[i].full[...]
+                work[i].close(STAGES)
+            else:
+                work[i].finish(DOWN[-1])
+                sent[i][...] = work[i].from_far[...]
+                work[i].close(DOWN)
+
+    @pl.when(pair == 0)
+    def _():
+        place.greet()
+        for item in work:
+            item.start("core")
+
     scale = HEAD_SIZE ** (-0.5)
     key_left = lane_ids(LEN) < HEAD_SIZE
     tile_lane = lane_ids(ROWS)
@@ -719,6 +1505,13 @@
         part = slice(h * HEAD_SIZE, (h + 1) * HEAD_SIZE)
         for i in range(PQ // ROWS):
             rows = slice(i * ROWS, (i + 1) * ROWS)
+            for slot in EARLY_SLOTS:
+                if slot % SLOTS == h * (PQ // ROWS) + i:
+
+                    @pl.when(pair == slot // SLOTS)
+                    def _():
+                        exchange(slot)
+
             join = join_ref[h, rows, :]
             grad = jnp.where(mine, grad_ref[rows, :].astype(F32), 0.0)
             dot = -jnp.sum(grad * mixture_ref[rows, :].astype(F32), axis=1, keepdims=True)
@@ -754,7 +1547,9 @@
     position = jnp.where(left, rounded[1], rounded[0])
     turned = jnp.concatenate([position * cos_ref[...], position * sin_ref[...]], axis=1)
     turned_high, turned_low = split(turned)
-    shifted_grad = mm(turned_high, map_back_ref[0]) + mm(turned_low, map_back_ref[0])
+    plain, swapped = pair_maps(relative_ref[...])
+    maps = jnp.concatenate([plain, swapped], axis=1)
+    shifted_grad = mm(turned_high, maps, NT) + mm(turned_low, maps, NT)
     side = query_side_ref[...]
     sames, others = [], []
     for h in range(2):
@@ -765,10 +1560,10 @@
         others.append((other * scale).astype(BF16).astype(F32))
     same = jnp.where(left, sames[0], sames[1])
     other = jnp.where(left, others[0], others[1])
-    position_add = rows_ref[0, 0:1, :]
-    type_add = rows_ref[0, 1:2, :]
-    type_other = rows_ref[0, 2:3, :]
-    type_same = rows_ref[0, 3:4, :]
+    position_add = vectors_ref[8:9, :]
+    type_add = vectors_ref[9:10, :]
+    type_other = vectors_ref[10:11, :]
+    type_same = vectors_ref[11:12, :]
     typed_grad = same * type_same + other * type_other
     grad_query_ref[...] = (content + shifted_grad + typed_grad).astype(BF16)
     query = query_ref[...]
@@ -787,10 +1582,32 @@
     sums_ref[0, 4:5, :] = row(kinds * same)
     sums_ref[0, 5:6, :] = row(grad_value_ref[...].astype(F32))
 
+    @pl.when(pair == PAIRS - 1)
+    def _():
+        exchange(PAIRS * SLOTS)
+
 
 def attend_backward(
-    join, pairs, query, mixture, grad, map_back, rows, query_side, key_side, phase, cosm, sinm
+    join,
+    pairs,
+    query,
+    mixture,
+    grad,
+    relative,
+    vectors,
+    query_side,
+    key_side,
+    phase,
+    cosm,
+    sinm,
+    grads,
 ):
+    early, _ = grad_chunks()
+    anywhere = pl.BlockSpec(memory_space=pl.ANY)
+    shapes = [
+        chunk[4:] if i < WHOLE else (chunk[4] // 4, chunk[5] // 2)
+        for i, chunk in enumerate(early)
+    ]
     whole = lambda shape: pl.BlockSpec(shape, lambda i: (0, 0))
     return pl.pallas_call(
         attend_back_kernel,
@@ -802,13 +1619,14 @@
             pl.BlockSpec((PQ, LANES), lambda i: (0, i)),
             pl.BlockSpec((PQ, LANES), lambda i: (0, i)),
             pl.BlockSpec((PQ, LANES), lambda i: (0, i)),
-            pl.BlockSpec((1, 2 * LANES, LANES), lambda i: (i, 0, 0)),
-            pl.BlockSpec((1, 8, LANES), lambda i: (i, 0, 0)),
+            pl.BlockSpec((LANES, HEAD_SIZE), lambda i: (i, 0)),
+            pl.BlockSpec((VECTORS, LANES), lambda i: (0, i)),
             whole((PQ, LANES)),
             whole((LEN, LANES)),
             whole((LEN, LANES)),
             whole((PQ, LANES)),
             whole((PQ, LANES)),
+            *[anywhere] * 3,
         ],
         out_specs=[
             pl.BlockSpec((PQ, LANES), lambda i: (0, i)),
@@ -816,6 +1634,7 @@
             pl.BlockSpec((LEN, LANES), lambda i: (0, i)),
             pl.BlockSpec((1, 8, LANES), lambda i: (i, 0, 0)),
             pl.BlockSpec((1, LANES, 2 * LANES), lambda i: (i, 0, 0)),
+            *[whole(shape) for shape in shapes],
         ],
         out_shape=[
             jax.ShapeDtypeStruct((PQ, MODEL_WIDTH), BF16),
@@ -823,6 +1642,7 @@
             jax.ShapeDtypeStruct((LEN, MODEL_WIDTH), BF16),
             jax.ShapeDtypeStruct((PAIRS, 8, LANES), F32),
             jax.ShapeDtypeStruct((PAIRS, LANES, 2 * LANES), F32),
+            *[jax.ShapeDtypeStruct(shape, BF16) for shape in shapes],
         ],
         scratch_shapes=[
             pltpu.VMEM((LEN, 2 * LANES), BF16),
@@ -830,13 +1650,20 @@
             pltpu.VMEM((LANES, LEN), F32),
             pltpu.VMEM((LANES, LEN), F32),
             pltpu.VMEM((2, PQ, 2 * LANES), F32),
+            *[pltpu.VMEM(chunk[4:], BF16) for chunk in early[:WHOLE]],
+            *[buffer for chunk in early for buffer in down_buffers(*chunk[4:], True)],
+            pltpu.SemaphoreType.DMA((len(early), 16)),
+            pltpu.SemaphoreType.DMA((len(early), 16)),
+            pltpu.SemaphoreType.DMA((len(early), 2)),
         ],
         cost_estimate=pl.CostEstimate(
             flops=10 * HEAD_COUNT * PQ * LEN * 256,
             bytes_accessed=32_000_000,
             transcendentals=HEAD_COUNT * PQ * LEN,
         ),
-        compiler_params=pltpu.CompilerParams(vmem_limit_bytes=58 * 2**20),
+        compiler_params=pltpu.CompilerParams(
+            collective_id=2, has_side_effects=True, vmem_limit_bytes=58 * 2**20
+        ),
         name="attend_backward",
     )(
         join,
@@ -845,13 +1672,14 @@
         query,
         mixture,
         grad,
-        map_back,
-        rows,
+        relative,
+        vectors,
         query_side,
         key_side,
         phase,
         cosm,
         sinm,
+        *grads,
     )
 
 
@@ -860,28 +1688,58 @@
     return jnp.concatenate([second, first], axis=axis)
 
 
-def pair_maps(relative, table):
-    relative = relative.reshape(PAIRS, 2, HEAD_SIZE, HEAD_SIZE)
-    nothing = jnp.zeros((PAIRS, HEAD_SIZE, HEAD_SIZE), F32)
-    turned = swap_halves(relative, 3)
-
-    def crossed(value):
-        top = jnp.concatenate([nothing, value[:, 0]], axis=2)
-        bottom = jnp.concatenate([value[:, 1], nothing], axis=2)
-        return jnp.concatenate([top, bottom], axis=1)
-
-    plain, swapped = crossed(relative), crossed(turned)
-    table = table.reshape(PAIRS, 2, 2, HEAD_SIZE)
-    columns = jnp.arange(LANES)
-    wanted = ((columns >= 3) & (columns < 6)).astype(F32)
-    kinds = []
-    for h in range(2):
-        for b in (1, 0):
-            vector = table[:, h, b]
-            zero = jnp.zeros_like(vector)
-            full = jnp.concatenate([vector, zero] if h == 0 else [zero, vector], axis=1)
-            kinds.append(full[:, :, None] * wanted[None, None, :])
-    return plain, swapped, kinds
+def labels_kernel(labels_ref, out_ref, stage, send, receive):
+    place = Place()
+    place.greet()
+    copies = []
+    for k in range(1, SG):
+        to = (place.seq + k) % SG
+        copy = pltpu.make_async_remote_copy(
+            src_ref=labels_ref.at[to],
+            dst_ref=stage.at[place.seq],
+            send_sem=send.at[k - 1],
+            recv_sem=receive.at[k - 1],
+            device_id=(to, place.dp),
+            device_id_type=MESH,
+        )
+        copy.start()
+        copies.append(copy)
+    stage[place.seq] = labels_ref[place.seq]
+    for copy in copies:
+        copy.wait()
+    out_ref[...] = stage[...]
+
+
+def move_labels(labels):
+    inside = pl.BlockSpec(memory_space=pltpu.VMEM)
+    return pl.pallas_call(
+        labels_kernel,
+        in_specs=[inside],
+        out_specs=inside,
+        out_shape=jax.ShapeDtypeStruct(labels.shape, jnp.int32),
+        scratch_shapes=[
+            pltpu.VMEM(labels.shape, jnp.int32),
+            pltpu.SemaphoreType.DMA((SG - 1,)),
+            pltpu.SemaphoreType.DMA((SG - 1,)),
+        ],
+        compiler_params=pltpu.CompilerParams(collective_id=4, has_side_effects=True),
+        name="labels",
+    )(labels)
+
+
+def angle_tables():
+    half = HEAD_SIZE // 2
+    rate = np.float32(-math.log(10000.0) / half)
+    frequency = np.exp(np.arange(half, dtype=np.float32) * rate)
+    angle = np.arange(LEN, dtype=np.float32)[:, None] * frequency[None, :]
+    cos, sin = np.cos(angle), np.sin(angle)
+    phase = np.concatenate([cos, sin, cos, sin], axis=1)
+    cos, sin = cos[0::2], sin[0::2]
+    return (
+        jnp.asarray(phase).astype(BF16),
+        np.concatenate([cos, -cos, cos, -cos], axis=1),
+        np.concatenate([sin, sin, sin, sin], axis=1),
+    )
 
 
 def sequence_body(
@@ -925,58 +1783,41 @@
         ],
         axis=1,
     )
-    labels = lax.all_to_all(labels, "seq", split_axis=0, concat_axis=0, tiled=True)
+    labels = move_labels(labels)
+    tokens, labels = lax.optimization_barrier((tokens, labels))
     rows = lax.all_to_all(tokens, "seq", split_axis=0, concat_axis=0, tiled=True)
-    small = jnp.concatenate(
-        [
-            low(value).reshape(-1)
-            for value in (
-                value_bias,
-                output_bias,
-                outer_bias,
-                attention_norm_gain,
-                first_shift,
-                second_gain,
-                second_shift,
-                content_bias,
-                position_bias,
-                type_bias,
-                inner_bias,
-                relative_kernel,
-                type_embed,
-            )
-        ]
-    )
-    small = lax.all_gather(small.reshape(1, -1), "dp", axis=0, tiled=True)
+    flat = lambda value: low(value).reshape(1, part)
+    vectors = [
+        flat(value)
+        for value in (
+            value_bias,
+            output_bias,
+            outer_bias,
+            attention_norm_gain,
+            first_shift,
+            second_gain,
+            second_shift,
+            content_bias,
+            position_bias,
+            type_bias,
+            type_embed[:, 0],
+            type_embed[:, 1],
+        )
+    ]
+    vectors.append(jnp.zeros((VECTORS - len(vectors), part), BF16))
+    vectors = lax.all_gather(jnp.concatenate(vectors, axis=0), "dp", axis=1, tiled=True)
+    vectors = vectors.astype(F32)
+    inner_add = lax.all_gather(low(inner_bias).reshape(1, -1), "dp", axis=1, tiled=True)
+    inner_add = inner_add.astype(F32)
+    relative = low(relative_kernel).reshape(part, HEAD_SIZE)
+    relative = lax.all_gather(relative, "dp", axis=0, tiled=True)
     first = jnp.concatenate([low(query_weight), low(key_weight), low(value_weight)], axis=1)
     first = lax.all_gather(first, "dp", axis=0, tiled=True)
-    next_weights = jnp.concatenate([low(output_weight), low(inner_weight)], axis=1)
-    next_weights = lax.all_gather(next_weights, "dp", axis=0, tiled=True)
+    inner_low = lax.all_gather(low(inner_weight), "dp", axis=0, tiled=True)
+    output_low = lax.all_gather(low(output_weight), "dp", axis=0, tiled=True)
     outer_low = lax.all_gather(low(outer_weight), "dp", axis=0, tiled=True)
 
-    def take(start, size):
-        return small[:, start : start + size].astype(F32)
-
-    vectors = [take(part * j, part).reshape(1, MODEL_WIDTH) for j in range(10)]
-    (
-        value_add,
-        output_add,
-        outer_add,
-        gain_one,
-        shift_one,
-        gain_two,
-        shift_two,
-        content_add,
-        position_add,
-        type_add,
-    ) = vectors
-    place = 10 * part
-    inner_add = take(place, FF // owners).reshape(1, FF)
-    place += FF // owners
     kernel_size = HEAD_COUNT * HEAD_SIZE * HEAD_SIZE // owners
-    relative = take(place, kernel_size).reshape(HEAD_COUNT, HEAD_SIZE, HEAD_SIZE)
-    place += kernel_size
-    table = take(place, HEAD_COUNT * 2 * HEAD_SIZE // owners).reshape(HEAD_COUNT, 2, HEAD_SIZE)
 
     segment_row = labels[:, 0:2].reshape(LEN)
     type_row = labels[:, 2:4].reshape(LEN)
@@ -1003,125 +1844,67 @@
         jnp.where(columns == query_docs, 0.0, FAR),
         (columns == 3 + classes(query_types, first_type, last_type)).astype(F32),
     )
-    frequency = frequencies()
-    key_angle = jnp.arange(LEN, dtype=F32)[:, None] * frequency[None, :]
-    phase = jnp.concatenate([jnp.cos(key_angle), jnp.sin(key_angle)], axis=1).astype(BF16)
-    phase = jnp.concatenate([phase, phase], axis=1)
-    query_angle = (2.0 * jnp.arange(PQ, dtype=F32))[:, None] * frequency[None, :]
-    cos, sin = jnp.cos(query_angle), jnp.sin(query_angle)
-    cosm = jnp.concatenate([cos, -cos, cos, -cos], axis=1)
-    sinm = jnp.concatenate([sin, sin, sin, sin], axis=1)
-
-    plain, swapped, kinds = pair_maps(relative, table)
-    stacked = jnp.concatenate([plain, swapped, *kinds], axis=2)
-    maps = low(jnp.concatenate([stacked, stacked], axis=1))
-    pair_vector = lambda vector: vector.reshape(PAIRS, 1, LANES)
-    position_pairs, type_pairs = pair_vector(position_add), pair_vector(type_add)
-    product = partial(jnp.einsum, "pke,pef->pkf", precision=highest)
-    map_add = jnp.concatenate(
-        [
-            product(position_pairs, stacked[:, :, : 2 * LANES]),
-            product(type_pairs, stacked[:, :, 2 * LANES :]),
-        ],
-        axis=2,
-    )
-    map_back = low(
-        jnp.concatenate([plain.transpose(0, 2, 1), swapped.transpose(0, 2, 1)], axis=1)
-    )
-    table_pairs = table.reshape(PAIRS, 2, 2, HEAD_SIZE).transpose(0, 2, 1, 3)
-    table_pairs = table_pairs.reshape(PAIRS, 2, LANES)
-    row_terms = jnp.concatenate(
-        [position_pairs, type_pairs, table_pairs, jnp.zeros((PAIRS, 4, LANES), F32)], axis=1
-    )
-
-    block = 2 * rows.shape[1] // 2
+    phase, cosm, sinm = angle_tables()
+
+    block = rows.shape[1]
     pooled_block = block // 2
     at = jnp.arange(block, dtype=jnp.int32)[None, None, :]
     want = 2 * jnp.arange(pooled_block, dtype=jnp.int32)[None, :, None]
     half = jnp.where(pair_same, 0.5, 1.0)[:, :, None]
-    pool = jnp.where(at == want, half, jnp.where(at == want + 1, 1.0 - half, 0.0)).astype(BF16)
-    pool = jnp.where(at == want + 1, jnp.where(pair_same, 0.5, 0.0)[:, :, None].astype(BF16), pool)
+    other_half = jnp.where(pair_same, 0.5, 0.0)[:, :, None]
+    pool = jnp.where(at == want, half, jnp.where(at == want + 1, other_half, 0.0)).astype(BF16)
 
     pooled = jnp.einsum("cpt,ctd->cpd", pool, rows, preferred_element_type=F32)
     pooled = pooled.reshape(PQ, MODEL_WIDTH)
     pooled_low = low(pooled)
     token_rows = rows.reshape(LEN, MODEL_WIDTH)
     query = mm(pooled_low, first[:, :MODEL_WIDTH])
+    value_add = vectors[0:1]
     pair_add = jnp.concatenate([jnp.zeros_like(value_add), value_add], axis=1)
     pairs = low(mm(token_rows, first[:, MODEL_WIDTH:]) + pair_add)
     mixture, join = attend_forward(
-        query, pairs, maps, map_add, content_add, query_side, key_side, phase, cosm, sinm
-    )
-
-    cotangent, _ = lax.optimization_barrier((cotangent, pairs))
+        query, pairs, relative, vectors, query_side, key_side, phase, cosm, sinm
+    )
+
+    cotangent, _ = lax.optimization_barrier((cotangent, labels))
     cotangent = lax.all_to_all(cotangent, "seq", split_axis=0, concat_axis=0, tiled=True)
-    upstream = cotangent.reshape(PQ, MODEL_WIDTH).astype(F32)
-
-    output_low, inner_low = next_weights[:, :MODEL_WIDTH], next_weights[:, MODEL_WIDTH:]
-    attention = mm(mixture, output_low) + output_add
-    hidden, normed_one, inverse_one = norm_forward(pooled + attention, gain_one, shift_one)
-    hidden_low = low(hidden)
-    expanded = mm(hidden_low, inner_low) + inner_add
-    active = low(jax.nn.gelu(expanded, approximate=True))
-    branch = mm(active, outer_low) + outer_add
-    result, normed_two, inverse_two = norm_forward(hidden + branch, gain_two, shift_two)
-    output = low(result).reshape(SG, PQ // SG, MODEL_WIDTH)
-    output = lax.all_to_all(output, "seq", split_axis=0, concat_axis=0, tiled=True)
-
-    total = lambda value: jnp.sum(value, axis=0)
-    grad_gain_two = total(upstream * normed_two)
-    grad_shift_two = total(upstream)
-    grad_second = norm_backward(upstream, normed_two, inverse_two, gain_two)
-    grad_branch = low(grad_second)
-    grad_outer_weight = mm(active, grad_branch, TN)
-    grad_outer_bias = total(grad_branch.astype(F32))
-    grad_active = mm(grad_branch, outer_low, NT)
-    _, gelu_pull = jax.vjp(partial(jax.nn.gelu, approximate=True), expanded)
-    grad_expanded = low(gelu_pull(grad_active)[0])
-    grad_inner_weight = mm(hidden_low, grad_expanded, TN)
-    grad_inner_bias = total(grad_expanded.astype(F32))
-
-    def shared(value):
-        value = lax.psum_scatter(low(value), "dp", scatter_dimension=0, tiled=True)
-        return lax.psum(value, "seq").astype(F32)
-
-    owned_outer = shared(grad_outer_weight)
-    owned_inner = shared(grad_inner_weight)
-    grad_hidden = grad_second + mm(grad_expanded, inner_low, NT)
-    grad_gain_one = total(grad_hidden * normed_one)
-    grad_shift_one = total(grad_hidden)
-    grad_first = norm_backward(grad_hidden, normed_one, inverse_one, gain_one)
-    grad_attention = low(grad_first)
-    grad_output_weight = mm(mixture, grad_attention, TN)
-    grad_output_bias = total(grad_attention.astype(F32))
-    grad_mixture = low(mm(grad_attention, output_low, NT))
-
-    grad_query, grad_key, grad_value, sums, grad_map = attend_backward(
+    upstream = cotangent.reshape(PQ, MODEL_WIDTH)
+
+    (
+        output,
+        grad_mixture,
+        grad_first,
+        grad_outer_weight,
+        grad_inner_weight,
+        grad_output_weight,
+        row_sums,
+        grad_inner_bias,
+    ) = mlp(
+        mixture, pooled, upstream, output_low, inner_low, outer_low, vectors, inner_add
+    )
+    (
+        grad_output_bias,
+        grad_outer_bias,
+        grad_gain_one,
+        grad_shift_one,
+        grad_gain_two,
+        grad_shift_two,
+    ) = [row_sums[j] for j in range(6)]
+    grad_query, grad_key, grad_value, sums, grad_map, *pieces = attend_backward(
         join,
         pairs,
         query,
         mixture,
         grad_mixture,
-        map_back,
-        row_terms,
+        relative,
+        vectors,
         query_side,
         key_side,
         phase,
         cosm,
         sinm,
-    )
-    grad_query_weight = mm(pooled_low, grad_query, TN)
-    grad_key_weight = mm(token_rows, grad_key, TN)
-    grad_value_weight = mm(token_rows, grad_value, TN)
-    grad_pooled = grad_first + mm(grad_query, first[:, :MODEL_WIDTH], NT)
-    grad_direct = mm(grad_key, first[:, MODEL_WIDTH : 2 * MODEL_WIDTH], NT)
-    grad_direct = grad_direct + mm(grad_value, first[:, 2 * MODEL_WIDTH :], NT)
-    high_pooled, low_pooled = split(grad_pooled.reshape(SG, pooled_block, MODEL_WIDTH))
-    spread = partial(jnp.einsum, "cpt,cpd->ctd", preferred_element_type=F32)
-    spread_sum = spread(pool, high_pooled) + spread(pool, low_pooled)
-    grad_tokens = low(grad_direct.reshape(SG, block, MODEL_WIDTH) + spread_sum)
-    grad_tokens = lax.all_to_all(grad_tokens, "seq", split_axis=0, concat_axis=0, tiled=True)
-
+        (grad_outer_weight, grad_inner_weight, grad_output_weight),
+    )
     crossed = grad_map.reshape(PAIRS, 2, HEAD_SIZE, 2, 2, HEAD_SIZE)
     grad_relative = jnp.stack(
         [
@@ -1153,18 +1936,27 @@
         ],
         axis=1,
     )
-    wide = 4 * MODEL_WIDTH
-    small_rows = small_grads.shape[1] // wide
-    late = jnp.concatenate(
-        [grad_query_weight, grad_key_weight, grad_value_weight, grad_output_weight], axis=1
-    ).reshape(owners, part, wide)
-    spare = jnp.zeros((owners, -small_rows % 8, wide), F32)
-    late = jnp.concatenate(
-        [late, small_grads.reshape(owners, small_rows, wide), spare], axis=1
-    ).reshape(-1, wide)
-    owned_late = shared(late)
-    squares = [owned_late[:part, j * MODEL_WIDTH : (j + 1) * MODEL_WIDTH] for j in range(4)]
-    small_owned = owned_late[part : part + small_rows].reshape(-1)
+    count = small_grads.shape[1]
+    room = SMALL_ROWS * SMALL_COLUMNS
+    small_grads = jnp.pad(small_grads, ((0, 0), (0, room - count)))
+    grad_tokens, small_owned, *owned = finish(
+        grad_query,
+        grad_key,
+        grad_value,
+        token_rows,
+        pooled_low,
+        grad_first,
+        pool,
+        first,
+        small_grads.reshape(owners, SMALL_ROWS, SMALL_COLUMNS),
+        pieces[WHOLE:],
+    )
+    owned = [*pieces[:WHOLE], *owned]
+    owned_outer = jnp.concatenate(owned[0:2], axis=0).astype(F32)
+    owned_inner = jnp.concatenate(owned[2:4], axis=1).astype(F32)
+    owned_output, *squares = [value.astype(F32) for value in owned[4:]]
+    squares.append(owned_output)
+    small_owned = small_owned.reshape(-1)
     place = 0
     pieces = []
     for size in [part] * 10 + [FF // owners, kernel_size, HEAD_COUNT * 2 * HEAD_SIZE // owners]:
@@ -1172,7 +1964,7 @@
         place += size
     heads = HEAD_COUNT // owners
     return (
-        output.reshape(SG, PQ // SG, MODEL_WIDTH),
+        output,
         grad_tokens,
         squares[0],
         squares[1],

time: 661 us -> 500 us (0.76)
  Pallas kernels: 119 us -> 348 us
  waiting for transfers between devices: 244 us -> 36 us
  matrix products: 126 us -> 13.7 us
  local copies, waits for them, and re-layouts: 57.3 us -> 23.8 us
  other arithmetic: 60.8 us -> 32.7 us
  starting transfers between devices: 27.4 us -> 9.35 us
  blocking collectives: 6.1 us -> 15.9 us
    pallas_call x0 -> x3, Pallas kernels: none -> 196 us  [the longest x1 120 us: finish(): pl.pallas_call(finish_kernel, in_specs=[inside] * (9 + len(early)), out_s...]
    all_to_all x3 -> x0, waiting for transfers between devices: 126 us -> none  [the longest x1 105 us: sequence_body(): lax.all_to_all(grad_tokens, 'seq', split_axis=0, concat_axis=0, tiled=True)]
    dot_general x17 -> x2, matrix products: 115 us -> 13 us  [mm(): return lax.dot_general(left, right, dims, preferred_element_type=F32)]
    psum x1 -> x0, waiting for transfers between devices: 87.4 us -> none  [shared(): return lax.psum(value, 'seq').astype(F32)]
    pallas_call x1, Pallas kernels: 73.7 us -> 106 us  [attend_backward(): pl.pallas_call(attend_back_kernel, grid=(PAIRS,), in_specs=[pl.BlockSpec(...]
    all_to_all x3 -> x0, starting transfers between devices: 16.8 us -> none  [the longest x1 7.25 us: sequence_body(): lax.all_to_all(labels, 'seq', split_axis=0, concat_axis=0, tiled=True)]
    concatenate x9 -> x0, other arithmetic: 16.6 us -> none  [the longest x1 5.97 us: sequence_body(): jnp.concatenate([late, small_grads.reshape(owners, small_rows, wide), spa...]
    concatenate x13 -> x2, local copies, waits for them, and re-layouts: 12.8 us -> 0.07 us  [the longest x1 0.06 us: sequence_body(): jnp.concatenate(vectors, axis=0)]
  transfers between devices with their start and end apart: 12 -> 6, of which waited for: 5 -> 1; matrix products, arithmetic and copies ran while one was open for 28% -> 7% of each run, Pallas kernels for 18% -> 11%
where the time goes in v3:
time: 500 us; the launch traced here: 494 us
  Pallas kernels  348 us (70%)
  waiting for transfers between devices  36 us (7%)
  other arithmetic  32.7 us (7%)
  local copies, waits for them, and re-layouts  23.8 us (5%)
  blocking collectives  15.9 us (3%)
  between operations  15 us (3%)
  matrix products  13.7 us (3%)
  starting transfers between devices  9.35 us (2%)
    pallas_call x1, Pallas kernels, finish(): pl.pallas_call(finish_kernel, in_specs=[inside] * (9 + len(early)), out_s...  120 us
    pallas_call x1, Pallas kernels, attend_backward(): pl.pallas_call(attend_back_kernel, grid=(PAIRS,), in_specs=[pl.BlockSpec(...  106 us
    pallas_call x1, Pallas kernels, mlp(): pl.pallas_call(mlp_kernel, grid=(ROW_TILES + FF_TILES,), in_specs=[fixed(...  64.5 us
    pallas_call x1, Pallas kernels, attend_forward(): pl.pallas_call(attend_kernel, grid=(PAIRS,), in_specs=[pl.BlockSpec((PQ,...  46 us
    all_to_all x1, waiting for transfers between devices, sequence_body(): lax.all_to_all(tokens, 'seq', split_axis=0, concat_axis=0, tiled=True)  35.9 us
    dot_general x2, matrix products, mm(): return lax.dot_general(left, right, dims, preferred_element_type=F32)  13 us
    convert_element_type x19, other arithmetic, sequence_body(): low = lambda value: value.astype(BF16)  10.6 us
    pallas_call x1, Pallas kernels, move_labels(): pl.pallas_call(labels_kernel, in_specs=[inside], out_specs=inside, out_sh...  10.6 us
  transfers between devices with their start and end apart: 6, of which 1 were waited for; matrix products, arithmetic and copies ran while one was open for 7% of the time, Pallas kernels for 11%

profile of v3, /device:TPU:0, one launch (start us, length us, event | category | flops | bytes accessed | tf_op | source)
XLA Modules:
  0.0 494.3 jit_solution(14014340825423564624)
XLA Ops:
  7.2 1.1 convert_element_type.123
  8.3 1.1 convert_element_type.124
  9.4 1.2 convert_element_type.125
  10.7 1.0 pad_maximum_fusion
  11.7 1.8 convert_element_type.144
  13.7 1.2 convert_element_type.145
  14.9 0.2 slice.158
  15.1 0.2 slice.160
  15.3 0.2 slice.159
  15.5 0.7 stack.40.labels_ref
  16.2 10.6 %labels.1 = s32[8,7,128]{2,1,0:T(8,128)} custom-call(s32[8,7,128]{2,1,0:T(8,128)} %stack.40.labels_ref), custom_call_target="tpu_custom_call" | custom-call | tf_op jit(solution)/shard_map/labels/pallas_call | solution.py:1715
  26.8 4.7 all-to-all-start
  31.7 2.9 convert_element_type.146
  34.6 0.5 slice.211
  35.8 5.3 %all-gather.1 = bf16[4,192,16]{1,2,0:T(8,128)(2,1)S(1)} all-gather(bf16[1,192,16]{1,2,0:T(8,128)(2,1)S(1)} %bitcast.93), channel_id=1, replica_groups=mesh['seq'=8,'dp'=4] {'dp'}, dimensions={0}, use_global_device_ids=true | all-gather | bytes 30720 | tf_op jit(solution)/shard_map/all_gather | solution.py:1808
  41.5 5.2 %all-gather.3 = bf16[4,1,768]{2,1,0:T(2,128)(2,1)S(1)} all-gather(bf16[1,1,768]{2,1,0:T(2,128)(2,1)S(1)} %reshape.409), channel_id=2, replica_groups=mesh['seq'=8,'dp'=4] {'dp'}, dimensions={0}, use_global_device_ids=true | all-gather | bytes 7680 | tf_op jit(solution)/shard_map/all_gather | solution.py:1810
  46.6 5.4 %all-gather.2 = bf16[4,192,64]{1,2,0:T(8,128)(2,1)S(1)} all-gather(bf16[1,192,64]{1,2,0:T(8,128)(2,1)S(1)} %copy.71), channel_id=1, replica_groups=mesh['seq'=8,'dp'=4] {'dp'}, dimensions={0}, use_global_device_ids=true | all-gather | bytes 122880 | tf_op jit(solution)/shard_map/all_gather | solution.py:1813
  52.1 0.8 copy.72
  52.9 0.6 convert.6.inner_add_ref
  53.5 1.3 fusion.12
  54.8 0.6 fusion.13
  55.4 2.6 select_add_fusion
  58.0 2.6 compare_select_fusion.4
  60.7 1.1 convert_select_fusion.query_side_ref
  61.9 1.1 select_convert_fusion.pool_ref
  63.0 2.1 fusion.5.key_side_ref
  65.1 35.9 %all-to-all-done = bf16[8,256,768]{2,1,0:T(8,128)(2,1)S(1)} async-done(((bf16[8,256,768]{2,1,0:T(8,128)(2,1)}), bf16[8,256,768]{2,1,0:T(8,128)(2,1)S(1)}, u32[]{:S(2)}, u32[]{:S(2)}) %all-to-all-start) | async-done | bytes 3145760 | tf_op jit(solution)/shard_map/all_to_all | solution.py:1788
  101.0 4.5 all-to-all-start.1
  105.5 0.7 fusion.8
  106.2 1.7 copy-done.1
  107.9 1.3 bitcast_convert_fusion.pooled_ref
  109.2 8.7 %add_convert_fusion.key_ref.value_ref = bf16[2048,1536]{1,0:T(8,128)(2,1)} fusion(bf16[2048,768]{1,0:T(8,128)(2,1)S(1)} %bitcast.62, f32[1536]{0:T(1024)S(1)} %pad_reduce_fusion, bf16[768,2304]{1,0:T(8,128)(2,1)} %all-gather.9.cloned.1.call-done.weights_ref), kind=kOutput, calls=%fused_computation | convolution fusion | flops 4838129664 | bytes 11802624 | tf_op jit(solution)/shard_map/dot_general | solution.py:566
  117.9 4.3 fusion.1.query_ref
  122.2 46.0 %attend_forward.1 = (bf16[1024,768]{1,0:T(8,128)(2,1)}, bf16[12,1024,256]{2,1,0:T(8,128)(2,1)}) custom-call(f32[1024,768]{1,0:T(8,128)} %fusion.1.query_ref, bf16[2048,1536]{1,0:T(8,128)(2,1)} %add_convert_fusion.key_ref.value_ref, bf16[2048,1536]{1,0:T(8,128)(2,1)} %add_convert_fusion.key_ref.value_ref, bf16[768,64]{1,0:T(8,128)(2,1)} %bitcast.75, ...), custom_call_target="tpu_custom_call" | custom-call | flops 25769803776 | bytes 20000000 | tf_op jit(solution)/shard_map/attend_forward/pallas_call | solution.py:681
  168.3 64.5 %mlp.1 = (bf16[8,128,768]{2,1,0:T(8,128)(2,1)}, bf16[1024,768]{1,0:T(8,128)(2,1)}, f32[1024,768]{1,0:T(8,128)}, bf16[3072,768]{1,0:T(8,128)(2,1)}, bf16[768,3072...) custom-call(bf16[1024,768]{1,0:T(8,128)(2,1)} %get-tuple-element.53.mixture_ref, ...), custom_call_target="tpu_custom_call" | custom-call | flops 32614907904 | bytes 40000000 | tf_op jit(solution)/shard_map/mlp/pallas_call | solution.py:1364
  232.8 106.4 %attend_backward.1 = (bf16[1024,768]{1,0:T(8,128)(2,1)}, bf16[2048,768]{1,0:T(8,128)(2,1)}, bf16[2048,768]{1,0:T(8,128)(2,1)}, f32[6,8,128]{2,1,0:T(8,128)}, f32...) custom-call(bf16[12,1024,256]{2,1,0:T(8,128)(2,1)} %get-tuple-elemen, ...), custom_call_target="tpu_custom_call" | custom-call | flops 64424509440 | bytes 32000000 | tf_op jit(solution)/shard_map/attend_backward/pallas_call | solution.py:1612
  339.2 0.7 slice.188
  340.0 0.9 slice_reduce_fusion
  340.9 2.2 reshape.396
  343.1 0.9 fusion.9
  344.6 0.2 reshape_reshape.3
  345.8 0.5 broadcast.218
  346.3 0.7 reduce.30
  347.0 0.2 concatenate.55
  347.2 0.9 copy.84
  348.1 120.4 %finish.1 = (bf16[8,256,768]{2,1,0:T(8,128)(2,1)}, f32[16,1024]{1,0:T(8,128)}, bf16[192,1536]{1,0:T(8,128)(2,1)}, bf16[192,768]{1,0:T(8,128)(2,1)}, bf16[192,768...) custom-call(bf16[1024,768]{1,0:T(8,128)(2,1)} %get-tuple-element.61.grad_query_ref, ...), custom_call_target="tpu_custom_call" | custom-call | tf_op jit(solution)/shard_map/finish/pallas_call | solution.py:1110
  468.6 1.0 slice.197
  469.6 1.0 slice.202
  470.6 0.9 copy.82
  471.5 0.7 fusion.11
  472.1 0.6 slice.218
  472.7 1.8 convert_element_type.149
  474.5 1.8 convert_element_type.150
  476.3 0.9 convert_element_type.151
  477.2 0.9 convert_element_type.152
  478.1 0.7 reshape.401
  478.8 0.6 fusion.10
  479.4 0.6 slice.228
  479.9 1.6 maximum_convert_fusion.1
  481.5 1.7 maximum_convert_fusion
  483.2 0.2 copy-done.5
  483.4 1.1 copy.87
  484.5 1.2 copy-done.3
  485.7 1.7 copy.88
  (139 shorter events, 3.0 us)
Async XLA Ops:
  7.2 102.0 %all-gather.9.cloned.1.call-start = ((), (), s32[]{:S(2)}) async-start(), calls=%async_computation.2 | async-start | bytes 4423680 | tf_op jit(solution)/shard_map/all_gather | solution.py:1815
  9.4 4.2 copy-start.4
  11.7 156.5 %all-gather.11.cloned.1.call-start = ((), (), s32[]{:S(2)}) async-start(), calls=%async_computation.3 | async-start | bytes 1474560 | tf_op jit(solution)/shard_map/all_gather | solution.py:1817
  13.6 1.3 copy-start.15
  13.6 1.7 copy-start.16
  13.6 154.7 %all-gather.13.cloned.1.call-start = ((), (), s32[]{:S(2)}) async-start(), calls=%async_computation.4 | async-start | bytes 5898240 | tf_op jit(solution)/shard_map/all_gather | solution.py:1816
  26.8 74.2 %all-to-all-start = ((bf16[8,256,768]{2,1,0:T(8,128)(2,1)}), bf16[8,256,768]{2,1,0:T(8,128)(2,1)S(1)}, u32[]{:S(2)}, u32[]{:S(2)}) async-start(bf16[8,256,768]{2,1,0:T(8,128)(2,1)} %param.26), calls=%async_computation | async-start | bytes 6291456 | tf_op jit(solution)/shard_map/all_to_all | solution.py:1788
  31.4 3.1 copy-start.12
  31.5 3.6 copy-start.20
  31.5 3.8 copy-start.21
  31.5 3.9 copy-start.22
  31.5 4.0 copy-start.23
  31.5 4.1 copy-start.24
  31.5 4.1 copy-start.25
  31.5 4.1 copy-start.26
  31.5 4.1 copy-start.27
  31.5 4.1 copy-start.28
  31.6 4.2 copy-start.29
  31.6 4.2 copy-start.30
  31.6 9.7 %copy-start.13 = (f32[3,64,64]{2,1,0:T(8,128)S(1)}, f32[3,64,64]{2,1,0:T(8,128)}, u32[]{:S(2)}) copy-start(f32[3,64,64]{2,1,0:T(8,128)} %param.47) | copy-start | bytes 147460
  31.6 9.8 %copy-start.19 = (f32[768]{0:T(1024)S(1)}, f32[768]{0:T(1024)}, u32[]{:S(2)}) copy-start(f32[768]{0:T(1024)} %param.38) | copy-start | bytes 9220
  31.6 136.7 %all-gather.15.cloned.1.call-start = ((), (), s32[]{:S(2)}) async-start(), calls=%async_computation.5 | async-start | bytes 5898240 | tf_op jit(solution)/shard_map/all_gather | solution.py:1818
  41.3 59.7 %copy-start.14 = (f32[768,16]{0,1:T(8,128)}, f32[768,16]{0,1:T(8,128)S(1)}, u32[]{:S(2)}) copy-start(f32[768,16]{0,1:T(8,128)S(1)} %reshape.414) | copy-start | bytes 147460
  101.0 8.2 %copy-start = (bf16[8,256,768]{2,1,0:T(8,128)(2,1)}, bf16[8,256,768]{2,1,0:T(8,128)(2,1)S(1)}, u32[]{:S(2)}) copy-start(bf16[8,256,768]{2,1,0:T(8,128)(2,1)S(1)} %all-to-all-done) | copy-start | bytes 9437188
  101.0 67.2 %all-to-all-start.1 = ((bf16[8,128,768]{2,1,0:T(8,128)(2,1)}), bf16[8,128,768]{2,1,0:T(8,128)(2,1)}, u32[]{:S(2)}, u32[]{:S(2)}) async-start(bf16[8,128,768]{2,1,0:T(8,128)(2,1)} %param.29), calls=%async_computation.1 | async-start | bytes 3145728 | tf_op jit(solution)/shard_map/all_to_all | solution.py:1870
  106.2 1.7 copy-start.1
  109.2 8.7 %copy-start.2 = (bf16[1024,768]{1,0:T(8,128)(2,1)S(1)}, bf16[1024,768]{1,0:T(8,128)(2,1)}, u32[]{:S(2)}) copy-start(bf16[1024,768]{1,0:T(8,128)(2,1)} %bitcast_convert_fusion.pooled_ref) | copy-start | bytes 4718596
  344.1 1.1 copy-start.17
  344.1 2.2 copy-start.18
  468.5 7.8 %copy-start.11 = (bf16[192,768]{1,0:T(8,128)(2,1)S(1)}, bf16[192,768]{1,0:T(8,128)(2,1)}, u32[]{:S(2)}) copy-start(bf16[192,768]{1,0:T(8,128)(2,1)} %get-tuple-element.74) | copy-start | bytes 884740
  468.5 8.7 %copy-start.10 = (bf16[192,768]{1,0:T(8,128)(2,1)S(1)}, bf16[192,768]{1,0:T(8,128)(2,1)}, u32[]{:S(2)}) copy-start(bf16[192,768]{1,0:T(8,128)(2,1)} %get-tuple-element.75) | copy-start | bytes 884740
  468.5 11.4 %copy-start.7 = (bf16[384,768]{1,0:T(8,128)(2,1)S(1)}, bf16[384,768]{1,0:T(8,128)(2,1)}, u32[]{:S(2)}) copy-start(bf16[384,768]{1,0:T(8,128)(2,1)} %get-tuple-element.78) | copy-start | bytes 1769476
  468.6 11.4 %copy-start.8 = (bf16[384,768]{1,0:T(8,128)(2,1)S(1)}, bf16[384,768]{1,0:T(8,128)(2,1)}, u32[]{:S(2)}) copy-start(bf16[384,768]{1,0:T(8,128)(2,1)} %get-tuple-element.79) | copy-start | bytes 1769476
  477.2 4.3 copy-start.6
  477.2 4.3 copy-start.9
  481.5 1.9 copy-start.5
  483.2 2.5 copy-start.3
Sparse Core Ops, SparseCore 0:
  11.8 33.6 all-gather.8
  47.6 17.4 all-gather.10
  67.3 37.4 all-gather.12
  106.2 37.4 all-gather.14

commit v4 on v3

--- a/solution.py
+++ b/solution.py
@@ -591,6 +591,20 @@
     return plain, swapped
 
 
+def fold_maps(grads):
+    row = lax.broadcasted_iota(jnp.int32, (LANES, 2 * LANES), 0)
+    lane = lax.broadcasted_iota(jnp.int32, (LANES, 2 * LANES), 1)
+    crossed = (row < HEAD_SIZE) != (lane % LANES < HEAD_SIZE)
+    high, low = split(jnp.where(crossed, grads, 0.0))
+    row = lax.broadcasted_iota(jnp.int32, (2 * LANES, LANES), 0)
+    lane = lax.broadcasted_iota(jnp.int32, (2 * LANES, LANES), 1)
+    half = HEAD_SIZE // 2
+    at = row % HEAD_SIZE
+    partner = jnp.where(at < half, at + half, at - half)
+    fold = (jnp.where(row < LANES, at, partner) == lane).astype(BF16)
+    return mm(high, fold) + mm(low, fold)
+
+
 def kind_maps(vectors):
     row = lax.broadcasted_iota(jnp.int32, (VECTORS, 4 * LANES), 0)
     column = lax.broadcasted_iota(jnp.int32, (VECTORS, 4 * LANES), 1)
@@ -600,6 +614,391 @@
     row = lax.broadcasted_iota(jnp.int32, (LANES, 4 * LANES), 0)
     column = lax.broadcasted_iota(jnp.int32, (LANES, 4 * LANES), 1)
     return jnp.where((row < HEAD_SIZE) == (column < 2 * LANES), both, 0.0).astype(BF16)
+
+
+MESH = pl.DeviceIdType.MESH
+SUM_ROWS = 48
+STAGES = ("core", "y", "x", "near", "far", "far_back", "near_back", "x_back")
+
+
+class Place:
+    def __init__(self):
+        self.seq, self.dp = lax.axis_index("seq"), lax.axis_index("dp")
+        self.core, self.y = self.dp % 2, self.dp // 2
+        self.x, self.near, self.far = self.seq % 2, (self.seq // 2) % 2, self.seq // 4
+        self.partner = {
+            "core": (self.seq, self.dp + 1 - 2 * self.core),
+            "y": (self.seq, self.dp + 2 - 4 * self.y),
+            "x": (self.seq + 1 - 2 * self.x, self.dp),
+            "near": (self.seq + 2 - 4 * self.near, self.dp),
+            "far": (self.seq + 4 - 8 * self.far, self.dp),
+        }
+
+    def peers(self):
+        return [((self.seq + k) % SG, self.dp) for k in range(1, SG)]
+
+    def greet(self):
+        barrier = pltpu.get_barrier_semaphore()
+        others = [self.partner["core"], self.partner["y"], *self.peers()]
+        for device in others:
+            pl.semaphore_signal(barrier, inc=1, device_id=device, device_id_type=MESH)
+        pl.semaphore_wait(barrier, len(others))
+
+
+def add_rows(target, addend, rows):
+    def step(i, carry):
+        at = pl.ds(pl.multiple_of(i * SUM_ROWS, 16), SUM_ROWS)
+        left, right = target(at), addend(at)
+        left[...] = left[...] + right[...]
+        return carry
+
+    lax.fori_loop(0, rows // SUM_ROWS, step, 0)
+
+
+class Chunk:
+    def __init__(self, place, index, source, rows, columns, buffers, send, receive, local):
+        self.place, self.source, self.rows, self.columns = place, source, rows, columns
+        self.own, self.from_core, self.from_y, self.from_x, self.from_near, self.from_far, self.full = buffers
+        self.send_at = lambda stage, k=0: send.at[index, STAGES.index(stage) + (8 if k else 0)]
+        self.receive_at = lambda stage, k=0: receive.at[index, STAGES.index(stage) + (8 if k else 0)]
+        self.local = lambda k: local.at[index, k]
+        half, quarter = rows // 2, rows // 4
+        self.my_columns = pl.ds(pl.multiple_of(place.x * (columns // 2), 128), columns // 2)
+        self.other_columns = pl.ds(
+            pl.multiple_of((1 - place.x) * (columns // 2), 128), columns // 2
+        )
+        self.my_half = pl.multiple_of(place.near * half, 16)
+        self.my_quarter = pl.multiple_of(place.near * half + place.far * quarter, 16)
+
+    def remote(self, stage, source, target, k=0):
+        return pltpu.make_async_remote_copy(
+            src_ref=source,
+            dst_ref=target,
+            send_sem=self.send_at(stage, k),
+            recv_sem=self.receive_at(stage, k),
+            device_id=self.place.partner[stage.split("_")[0]],
+            device_id_type=MESH,
+        )
+
+    def locals(self):
+        if self.own is None:
+            return []
+        return [
+            pltpu.make_async_copy(
+                self.source(2 * k + self.place.core), self.own.at[k], self.local(k)
+            )
+            for k in range(2)
+        ]
+
+    def copies(self, stage):
+        place, rows = self.place, self.rows
+        half, quarter = rows // 2, rows // 4
+        if stage == "core":
+            return [
+                self.remote(
+                    stage, self.source(2 * k + 1 - place.core), self.from_core.at[k], k
+                )
+                for k in range(2)
+            ]
+        if stage == "y":
+            return [self.remote(stage, self.from_core.at[1 - place.y], self.from_y)]
+        if stage == "x":
+            return [self.remote(stage, self.from_y.at[:, self.other_columns], self.from_x)]
+        if stage == "near":
+            other = pl.ds(pl.multiple_of((1 - place.near) * half, 16), half)
+            return [self.remote(stage, self.from_x.at[other, :], self.from_near)]
+        if stage == "far":
+            other = pl.ds(pl.multiple_of((1 - place.far) * quarter, 16), quarter)
+            return [self.remote(stage, self.from_near.at[other, :], self.from_far)]
+        if stage == "far_back":
+            mine = self.full.at[pl.ds(self.my_quarter, quarter), self.my_columns]
+            return [self.remote(stage, self.from_far, mine)]
+        if stage == "near_back":
+            mine = self.full.at[pl.ds(self.my_half, half), self.my_columns]
+            return [self.remote(stage, mine, mine)]
+        mine = self.full.at[:, self.my_columns]
+        return [self.remote(stage, mine, mine)]
+
+    def start(self, stage):
+        if stage == "core":
+            for copy in self.locals():
+                copy.start()
+        for copy in self.copies(stage):
+            copy.start()
+
+    def finish(self, stage):
+        place, rows = self.place, self.rows
+        half, quarter = rows // 2, rows // 4
+        for copy in self.copies(stage):
+            copy.wait_recv()
+        if stage == "core":
+            for copy in self.locals():
+                copy.wait()
+            for k in range(2):
+                kept = (
+                    self.source(2 * k + place.core) if self.own is None else self.own.at[k]
+                )
+                add_rows(
+                    lambda at: self.from_core.at[k, at, :], lambda at: kept.at[at, :], rows
+                )
+        elif stage == "y":
+            add_rows(
+                lambda at: self.from_y.at[at, :],
+                lambda at: self.from_core.at[place.y, at, :],
+                rows,
+            )
+        elif stage == "x":
+            add_rows(
+                lambda at: self.from_x.at[at, :],
+                lambda at: self.from_y.at[at, self.my_columns],
+                rows,
+            )
+        elif stage == "near":
+            add_rows(
+                lambda at: self.from_near.at[at, :],
+                lambda at: self.from_x.at[
+                    pl.ds(pl.multiple_of(at.start + self.my_half, 16), SUM_ROWS), :
+                ],
+                half,
+            )
+        elif stage == "far":
+            begin = place.far * quarter
+            add_rows(
+                lambda at: self.from_far.at[at, :],
+                lambda at: self.from_near.at[
+                    pl.ds(pl.multiple_of(at.start + begin, 16), SUM_ROWS), :
+                ],
+                quarter,
+            )
+
+    def place_piece(self):
+        def step(i, carry):
+            at = pl.ds(pl.multiple_of(i * SUM_ROWS, 16), SUM_ROWS)
+            to = pl.ds(pl.multiple_of(i * SUM_ROWS + self.my_quarter, 16), SUM_ROWS)
+            self.full[to, self.my_columns] = self.from_far[at, :]
+            return carry
+
+        lax.fori_loop(0, self.rows // 4 // SUM_ROWS, step, 0)
+
+    def step(self, stage):
+        at = STAGES.index(stage)
+        if at > 0:
+            self.finish(STAGES[at - 1])
+        if stage == "far_back":
+            self.place_piece()
+        self.start(stage)
+
+    def close(self, stages):
+        for stage in stages:
+            for copy in self.copies(stage):
+                copy.wait_send()
+
+
+DOWN, UP = STAGES[:5], STAGES[5:]
+WHOLE = 3
+
+
+def down_buffers(rows, columns, own):
+    buffer = lambda *shape: pltpu.VMEM(shape, BF16)
+    return [
+        *([buffer(2, rows, columns)] if own else []),
+        buffer(2, rows, columns),
+        buffer(rows, columns),
+        buffer(rows, columns // 2),
+        buffer(rows // 2, columns // 2),
+        buffer(rows // 4, columns // 2),
+    ]
+
+
+def grad_chunks():
+    quarter = MODEL_WIDTH // 4
+    half = MODEL_WIDTH // 2
+    early = [
+        (0, MODEL_WIDTH, 0, 0, half, MODEL_WIDTH),
+        (0, MODEL_WIDTH, half, 0, half, MODEL_WIDTH),
+        (1, quarter, 0, 0, quarter, FF // 2),
+        (1, quarter, 0, FF // 2, quarter, FF // 2),
+        (2, quarter, 0, 0, quarter, MODEL_WIDTH),
+    ]
+    late = [(j, quarter, 0, 0, quarter, MODEL_WIDTH) for j in (3, 4, 5)]
+    late.insert(0, (6, quarter, 0, 0, quarter, 2 * LANES))
+    return early, late
+
+
+def chunk_source(grad, chunk):
+    _, owner_rows, row, column, rows, columns = chunk
+
+    def source(owner):
+        begin = pl.multiple_of(owner * owner_rows + row, 16)
+        return grad.at[pl.ds(begin, rows), pl.ds(column, columns)]
+
+    return source
+
+
+SEND_ORDER = (4, 3, 5, 2, 6, 1, 7, 0)
+
+
+def finish_kernel(
+    grad_query_ref,
+    grad_key_ref,
+    grad_value_ref,
+    tokens_ref,
+    pooled_ref,
+    grad_first_ref,
+    pool_ref,
+    weights_ref,
+    small_ref,
+    *refs,
+):
+    early, late = grad_chunks()
+    early = early[WHOLE:]
+    pieces, refs = refs[: len(early)], refs[len(early) :]
+    tokens_out, refs = refs[0], refs[1:]
+    count = len(early) + len(late)
+    outs, refs = refs[:count], refs[count:]
+    fulls, refs = refs[:count], refs[count:]
+    buffers, refs = refs[: 5 * len(late)], refs[5 * len(late) :]
+    (
+        tokens_stage,
+        late_grads,
+        send,
+        receive,
+        token_send,
+        token_receive,
+        token_local,
+    ) = refs
+    place = Place()
+    place.greet()
+    first = []
+    for i, chunk in enumerate(early):
+        kept = [None, None, None, None, None, pieces[i], fulls[i]]
+        first.append(Chunk(place, i, None, *chunk[4:], kept, send, receive, None))
+    second = []
+    for j, chunk in enumerate(late):
+        i = len(early) + j
+        kept = [None, *buffers[5 * j : 5 * j + 5], fulls[i]]
+        source = chunk_source(late_grads.at[j - 1] if j else small_ref, chunk)
+        second.append(Chunk(place, i, source, *chunk[4:], kept, send, receive, None))
+    for item in first:
+        item.place_piece()
+        item.start("far_back")
+    second[0].start("core")
+
+    moved = []
+
+    def send_tokens(k):
+        to = (place.seq + k) % SG
+        block = LEN // SG
+        rows = pl.ds(pl.multiple_of(to * block, block), block)
+        pooled_rows = pl.ds(pl.multiple_of(to * (block // 2), block // 2), block // 2)
+        weight = lambda j: weights_ref[:, j * MODEL_WIDTH : (j + 1) * MODEL_WIDTH]
+        grad_pooled = grad_first_ref[pooled_rows, :] + mm(
+            grad_query_ref[pooled_rows, :], weight(0), NT
+        )
+        high, low = split(grad_pooled)
+        total = mm(grad_key_ref[rows, :], weight(1), NT)
+        total += mm(grad_value_ref[rows, :], weight(2), NT)
+        total += mm(pool_ref[to], high, TN) + mm(pool_ref[to], low, TN)
+        tokens_stage[to] = total.astype(BF16)
+        if k == 0:
+            copy = pltpu.make_async_copy(
+                tokens_stage.at[to], tokens_out.at[place.seq], token_local
+            )
+        else:
+            copy = pltpu.make_async_remote_copy(
+                src_ref=tokens_stage.at[to],
+                dst_ref=tokens_out.at[place.seq],
+                send_sem=token_send.at[k - 1],
+                recv_sem=token_receive.at[k - 1],
+                device_id=(to, place.dp),
+                device_id_type=MESH,
+            )
+        copy.start()
+        moved.append(copy)
+
+    for k in SEND_ORDER[:3]:
+        send_tokens(k)
+    for item in first:
+        item.step("near_back")
+    for k in SEND_ORDER[3:6]:
+        send_tokens(k)
+    for item in first:
+        item.step("x_back")
+    for k in SEND_ORDER[6:]:
+        send_tokens(k)
+
+    operands = [
+        (pooled_ref, grad_query_ref),
+        (tokens_ref, grad_key_ref),
+        (tokens_ref, grad_value_ref),
+    ]
+    for j, (left, right) in enumerate(operands):
+        for r in range(0, MODEL_WIDTH, 256):
+            late_grads[j, r : r + 256, :] = mm(left[:, r : r + 256], right[...], TN).astype(BF16)
+        second[j + 1].start("core")
+        second[j].step("y")
+    second[len(late) - 1].step("y")
+    for stage in STAGES[2:]:
+        for item in second:
+            item.step(stage)
+
+    for item, out in zip(first, outs):
+        item.finish(STAGES[-1])
+        out[...] = item.full[...]
+        item.close(UP)
+    for item, out in zip(second, outs[len(first) :]):
+        item.finish(STAGES[-1])
+        out[...] = item.full[...]
+        item.close(STAGES)
+    for copy in moved:
+        copy.wait()
+
+
+def finish(
+    grad_query, grad_key, grad_value, tokens, pooled, grad_first, pool, weights, small, pieces
+):
+    anywhere = pl.BlockSpec(memory_space=pl.ANY)
+    early, late = grad_chunks()
+    early = early[WHOLE:]
+    chunks = early + late
+    count = len(chunks)
+    inside = pl.BlockSpec(memory_space=pltpu.VMEM)
+    out_tokens = (SG, LEN // SG, MODEL_WIDTH)
+    return pl.pallas_call(
+        finish_kernel,
+        in_specs=[inside] * (9 + len(early)),
+        out_specs=[anywhere, *[inside] * count],
+        out_shape=[
+            jax.ShapeDtypeStruct(out_tokens, BF16),
+            *[jax.ShapeDtypeStruct(chunk[4:], BF16) for chunk in chunks],
+        ],
+        scratch_shapes=[
+            *[pltpu.VMEM(chunk[4:], BF16) for chunk in chunks],
+            *[buffer for chunk in late for buffer in down_buffers(*chunk[4:], False)],
+            pltpu.VMEM(out_tokens, BF16),
+            pltpu.VMEM((3, MODEL_WIDTH, MODEL_WIDTH), BF16),
+            pltpu.SemaphoreType.DMA((count, 16)),
+            pltpu.SemaphoreType.DMA((count, 16)),
+            pltpu.SemaphoreType.DMA((SG - 1,)),
+            pltpu.SemaphoreType.DMA((SG - 1,)),
+            pltpu.SemaphoreType.DMA,
+        ],
+        compiler_params=pltpu.CompilerParams(
+            collective_id=3, has_side_effects=True, vmem_limit_bytes=58 * 2**20
+        ),
+        name="finish",
+    )(
+        grad_query,
+        grad_key,
+        grad_value,
+        tokens,
+        pooled,
+        grad_first,
+        pool,
+        weights,
+        small,
+        *pieces,
+    )
 
 
 def attend_kernel(
@@ -613,11 +1012,44 @@
     phase_ref,
     cos_ref,
     sin_ref,
+    cotangent_ref,
     mixture_ref,
     join_ref,
+    upstream_ref,
     key_join,
     value_join,
+    send,
+    receive,
+    local,
 ):
+    place = Place()
+
+    def upstream_copies():
+        copies = [
+            pltpu.make_async_copy(
+                cotangent_ref.at[place.seq], upstream_ref.at[place.seq], local
+            )
+        ]
+        for k in range(1, SG):
+            to = (place.seq + k) % SG
+            copies.append(
+                pltpu.make_async_remote_copy(
+                    src_ref=cotangent_ref.at[to],
+                    dst_ref=upstream_ref.at[place.seq],
+                    send_sem=send.at[k - 1],
+                    recv_sem=receive.at[k - 1],
+                    device_id=(to, place.dp),
+                    device_id_type=MESH,
+                )
+            )
+        return copies
+
+    @pl.when(pl.program_id(0) == 0)
+    def _():
+        place.greet()
+        for copy in upstream_copies():
+            copy.start()
+
     query = query_ref[...]
     high, low = split(query)
     plain, swapped = pair_maps(relative_ref[...])
@@ -675,8 +1107,15 @@
             inside = (tile_lane >= 6) & (tile_lane < 9)
             join_ref[h, rows, LANES:] = jnp.where(inside, extra, kept).astype(BF16)
 
-
-def attend_forward(query, pairs, relative, vectors, query_side, key_side, phase, cosm, sinm):
+    @pl.when(pl.program_id(0) == PAIRS - 1)
+    def _():
+        for copy in upstream_copies():
+            copy.wait()
+
+
+def attend_forward(
+    query, pairs, relative, vectors, query_side, key_side, phase, cosm, sinm, cotangent
+):
     whole = lambda shape: pl.BlockSpec(shape, lambda i: (0, 0))
     return pl.pallas_call(
         attend_kernel,
@@ -692,465 +1131,38 @@
             whole((LEN, LANES)),
             whole((PQ, LANES)),
             whole((PQ, LANES)),
+            pl.BlockSpec(memory_space=pl.ANY),
         ],
         out_specs=[
             pl.BlockSpec((PQ, LANES), lambda i: (0, i)),
             pl.BlockSpec((2, PQ, 2 * LANES), lambda i: (i, 0, 0)),
+            pl.BlockSpec(memory_space=pl.ANY),
         ],
         out_shape=[
             jax.ShapeDtypeStruct((PQ, MODEL_WIDTH), BF16),
             jax.ShapeDtypeStruct((HEAD_COUNT, PQ, 2 * LANES), BF16),
+            jax.ShapeDtypeStruct(cotangent.shape, BF16),
         ],
         scratch_shapes=[
             pltpu.VMEM((LEN, 2 * LANES), BF16),
             pltpu.VMEM((LEN, 2 * LANES), BF16),
+            pltpu.SemaphoreType.DMA((SG - 1,)),
+            pltpu.SemaphoreType.DMA((SG - 1,)),
+            pltpu.SemaphoreType.DMA,
         ],
         cost_estimate=pl.CostEstimate(
             flops=4 * HEAD_COUNT * PQ * LEN * 256,
             bytes_accessed=20_000_000,
             transcendentals=HEAD_COUNT * PQ * LEN,
         ),
-        compiler_params=pltpu.CompilerParams(vmem_limit_bytes=56 * 2**20),
+        compiler_params=pltpu.CompilerParams(
+            collective_id=5, has_side_effects=True, vmem_limit_bytes=56 * 2**20
+        ),
         name="attend_forward",
-    )(query, pairs, pairs, relative, vectors, query_side, key_side, phase, cosm, sinm)
-
-
-MESH = pl.DeviceIdType.MESH
-SUM_ROWS = 48
-STAGES = ("core", "y", "x", "near", "far", "far_back", "near_back", "x_back")
-SMALL_ROWS = 16
-SMALL_COLUMNS = 1024
-
-
-class Place:
-    def __init__(self):
-        self.seq, self.dp = lax.axis_index("seq"), lax.axis_index("dp")
-        self.core, self.y = self.dp % 2, self.dp // 2
-        self.x, self.near, self.far = self.seq % 2, (self.seq // 2) % 2, self.seq // 4
-        self.partner = {
-            "core": (self.seq, self.dp + 1 - 2 * self.core),
-            "y": (self.seq, self.dp + 2 - 4 * self.y),
-            "x": (self.seq + 1 - 2 * self.x, self.dp),
-            "near": (self.seq + 2 - 4 * self.near, self.dp),
-            "far": (self.seq + 4 - 8 * self.far, self.dp),
-        }
-
-    def peers(self):
-        return [((self.seq + k) % SG, self.dp) for k in range(1, SG)]
-
-    def greet(self):
-        barrier = pltpu.get_barrier_semaphore()
-        others = [self.partner["core"], self.partner["y"], *self.peers()]
-        for device in others:
-            pl.semaphore_signal(barrier, inc=1, device_id=device, device_id_type=MESH)
-        pl.semaphore_wait(barrier, len(others))
-
-
-def add_rows(target, addend, rows):
-    def step(i, carry):
-        at = pl.ds(pl.multiple_of(i * SUM_ROWS, 16), SUM_ROWS)
-        left, right = target(at), addend(at)
-        left[...] = left[...] + right[...]
-        return carry
-
-    lax.fori_loop(0, rows // SUM_ROWS, step, 0)
-
-
-class Chunk:
-    def __init__(self, place, index, source, rows, columns, buffers, send, receive, local):
-        self.place, self.source, self.rows, self.columns = place, source, rows, columns
-        self.own, self.from_core, self.from_y, self.from_x, self.from_near, self.from_far, self.full = buffers
-        self.send_at = lambda stage, k=0: send.at[index, STAGES.index(stage) + (8 if k else 0)]
-        self.receive_at = lambda stage, k=0: receive.at[index, STAGES.index(stage) + (8 if k else 0)]
-        self.local = lambda k: local.at[index, k]
-        half, quarter = rows // 2, rows // 4
-        self.my_columns = pl.ds(pl.multiple_of(place.x * (columns // 2), 128), columns // 2)
-        self.other_columns = pl.ds(
-            pl.multiple_of((1 - place.x) * (columns // 2), 128), columns // 2
-        )
-        self.my_half = pl.multiple_of(place.near * half, 16)
-        self.my_quarter = pl.multiple_of(place.near * half + place.far * quarter, 16)
-
-    def remote(self, stage, source, target, k=0):
-        return pltpu.make_async_remote_copy(
-            src_ref=source,
-            dst_ref=target,
-            send_sem=self.send_at(stage, k),
-            recv_sem=self.receive_at(stage, k),
-            device_id=self.place.partner[stage.split("_")[0]],
-            device_id_type=MESH,
-        )
-
-    def locals(self):
-        if self.own is None:
-            return []
-        return [
-            pltpu.make_async_copy(
-                self.source(2 * k + self.place.core), self.own.at[k], self.local(k)
-            )
-            for k in range(2)
-        ]
-
-    def copies(self, stage):
-        place, rows = self.place, self.rows
-        half, quarter = rows // 2, rows // 4
-        if stage == "core":
-            return [
-                self.remote(
-                    stage, self.source(2 * k + 1 - place.core), self.from_core.at[k], k
-                )
-                for k in range(2)
-            ]
-        if stage == "y":
-            return [self.remote(stage, self.from_core.at[1 - place.y], self.from_y)]
-        if stage == "x":
-            return [self.remote(stage, self.from_y.at[:, self.other_columns], self.from_x)]
-        if stage == "near":
-            other = pl.ds(pl.multiple_of((1 - place.near) * half, 16), half)
-            return [self.remote(stage, self.from_x.at[other, :], self.from_near)]
-        if stage == "far":
-            other = pl.ds(pl.multiple_of((1 - place.far) * quarter, 16), quarter)
-            return [self.remote(stage, self.from_near.at[other, :], self.from_far)]
-        if stage == "far_back":
-            mine = self.full.at[pl.ds(self.my_quarter, quarter), self.my_columns]
-            return [self.remote(stage, self.from_far, mine)]
-        if stage == "near_back":
-            mine = self.full.at[pl.ds(self.my_half, half), self.my_columns]
-            return [self.remote(stage, mine, mine)]
-        mine = self.full.at[:, self.my_columns]
-        return [self.remote(stage, mine, mine)]
-
-    def start(self, stage):
-        if stage == "core":
-            for copy in self.locals():
-                copy.start()
-        for copy in self.copies(stage):
-            copy.start()
-
-    def finish(self, stage):
-        place, rows = self.place, self.rows
-        half, quarter = rows // 2, rows // 4
-        for copy in self.copies(stage):
-            copy.wait_recv()
-        if stage == "core":
-            for copy in self.locals():
-                copy.wait()
-            for k in range(2):
-                kept = (
-                    self.source(2 * k + place.core) if self.own is None else self.own.at[k]
-                )
-                add_rows(
-                    lambda at: self.from_core.at[k, at, :], lambda at: kept.at[at, :], rows
-                )
-        elif stage == "y":
-            add_rows(
-                lambda at: self.from_y.at[at, :],
-                lambda at: self.from_core.at[place.y, at, :],
-                rows,
-            )
-        elif stage == "x":
-            add_rows(
-                lambda at: self.from_x.at[at, :],
-                lambda at: self.from_y.at[at, self.my_columns],
-                rows,
-            )
-        elif stage == "near":
-            add_rows(
-                lambda at: self.from_near.at[at, :],
-                lambda at: self.from_x.at[
-                    pl.ds(pl.multiple_of(at.start + self.my_half, 16), SUM_ROWS), :
-                ],
-                half,
-            )
-        elif stage == "far":
-            begin = place.far * quarter
-            add_rows(
-                lambda at: self.from_far.at[at, :],
-                lambda at: self.from_near.at[
-                    pl.ds(pl.multiple_of(at.start + begin, 16), SUM_ROWS), :
-                ],
-                quarter,
-            )
-
-    def place_piece(self):
-        def step(i, carry):
-            at = pl.ds(pl.multiple_of(i * SUM_ROWS, 16), SUM_ROWS)
-            to = pl.ds(pl.multiple_of(i * SUM_ROWS + self.my_quarter, 16), SUM_ROWS)
-            self.full[to, self.my_columns] = self.from_far[at, :]
-            return carry
-
-        lax.fori_loop(0, self.rows // 4 // SUM_ROWS, step, 0)
-
-    def step(self, stage):
-        at = STAGES.index(stage)
-        if at > 0:
-            self.finish(STAGES[at - 1])
-        if stage == "far_back":
-            self.place_piece()
-        self.start(stage)
-
-    def close(self, stages):
-        for stage in stages:
-            for copy in self.copies(stage):
-                copy.wait_send()
-
-
-DOWN, UP = STAGES[:5], STAGES[5:]
-WHOLE = 3
-
-
-def down_buffers(rows, columns, own):
-    buffer = lambda *shape: pltpu.VMEM(shape, BF16)
-    return [
-        *([buffer(2, rows, columns)] if own else []),
-        buffer(2, rows, columns),
-        buffer(rows, columns),
-        buffer(rows, columns // 2),
-        buffer(rows // 2, columns // 2),
-        buffer(rows // 4, columns // 2),
-    ]
-
-
-def grad_chunks():
-    quarter = MODEL_WIDTH // 4
-    half = MODEL_WIDTH // 2
-    early = [
-        (0, MODEL_WIDTH, 0, 0, half, MODEL_WIDTH),
-        (0, MODEL_WIDTH, half, 0, half, MODEL_WIDTH),
-        (1, quarter, 0, 0, quarter, FF // 2),
-        (1, quarter, 0, FF // 2, quarter, FF // 2),
-        (2, quarter, 0, 0, quarter, MODEL_WIDTH),
-    ]
-    late = [(j, quarter, 0, 0, quarter, MODEL_WIDTH) for j in (3, 4, 5)]
-    return early, late
-
-
-def chunk_source(grad, chunk):
-    _, owner_rows, row, column, rows, columns = chunk
-
-    def source(owner):
-        begin = pl.multiple_of(owner * owner_rows + row, 16)
-        return grad.at[pl.ds(begin, rows), pl.ds(column, columns)]
-
-    return source
-
-
-SEND_ORDER = (4, 3, 5, 2, 6, 1, 7, 0)
-
-
-def finish_kernel(
-    grad_query_ref,
-    grad_key_ref,
-    grad_value_ref,
-    tokens_ref,
-    pooled_ref,
-    grad_first_ref,
-    pool_ref,
-    weights_ref,
-    small_ref,
-    *refs,
-):
-    early, late = grad_chunks()
-    early = early[WHOLE:]
-    pieces, refs = refs[: len(early)], refs[len(early) :]
-    tokens_out, small_out, refs = refs[0], refs[1], refs[2:]
-    count = len(early) + len(late)
-    outs, refs = refs[:count], refs[count:]
-    fulls, refs = refs[:count], refs[count:]
-    buffers, refs = refs[: 5 * len(late)], refs[5 * len(late) :]
-    (
-        tokens_stage,
-        late_grads,
-        send,
-        receive,
-        token_send,
-        token_receive,
-        token_local,
-        small_core,
-        small_y,
-        small_all,
-        small_send,
-        small_receive,
-    ) = refs
-    place = Place()
-    place.greet()
-    first = []
-    for i, chunk in enumerate(early):
-        kept = [None, None, None, None, None, pieces[i], fulls[i]]
-        first.append(Chunk(place, i, None, *chunk[4:], kept, send, receive, None))
-    second = []
-    for j, chunk in enumerate(late):
-        i = len(early) + j
-        kept = [None, *buffers[5 * j : 5 * j + 5], fulls[i]]
-        source = chunk_source(late_grads.at[j], chunk)
-        second.append(Chunk(place, i, source, *chunk[4:], kept, send, receive, None))
-    for item in first:
-        item.place_piece()
-        item.start("far_back")
-
-    moved = []
-
-    def send_tokens(k):
-        to = (place.seq + k) % SG
-        block = LEN // SG
-        rows = pl.ds(pl.multiple_of(to * block, block), block)
-        pooled_rows = pl.ds(pl.multiple_of(to * (block // 2), block // 2), block // 2)
-        weight = lambda j: weights_ref[:, j * MODEL_WIDTH : (j + 1) * MODEL_WIDTH]
-        grad_pooled = grad_first_ref[pooled_rows, :] + mm(
-            grad_query_ref[pooled_rows, :], weight(0), NT
-        )
-        high, low = split(grad_pooled)
-        total = mm(grad_key_ref[rows, :], weight(1), NT)
-        total += mm(grad_value_ref[rows, :], weight(2), NT)
-        total += mm(pool_ref[to], high, TN) + mm(pool_ref[to], low, TN)
-        tokens_stage[to] = total.astype(BF16)
-        if k == 0:
-            copy = pltpu.make_async_copy(
-                tokens_stage.at[to], tokens_out.at[place.seq], token_local
-            )
-        else:
-            copy = pltpu.make_async_remote_copy(
-                src_ref=tokens_stage.at[to],
-                dst_ref=tokens_out.at[place.seq],
-                send_sem=token_send.at[k - 1],
-                recv_sem=token_receive.at[k - 1],
-                device_id=(to, place.dp),
-                device_id_type=MESH,
-            )
-        copy.start()
-        moved.append(copy)
-
-    for k in SEND_ORDER[:3]:
-        send_tokens(k)
-    for item in first:
-        item.step("near_back")
-    for k in SEND_ORDER[3:6]:
-        send_tokens(k)
-    for item in first:
-        item.step("x_back")
-    for k in SEND_ORDER[6:]:
-        send_tokens(k)
-
-    def small_copy(source, target, slot, device):
-        return pltpu.make_async_remote_copy(
-            src_ref=source,
-            dst_ref=target,
-            send_sem=small_send.at[slot],
-            recv_sem=small_receive.at[slot],
-            device_id=device,
-            device_id_type=MESH,
-        )
-
-    core_copies = [
-        small_copy(
-            small_ref.at[2 * k + 1 - place.core], small_core.at[k], k, place.partner["core"]
-        )
-        for k in range(2)
-    ]
-    for copy in core_copies:
-        copy.start()
-    operands = [
-        (pooled_ref, grad_query_ref),
-        (tokens_ref, grad_key_ref),
-        (tokens_ref, grad_value_ref),
-    ]
-    for j, (left, right) in enumerate(operands):
-        for r in range(0, MODEL_WIDTH, 256):
-            late_grads[j, r : r + 256, :] = mm(left[:, r : r + 256], right[...], TN).astype(BF16)
-        second[j].start("core")
-    for k, copy in enumerate(core_copies):
-        copy.wait_recv()
-        small_core[k] += small_ref[2 * k + place.core]
-    y_copy = small_copy(small_core.at[1 - place.y], small_y, 2, place.partner["y"])
-    y_copy.start()
-    for item in second:
-        item.step("y")
-    y_copy.wait_recv()
-    small_all[place.seq] = small_core[place.y] + small_y[...]
-    small_copies = []
-    for k, device in enumerate(place.peers()):
-        copy = small_copy(small_all.at[place.seq], small_all.at[place.seq], 3 + k, device)
-        copy.start()
-        small_copies.append(copy)
-    for stage in STAGES[2:]:
-        for item in second:
-            item.step(stage)
-
-    for item, out in zip(first, outs):
-        item.finish(STAGES[-1])
-        out[...] = item.full[...]
-        item.close(UP)
-    for copy in small_copies:
-        copy.wait_recv()
-    total = small_all[0]
-    for k in range(1, SG):
-        total = total + small_all[k]
-    small_out[...] = total
-    for item, out in zip(second, outs[len(first) :]):
-        item.finish(STAGES[-1])
-        out[...] = item.full[...]
-        item.close(STAGES)
-    for copy in [*core_copies, y_copy, *small_copies]:
-        copy.wait_send()
-    for copy in moved:
-        copy.wait()
-
-
-def finish(
-    grad_query, grad_key, grad_value, tokens, pooled, grad_first, pool, weights, small, pieces
-):
-    anywhere = pl.BlockSpec(memory_space=pl.ANY)
-    early, late = grad_chunks()
-    early = early[WHOLE:]
-    chunks = early + late
-    count = len(chunks)
-    small_shape = (SMALL_ROWS, SMALL_COLUMNS)
-    inside = pl.BlockSpec(memory_space=pltpu.VMEM)
-    out_tokens = (SG, LEN // SG, MODEL_WIDTH)
-    return pl.pallas_call(
-        finish_kernel,
-        in_specs=[inside] * (9 + len(early)),
-        out_specs=[anywhere, inside, *[inside] * count],
-        out_shape=[
-            jax.ShapeDtypeStruct(out_tokens, BF16),
-            jax.ShapeDtypeStruct(small_shape, F32),
-            *[jax.ShapeDtypeStruct(chunk[4:], BF16) for chunk in chunks],
-        ],
-        scratch_shapes=[
-            *[pltpu.VMEM(chunk[4:], BF16) for chunk in chunks],
-            *[buffer for chunk in late for buffer in down_buffers(*chunk[4:], False)],
-            pltpu.VMEM(out_tokens, BF16),
-            pltpu.VMEM((3, MODEL_WIDTH, MODEL_WIDTH), BF16),
-            pltpu.SemaphoreType.DMA((count, 16)),
-            pltpu.SemaphoreType.DMA((count, 16)),
-            pltpu.SemaphoreType.DMA((SG - 1,)),
-            pltpu.SemaphoreType.DMA((SG - 1,)),
-            pltpu.SemaphoreType.DMA,
-            pltpu.VMEM((2, *small_shape), F32),
-            pltpu.VMEM(small_shape, F32),
-            pltpu.VMEM((SG, *small_shape), F32),
-            pltpu.SemaphoreType.DMA((SG + 2,)),
-            pltpu.SemaphoreType.DMA((SG + 2,)),
-        ],
-        compiler_params=pltpu.CompilerParams(
-            collective_id=3, has_side_effects=True, vmem_limit_bytes=58 * 2**20
-        ),
-        name="finish",
-    )(
-        grad_query,
-        grad_key,
-        grad_value,
-        tokens,
-        pooled,
-        grad_first,
-        pool,
-        weights,
-        small,
-        *pieces,
-    )
-
-
-FF_STEP = 512
+    )(query, pairs, pairs, relative, vectors, query_side, key_side, phase, cosm, sinm, cotangent)
+
+
+FF_STEP = 768
 FF_TILES = FF // FF_STEP
 ROW_TILES = PQ // ROWS
 
@@ -1449,14 +1461,14 @@
     phase_ref,
     cos_ref,
     sin_ref,
+    mlp_sums_ref,
     grad_outer_ref,
     grad_inner_ref,
     grad_output_ref,
     grad_query_ref,
     grad_key_ref,
     grad_value_ref,
-    sums_ref,
-    grad_map_ref,
+    small_ref,
     *refs,
 ):
     early, _ = grad_chunks()
@@ -1568,19 +1580,31 @@
     grad_query_ref[...] = (content + shifted_grad + typed_grad).astype(BF16)
     query = query_ref[...]
     shifted_high, shifted_low = split(query + position_add)
-    grad_map_ref[0] = (
+    grad_map = (
         mm(shifted_high, turned_high, TN)
         + mm(shifted_low, turned_high, TN)
         + mm(shifted_high, turned_low, TN)
     )
     kinds = query + type_add
     row = lambda v: jnp.sum(v, axis=0, keepdims=True)
-    sums_ref[0, 0:1, :] = row(content)
-    sums_ref[0, 1:2, :] = row(shifted_grad)
-    sums_ref[0, 2:3, :] = row(typed_grad)
-    sums_ref[0, 3:4, :] = row(kinds * other)
-    sums_ref[0, 4:5, :] = row(kinds * same)
-    sums_ref[0, 5:6, :] = row(grad_value_ref[...].astype(F32))
+    below = mlp_sums_ref[...]
+    columns = jnp.concatenate(
+        [
+            jnp.zeros((HEAD_SIZE, LANES), F32),
+            row(grad_value_ref[...].astype(F32)),
+            row(content),
+            row(shifted_grad),
+            row(typed_grad),
+            row(kinds * other),
+            row(kinds * same),
+            jnp.zeros((2, LANES), F32),
+            below,
+            jnp.zeros((LANES - HEAD_SIZE - 24, LANES), F32),
+        ],
+        axis=0,
+    )
+    small_ref[:, :LANES] = (fold_maps(grad_map) + columns.T).astype(BF16)
+    small_ref[:, LANES:] = jnp.zeros((LANES, LANES), BF16)
 
     @pl.when(pair == PAIRS - 1)
     def _():
@@ -1600,6 +1624,7 @@
     phase,
     cosm,
     sinm,
+    mlp_sums,
     grads,
 ):
     early, _ = grad_chunks()
@@ -1626,22 +1651,21 @@
             whole((LEN, LANES)),
             whole((PQ, LANES)),
             whole((PQ, LANES)),
+            pl.BlockSpec((16, LANES), lambda i: (0, i)),
             *[anywhere] * 3,
         ],
         out_specs=[
             pl.BlockSpec((PQ, LANES), lambda i: (0, i)),
             pl.BlockSpec((LEN, LANES), lambda i: (0, i)),
             pl.BlockSpec((LEN, LANES), lambda i: (0, i)),
-            pl.BlockSpec((1, 8, LANES), lambda i: (i, 0, 0)),
-            pl.BlockSpec((1, LANES, 2 * LANES), lambda i: (i, 0, 0)),
+            pl.BlockSpec((LANES, 2 * LANES), lambda i: (i, 0)),
             *[whole(shape) for shape in shapes],
         ],
         out_shape=[
             jax.ShapeDtypeStruct((PQ, MODEL_WIDTH), BF16),
             jax.ShapeDtypeStruct((LEN, MODEL_WIDTH), BF16),
             jax.ShapeDtypeStruct((LEN, MODEL_WIDTH), BF16),
-            jax.ShapeDtypeStruct((PAIRS, 8, LANES), F32),
-            jax.ShapeDtypeStruct((PAIRS, LANES, 2 * LANES), F32),
+            jax.ShapeDtypeStruct((MODEL_WIDTH, 2 * LANES), BF16),
             *[jax.ShapeDtypeStruct(shape, BF16) for shape in shapes],
         ],
         scratch_shapes=[
@@ -1679,13 +1703,9 @@
         phase,
         cosm,
         sinm,
+        mlp_sums,
         *grads,
     )
-
-
-def swap_halves(value, axis):
-    first, second = jnp.split(value, 2, axis=axis)
-    return jnp.concatenate([second, first], axis=axis)
 
 
 def labels_kernel(labels_ref, out_ref, stage, send, receive):
@@ -1817,7 +1837,6 @@
     output_low = lax.all_gather(low(output_weight), "dp", axis=0, tiled=True)
     outer_low = lax.all_gather(low(outer_weight), "dp", axis=0, tiled=True)
 
-    kernel_size = HEAD_COUNT * HEAD_SIZE * HEAD_SIZE // owners
 
     segment_row = labels[:, 0:2].reshape(LEN)
     type_row = labels[:, 2:4].reshape(LEN)
@@ -1862,13 +1881,10 @@
     value_add = vectors[0:1]
     pair_add = jnp.concatenate([jnp.zeros_like(value_add), value_add], axis=1)
     pairs = low(mm(token_rows, first[:, MODEL_WIDTH:]) + pair_add)
-    mixture, join = attend_forward(
-        query, pairs, relative, vectors, query_side, key_side, phase, cosm, sinm
-    )
-
-    cotangent, _ = lax.optimization_barrier((cotangent, labels))
-    cotangent = lax.all_to_all(cotangent, "seq", split_axis=0, concat_axis=0, tiled=True)
-    upstream = cotangent.reshape(PQ, MODEL_WIDTH)
+    mixture, join, upstream = attend_forward(
+        query, pairs, relative, vectors, query_side, key_side, phase, cosm, sinm, cotangent
+    )
+    upstream = upstream.reshape(PQ, MODEL_WIDTH)
 
     (
         output,
@@ -1882,15 +1898,13 @@
     ) = mlp(
         mixture, pooled, upstream, output_low, inner_low, outer_low, vectors, inner_add
     )
-    (
-        grad_output_bias,
-        grad_outer_bias,
-        grad_gain_one,
-        grad_shift_one,
-        grad_gain_two,
-        grad_shift_two,
-    ) = [row_sums[j] for j in range(6)]
-    grad_query, grad_key, grad_value, sums, grad_map, *pieces = attend_backward(
+    inner_rows = grad_inner_bias.reshape(owners, owners, part).transpose(1, 0, 2)
+    mlp_sums = jnp.concatenate(
+        [row_sums, inner_rows.reshape(owners, MODEL_WIDTH), jnp.zeros((4, MODEL_WIDTH), F32)],
+        axis=0,
+    )
+
+    grad_query, grad_key, grad_value, small_grads, *pieces = attend_backward(
         join,
         pairs,
         query,
@@ -1903,43 +1917,10 @@
         phase,
         cosm,
         sinm,
+        mlp_sums,
         (grad_outer_weight, grad_inner_weight, grad_output_weight),
     )
-    crossed = grad_map.reshape(PAIRS, 2, HEAD_SIZE, 2, 2, HEAD_SIZE)
-    grad_relative = jnp.stack(
-        [
-            crossed[:, h, :, 0, 1 - h] + swap_halves(crossed[:, h, :, 1, 1 - h], 2)
-            for h in range(2)
-        ],
-        axis=1,
-    ).reshape(HEAD_COUNT, HEAD_SIZE, HEAD_SIZE)
-    grad_table = sums[:, 3:5].reshape(PAIRS, 2, 2, HEAD_SIZE).transpose(0, 2, 1, 3)
-    sum_row = lambda j: sums[:, j].reshape(owners, -1)
-    small_grads = jnp.concatenate(
-        [
-            value.reshape(owners, -1)
-            for value in (
-                sum_row(5),
-                grad_output_bias,
-                grad_outer_bias,
-                grad_gain_one,
-                grad_shift_one,
-                grad_gain_two,
-                grad_shift_two,
-                sum_row(0),
-                sum_row(1),
-                sum_row(2),
-                grad_inner_bias,
-                grad_relative,
-                grad_table,
-            )
-        ],
-        axis=1,
-    )
-    count = small_grads.shape[1]
-    room = SMALL_ROWS * SMALL_COLUMNS
-    small_grads = jnp.pad(small_grads, ((0, 0), (0, room - count)))
-    grad_tokens, small_owned, *owned = finish(
+    grad_tokens, *owned = finish(
         grad_query,
         grad_key,
         grad_value,
@@ -1948,20 +1929,16 @@
         grad_first,
         pool,
         first,
-        small_grads.reshape(owners, SMALL_ROWS, SMALL_COLUMNS),
+        small_grads,
         pieces[WHOLE:],
     )
     owned = [*pieces[:WHOLE], *owned]
     owned_outer = jnp.concatenate(owned[0:2], axis=0).astype(F32)
     owned_inner = jnp.concatenate(owned[2:4], axis=1).astype(F32)
-    owned_output, *squares = [value.astype(F32) for value in owned[4:]]
+    owned_output, small_owned, *squares = [value.astype(F32) for value in owned[4:]]
     squares.append(owned_output)
-    small_owned = small_owned.reshape(-1)
-    place = 0
-    pieces = []
-    for size in [part] * 10 + [FF // owners, kernel_size, HEAD_COUNT * 2 * HEAD_SIZE // owners]:
-        pieces.append(small_owned[place : place + size])
-        place += size
+    columns = small_owned[:, HEAD_SIZE : HEAD_SIZE + 24].T
+    vector = lambda j: columns[j]
     heads = HEAD_COUNT // owners
     return (
         output,
@@ -1972,19 +1949,19 @@
         squares[3],
         owned_inner,
         owned_outer,
-        pieces[0],
-        pieces[1],
-        pieces[10],
-        pieces[2],
-        pieces[3],
-        pieces[4],
-        pieces[5],
-        pieces[6],
-        pieces[7].reshape(heads, HEAD_SIZE),
-        pieces[8].reshape(heads, HEAD_SIZE),
-        pieces[9].reshape(heads, HEAD_SIZE),
-        pieces[11].reshape(heads, HEAD_SIZE, HEAD_SIZE),
-        pieces[12].reshape(heads, 2, HEAD_SIZE),
+        vector(0),
+        vector(8),
+        columns[16:20].reshape(FF // owners),
+        vector(9),
+        vector(10),
+        vector(11),
+        vector(12),
+        vector(13),
+        vector(1).reshape(heads, HEAD_SIZE),
+        vector(2).reshape(heads, HEAD_SIZE),
+        vector(3).reshape(heads, HEAD_SIZE),
+        small_owned[:, :HEAD_SIZE].reshape(heads, HEAD_SIZE, HEAD_SIZE),
+        columns[4:6].reshape(2, heads, HEAD_SIZE).transpose(1, 0, 2),
     )
 
 

time: 500 us -> 479 us (0.958)
  Pallas kernels: 348 us -> 340 us
  local copies, waits for them, and re-layouts: 23.8 us -> 17.4 us
    pallas_call x1, Pallas kernels: 64.5 us -> 56.8 us  [mlp(): pl.pallas_call(mlp_kernel, grid=(ROW_TILES + FF_TILES,), in_specs=[fixed(...]
    pallas_call x1, Pallas kernels: 120 us -> 115 us  [finish(): pl.pallas_call(finish_kernel, in_specs=[inside] * (9 + len(early)), out_s...]
  transfers between devices with their start and end apart: 6 -> 5, of which waited for: 1 -> 1; matrix products, arithmetic and copies ran while one was open for 7% -> 7% of each run, Pallas kernels for 11% -> 13%
where the time goes in v4:
time: 479 us; the launch traced here: 475 us
  Pallas kernels  340 us (71%)
  waiting for transfers between devices  35.8 us (7%)
  other arithmetic  33.8 us (7%)
  local copies, waits for them, and re-layouts  17.4 us (4%)
  blocking collectives  15.9 us (3%)
  between operations  14.7 us (3%)
  matrix products  12.6 us (3%)
  starting transfers between devices  4.83 us (1%)
    pallas_call x1, Pallas kernels, finish(): pl.pallas_call(finish_kernel, in_specs=[inside] * (9 + len(early)), out_s...  115 us
    pallas_call x1, Pallas kernels, attend_backward(): pl.pallas_call(attend_back_kernel, grid=(PAIRS,), in_specs=[pl.BlockSpec(...  108 us
    pallas_call x1, Pallas kernels, mlp(): pl.pallas_call(mlp_kernel, grid=(ROW_TILES + FF_TILES,), in_specs=[fixed(...  56.8 us
    pallas_call x1, Pallas kernels, attend_forward(): pl.pallas_call(attend_kernel, grid=(PAIRS,), in_specs=[pl.BlockSpec((PQ,...  49.6 us
    all_to_all x1, waiting for transfers between devices, sequence_body(): lax.all_to_all(tokens, 'seq', split_axis=0, concat_axis=0, tiled=True)  35.7 us
    dot_general x2, matrix products, mm(): return lax.dot_general(left, right, dims, preferred_element_type=F32)  11.9 us
    pallas_call x1, Pallas kernels, move_labels(): pl.pallas_call(labels_kernel, in_specs=[inside], out_specs=inside, out_sh...  10.6 us
    convert_element_type x19, other arithmetic, sequence_body(): low = lambda value: value.astype(BF16)  9.59 us
  transfers between devices with their start and end apart: 5, of which 1 were waited for; matrix products, arithmetic and copies ran while one was open for 7% of the time, Pallas kernels for 13%

profile of v4, /device:TPU:0, one launch (start us, length us, event | category | flops | bytes accessed | tf_op | source)
XLA Modules:
  0.0 474.7 jit_solution(7053422435116116676)
XLA Ops:
  7.2 1.1 convert_element_type.124
  8.3 1.2 convert_element_type.125
  9.5 1.2 convert_element_type.126
  10.8 1.0 pad_maximum_fusion
  11.8 0.7 convert_element_type.145
  12.7 1.2 convert_element_type.146
  13.9 0.2 slice.108
  14.1 0.2 slice.110
  14.3 0.2 slice.109
  14.5 0.7 stack.35.labels_ref
  15.2 10.6 %labels.1 = s32[8,7,128]{2,1,0:T(8,128)} custom-call(s32[8,7,128]{2,1,0:T(8,128)} %stack.35.labels_ref), custom_call_target="tpu_custom_call" | custom-call | tf_op jit(solution)/shard_map/labels/pallas_call | solution.py:1735
  25.8 4.7 all-to-all-start
  30.7 2.8 convert_element_type.147
  33.6 0.5 slice.145
  34.3 0.1 reshape.297
  34.8 5.3 %all-gather.1 = bf16[4,192,16]{1,2,0:T(8,128)(2,1)S(1)} all-gather(bf16[1,192,16]{1,2,0:T(8,128)(2,1)S(1)} %bitcast.66), channel_id=1, replica_groups=mesh['seq'=8,'dp'=4] {'dp'}, dimensions={0}, use_global_device_ids=true | all-gather | bytes 30720 | tf_op jit(solution)/shard_map/all_gather | solution.py:1828
  40.2 0.1 reshape.322
  40.3 0.1 copy.64
  40.4 5.2 %all-gather.3 = bf16[4,1,768]{2,1,0:T(2,128)(2,1)S(1)} all-gather(bf16[1,1,768]{2,1,0:T(2,128)(2,1)S(1)} %reshape.317), channel_id=2, replica_groups=mesh['seq'=8,'dp'=4] {'dp'}, dimensions={0}, use_global_device_ids=true | all-gather | bytes 7680 | tf_op jit(solution)/shard_map/all_gather | solution.py:1830
  45.6 5.4 %all-gather.2 = bf16[4,192,64]{1,2,0:T(8,128)(2,1)S(1)} all-gather(bf16[1,192,64]{1,2,0:T(8,128)(2,1)S(1)} %copy.64), channel_id=1, replica_groups=mesh['seq'=8,'dp'=4] {'dp'}, dimensions={0}, use_global_device_ids=true | all-gather | bytes 122880 | tf_op jit(solution)/shard_map/all_gather | solution.py:1833
  51.0 0.8 copy.65
  51.9 0.6 convert.6.inner_add_ref
  52.6 1.3 fusion.9
  53.9 0.6 fusion.10
  54.5 2.6 select_add_fusion
  57.1 2.6 compare_select_fusion.4
  59.7 0.1 iota_compare_fusion.4
  59.8 1.1 convert_select_fusion.query_side_ref
  60.9 1.1 select_convert_fusion.pool_ref
  62.1 2.3 fusion.5.key_side_ref
  64.4 35.7 %all-to-all-done = bf16[8,256,768]{2,1,0:T(8,128)(2,1)S(1)} async-done(((bf16[8,256,768]{2,1,0:T(8,128)(2,1)}), bf16[8,256,768]{2,1,0:T(8,128)(2,1)S(1)}, u32[]{:S(2)}, u32[]{:S(2)}) %all-to-all-start) | async-done | bytes 3145760 | tf_op jit(solution)/shard_map/all_to_all | solution.py:1808
  100.0 0.7 fusion.8
  100.7 2.0 copy-done.1
  102.7 1.3 bitcast_convert_fusion.pooled_ref
  104.0 4.9 %fusion.1.query_ref = f32[1024,768]{1,0:T(8,128)} fusion(bf16[1024,768]{1,0:T(8,128)(2,1)} %bitcast_convert_fusion.pooled_ref, bf16[768,2304]{1,0:T(8,128)(2,1)} %all-gather.9.cloned.1.call-done.weights_ref), kind=kOutput, calls=%fused_computation.2 | convolution fusion | flops 1207959552 | bytes 5898240 | tf_op jit(solution)/shard_map/dot_general | solution.py:566
  109.0 7.0 %add_convert_fusion.key_ref.value_ref = bf16[2048,1536]{1,0:T(8,128)(2,1)} fusion(bf16[2048,768]{1,0:T(8,128)(2,1)S(1)} %bitcast.43, f32[1536]{0:T(1024)S(1)} %pad_reduce_fusion, bf16[768,2304]{1,0:T(8,128)(2,1)S(1)} %copy-done.2), kind=kOutput, calls=%fused_computation | convolution fusion | flops 4838129664 | bytes 11804672 | tf_op jit(solution)/shard_map/dot_general | solution.py:566
  115.9 49.6 %attend_forward.1 = (bf16[1024,768]{1,0:T(8,128)(2,1)}, bf16[12,1024,256]{2,1,0:T(8,128)(2,1)}, bf16[8,128,768]{2,1,0:T(8,128)(2,1)}) custom-call(f32[1024,768]{1,0:T(8,128)} %fusion.1.query_ref, bf16[2048,1536]{1,0:T(8,128)(2,1)} %add_convert_fusion.key_ref.value_ref, bf16[2048,1536]{1,0:T(8,128)(2,1)} %add_convert_fusion.key_ref.value_ref, ...), custom_call_target="tpu_custom_call" | custom-call | flops 25769803776 | bytes 20000000 | tf_op jit(solution)/shard_map/attend_forward/pallas_call | solution.py:1120
  165.6 56.8 %mlp.1 = (bf16[8,128,768]{2,1,0:T(8,128)(2,1)}, bf16[1024,768]{1,0:T(8,128)(2,1)}, f32[1024,768]{1,0:T(8,128)}, bf16[3072,768]{1,0:T(8,128)(2,1)}, bf16[768,3072...) custom-call(bf16[1024,768]{1,0:T(8,128)(2,1)} %get-tuple-element.52.mixture_ref, ...), custom_call_target="tpu_custom_call" | custom-call | flops 32614907904 | bytes 40000000 | tf_op jit(solution)/shard_map/mlp/pallas_call | solution.py:1376
  222.4 0.5 broadcast.218
  222.9 1.4 reduce.30
  224.4 0.1 reshape.306
  224.5 1.4 maximum_maximum_fusion.mlp_sums_ref
  225.9 108.2 %attend_backward.1 = (bf16[1024,768]{1,0:T(8,128)(2,1)}, bf16[2048,768]{1,0:T(8,128)(2,1)}, bf16[2048,768]{1,0:T(8,128)(2,1)}, bf16[768,256]{1,0:T(8,128)(2,1)},...) custom-call(bf16[12,1024,256]{2,1,0:T(8,128)(2,1)} %get-tuple-elemen, ...), custom_call_target="tpu_custom_call" | custom-call | flops 64424509440 | bytes 32000000 | tf_op jit(solution)/shard_map/attend_backward/pallas_call | solution.py:1637
  334.1 114.6 %finish.1 = (bf16[8,256,768]{2,1,0:T(8,128)(2,1)}, bf16[192,1536]{1,0:T(8,128)(2,1)}, bf16[192,768]{1,0:T(8,128)(2,1)}, bf16[192,256]{1,0:T(8,128)(2,1)}, bf16[1...) custom-call(bf16[1024,768]{1,0:T(8,128)(2,1)} %get-tuple-element.62.grad_query_ref, ...), custom_call_target="tpu_custom_call" | custom-call | tf_op jit(solution)/shard_map/finish/pallas_call | solution.py:967
  448.7 1.0 convert_element_type.156
  449.8 0.1 slice.149
  449.9 0.1 slice.159
  450.0 1.3 slice_reduce_fusion
  451.3 1.4 slice.158
  452.7 1.8 convert_element_type.150
  454.5 0.9 convert_element_type.151
  455.4 0.9 convert_element_type.152
  456.3 0.9 convert_element_type.153
  457.2 0.7 reshape.307
  457.9 0.7 copy.68
  458.5 0.7 reshape_squeeze.11
  459.2 0.7 reshape_squeeze.12
  459.9 0.7 reshape_squeeze.13
  460.5 1.6 maximum_convert_fusion.1
  462.1 1.7 maximum_convert_fusion
  463.8 0.2 copy-done.5
  464.0 1.1 copy.73
  465.1 1.2 copy-done.3
  466.3 1.7 copy.74
  (117 shorter events, 1.4 us)
Async XLA Ops:
  7.2 96.8 %all-gather.9.cloned.1.call-start = ((), (), s32[]{:S(2)}) async-start(), calls=%async_computation.1 | async-start | bytes 4423680 | tf_op jit(solution)/shard_map/all_gather | solution.py:1835
  8.3 3.5 copy-start.10
  9.5 3.2 copy-start.4
  11.8 153.8 %all-gather.11.cloned.1.call-start = ((), (), s32[]{:S(2)}) async-start(), calls=%async_computation.2 | async-start | bytes 1474560 | tf_op jit(solution)/shard_map/all_gather | solution.py:1837
  12.6 1.3 copy-start.17
  12.6 1.7 copy-start.18
  12.6 153.0 %all-gather.13.cloned.1.call-start = ((), (), s32[]{:S(2)}) async-start(), calls=%async_computation.3 | async-start | bytes 5898240 | tf_op jit(solution)/shard_map/all_gather | solution.py:1836
  25.8 74.2 %all-to-all-start = ((bf16[8,256,768]{2,1,0:T(8,128)(2,1)}), bf16[8,256,768]{2,1,0:T(8,128)(2,1)S(1)}, u32[]{:S(2)}, u32[]{:S(2)}) async-start(bf16[8,256,768]{2,1,0:T(8,128)(2,1)} %param.26), calls=%async_computation | async-start | bytes 6291456 | tf_op jit(solution)/shard_map/all_to_all | solution.py:1808
  30.5 3.1 copy-start.14
  30.5 3.6 copy-start.20
  30.5 3.8 copy-start.21
  30.5 3.9 copy-start.22
  30.5 4.0 copy-start.23
  30.5 4.0 copy-start.24
  30.5 4.0 copy-start.25
  30.5 4.1 copy-start.26
  30.6 4.1 copy-start.27
  30.6 4.1 copy-start.28
  30.6 4.1 copy-start.29
  30.6 4.1 copy-start.30
  30.6 9.7 %copy-start.15 = (f32[3,64,64]{2,1,0:T(8,128)S(1)}, f32[3,64,64]{2,1,0:T(8,128)}, u32[]{:S(2)}) copy-start(f32[3,64,64]{2,1,0:T(8,128)} %param.47) | copy-start | bytes 147460
  30.6 9.8 %copy-start.19 = (f32[768]{0:T(1024)S(1)}, f32[768]{0:T(1024)}, u32[]{:S(2)}) copy-start(f32[768]{0:T(1024)} %param.38) | copy-start | bytes 9220
  30.6 135.0 %all-gather.15.cloned.1.call-start = ((), (), s32[]{:S(2)}) async-start(), calls=%async_computation.4 | async-start | bytes 5898240 | tf_op jit(solution)/shard_map/all_gather | solution.py:1838
  40.3 60.4 %copy-start.16 = (f32[768,16]{0,1:T(8,128)}, f32[768,16]{0,1:T(8,128)S(1)}, u32[]{:S(2)}) copy-start(f32[768,16]{0,1:T(8,128)S(1)} %reshape.322) | copy-start | bytes 147460
  100.0 8.9 %copy-start = (bf16[8,256,768]{2,1,0:T(8,128)(2,1)}, bf16[8,256,768]{2,1,0:T(8,128)(2,1)S(1)}, u32[]{:S(2)}) copy-start(bf16[8,256,768]{2,1,0:T(8,128)(2,1)S(1)} %all-to-all-done) | copy-start | bytes 9437188
  100.7 2.0 copy-start.1
  104.0 5.0 %copy-start.2 = (bf16[768,2304]{1,0:T(8,128)(2,1)S(1)}, bf16[768,2304]{1,0:T(8,128)(2,1)}, u32[]{:S(2)}) copy-start(bf16[768,2304]{1,0:T(8,128)(2,1)} %all-gather.9.cloned.1.call-done.weights_ref) | copy-start | bytes 10616836
  448.7 5.8 %copy-start.13 = (bf16[192,768]{1,0:T(8,128)(2,1)S(1)}, bf16[192,768]{1,0:T(8,128)(2,1)}, u32[]{:S(2)}) copy-start(bf16[192,768]{1,0:T(8,128)(2,1)} %get-tuple-element.71) | copy-start | bytes 884740
  448.7 6.7 %copy-start.12 = (bf16[192,768]{1,0:T(8,128)(2,1)S(1)}, bf16[192,768]{1,0:T(8,128)(2,1)}, u32[]{:S(2)}) copy-start(bf16[192,768]{1,0:T(8,128)(2,1)} %get-tuple-element.72) | copy-start | bytes 884740
  448.7 7.5 %copy-start.11 = (bf16[192,768]{1,0:T(8,128)(2,1)S(1)}, bf16[192,768]{1,0:T(8,128)(2,1)}, u32[]{:S(2)}) copy-start(bf16[192,768]{1,0:T(8,128)(2,1)} %get-tuple-element.73) | copy-start | bytes 884740
  450.0 10.5 %copy-start.7 = (bf16[384,768]{1,0:T(8,128)(2,1)S(1)}, bf16[384,768]{1,0:T(8,128)(2,1)}, u32[]{:S(2)}) copy-start(bf16[384,768]{1,0:T(8,128)(2,1)} %get-tuple-element.76) | copy-start | bytes 1769476
  450.0 10.5 %copy-start.8 = (bf16[384,768]{1,0:T(8,128)(2,1)S(1)}, bf16[384,768]{1,0:T(8,128)(2,1)}, u32[]{:S(2)}) copy-start(bf16[384,768]{1,0:T(8,128)(2,1)} %get-tuple-element.77) | copy-start | bytes 1769476
  456.3 5.8 %copy-start.6 = (bf16[192,1536]{1,0:T(8,128)(2,1)S(1)}, bf16[192,1536]{1,0:T(8,128)(2,1)}, u32[]{:S(2)}) copy-start(bf16[192,1536]{1,0:T(8,128)(2,1)} %get-tuple-element.74) | copy-start | bytes 1769476
  456.3 5.8 %copy-start.9 = (bf16[192,1536]{1,0:T(8,128)(2,1)S(1)}, bf16[192,1536]{1,0:T(8,128)(2,1)}, u32[]{:S(2)}) copy-start(bf16[192,1536]{1,0:T(8,128)(2,1)} %get-tuple-element.75) | copy-start | bytes 1769476
  462.1 1.9 copy-start.5
  463.8 2.5 copy-start.3
Sparse Core Ops, SparseCore 0:
  11.9 33.6 all-gather.8
  47.7 17.4 all-gather.10
  67.3 37.4 all-gather.12
  106.8 37.4 all-gather.14

commit v5 on v4

--- a/solution.py
+++ b/solution.py
@@ -1708,8 +1708,33 @@
     )
 
 
-def labels_kernel(labels_ref, out_ref, stage, send, receive):
+def labels_kernel(
+    labels_ref,
+    query_ref,
+    key_ref,
+    value_ref,
+    output_ref,
+    inner_ref,
+    outer_ref,
+    out_ref,
+    first_low,
+    output_low,
+    inner_low,
+    outer_low,
+    stage,
+    send,
+    receive,
+    local,
+    *full,
+):
     place = Place()
+    refs = (query_ref, key_ref, value_ref, output_ref, inner_ref, outer_ref)
+    loads = [
+        pltpu.make_async_copy(ref, buffer, local.at[j])
+        for j, (ref, buffer) in enumerate(zip(refs, full))
+    ]
+    for load in loads:
+        load.start()
     place.greet()
     copies = []
     for k in range(1, SG):
@@ -1725,26 +1750,41 @@
         copy.start()
         copies.append(copy)
     stage[place.seq] = labels_ref[place.seq]
+    for j, load in enumerate(loads):
+        load.wait()
+        if j < 3:
+            first_low[:, j * MODEL_WIDTH : (j + 1) * MODEL_WIDTH] = full[j][...].astype(BF16)
+        else:
+            (output_low, inner_low, outer_low)[j - 3][...] = full[j][...].astype(BF16)
     for copy in copies:
         copy.wait()
     out_ref[...] = stage[...]
 
 
-def move_labels(labels):
+def move_labels(labels, weights):
     inside = pl.BlockSpec(memory_space=pltpu.VMEM)
+    part = weights[0].shape[0]
+    shapes = [(part, 3 * MODEL_WIDTH), *[weight.shape for weight in weights[3:]]]
     return pl.pallas_call(
         labels_kernel,
-        in_specs=[inside],
-        out_specs=inside,
-        out_shape=jax.ShapeDtypeStruct(labels.shape, jnp.int32),
+        in_specs=[inside, *[pl.BlockSpec(memory_space=pl.ANY)] * 6],
+        out_specs=[inside] * 5,
+        out_shape=[
+            jax.ShapeDtypeStruct(labels.shape, jnp.int32),
+            *[jax.ShapeDtypeStruct(shape, BF16) for shape in shapes],
+        ],
         scratch_shapes=[
             pltpu.VMEM(labels.shape, jnp.int32),
             pltpu.SemaphoreType.DMA((SG - 1,)),
             pltpu.SemaphoreType.DMA((SG - 1,)),
+            pltpu.SemaphoreType.DMA((len(weights),)),
+            *[pltpu.VMEM(weight.shape, F32) for weight in weights],
         ],
-        compiler_params=pltpu.CompilerParams(collective_id=4, has_side_effects=True),
+        compiler_params=pltpu.CompilerParams(
+            collective_id=4, has_side_effects=True, vmem_limit_bytes=58 * 2**20
+        ),
         name="labels",
-    )(labels)
+    )(labels, *weights)
 
 
 def angle_tables():
@@ -1790,20 +1830,15 @@
     owners = lax.axis_size("dp")
     part = MODEL_WIDTH // owners
     low = lambda value: value.astype(BF16)
-    even_segments, odd_segments = segments[:, 0::2], segments[:, 1::2]
+    half = segments.shape[1] // 2
     labels = jnp.stack(
-        [
-            segments[:, :128],
-            segments[:, 128:],
-            token_types[:, :128],
-            token_types[:, 128:],
-            even_segments,
-            token_types[:, 0::2],
-            (even_segments == odd_segments).astype(jnp.int32),
-        ],
+        [segments[:, :half], segments[:, half:], token_types[:, :half], token_types[:, half:]],
         axis=1,
     )
-    labels = move_labels(labels)
+    labels, first, output_low, inner_low, outer_low = move_labels(
+        labels,
+        (query_weight, key_weight, value_weight, output_weight, inner_weight, outer_weight),
+    )
     tokens, labels = lax.optimization_barrier((tokens, labels))
     rows = lax.all_to_all(tokens, "seq", split_axis=0, concat_axis=0, tiled=True)
     flat = lambda value: low(value).reshape(1, part)
@@ -1831,18 +1866,18 @@
     inner_add = inner_add.astype(F32)
     relative = low(relative_kernel).reshape(part, HEAD_SIZE)
     relative = lax.all_gather(relative, "dp", axis=0, tiled=True)
-    first = jnp.concatenate([low(query_weight), low(key_weight), low(value_weight)], axis=1)
     first = lax.all_gather(first, "dp", axis=0, tiled=True)
-    inner_low = lax.all_gather(low(inner_weight), "dp", axis=0, tiled=True)
-    output_low = lax.all_gather(low(output_weight), "dp", axis=0, tiled=True)
-    outer_low = lax.all_gather(low(outer_weight), "dp", axis=0, tiled=True)
+    inner_low = lax.all_gather(inner_low, "dp", axis=0, tiled=True)
+    output_low = lax.all_gather(output_low, "dp", axis=0, tiled=True)
+    outer_low = lax.all_gather(outer_low, "dp", axis=0, tiled=True)
 
 
     segment_row = labels[:, 0:2].reshape(LEN)
     type_row = labels[:, 2:4].reshape(LEN)
-    query_segments = labels[:, 4].reshape(PQ)
-    query_types = labels[:, 5].reshape(PQ)
-    pair_same = labels[:, 6] > 0
+    segment_pairs = segment_row.reshape(PQ, 2)
+    query_segments = segment_pairs[:, 0]
+    query_types = type_row.reshape(PQ, 2)[:, 0]
+    pair_same = (segment_pairs[:, 0] == segment_pairs[:, 1]).reshape(SG, PQ // SG)
 
     first_doc, last_doc = segment_row[0], segment_row[LEN - 1]
     first_type = type_row[0]

time: 479 us -> 476 us (level)
  other arithmetic: 33.8 us -> 28.3 us
    convert_element_type x19 -> x13, other arithmetic: 9.59 us -> 1.34 us  [sequence_body(): low = lambda value: value.astype(BF16)]
  transfers between devices with their start and end apart: 5 -> 5, of which waited for: 1 -> 1; matrix products, arithmetic and copies ran while one was open for 7% -> 7% of each run, Pallas kernels for 13% -> 10%
where the time goes in v5:
time: 476 us; the launch traced here: 471 us
  Pallas kernels  341 us (72%)
  waiting for transfers between devices  33.6 us (7%)
  other arithmetic  28.3 us (6%)
  local copies, waits for them, and re-layouts  20.1 us (4%)
  blocking collectives  16.8 us (4%)
  between operations  14.6 us (3%)
  matrix products  12.6 us (3%)
  starting transfers between devices  4.87 us (1%)
    pallas_call x1, Pallas kernels, finish(): pl.pallas_call(finish_kernel, in_specs=[inside] * (9 + len(early)), out_s...  115 us
    pallas_call x1, Pallas kernels, attend_backward(): pl.pallas_call(attend_back_kernel, grid=(PAIRS,), in_specs=[pl.BlockSpec(...  108 us
    pallas_call x1, Pallas kernels, mlp(): pl.pallas_call(mlp_kernel, grid=(ROW_TILES + FF_TILES,), in_specs=[fixed(...  57.2 us
    pallas_call x1, Pallas kernels, attend_forward(): pl.pallas_call(attend_kernel, grid=(PAIRS,), in_specs=[pl.BlockSpec((PQ,...  48.8 us
    all_to_all x1, waiting for transfers between devices, sequence_body(): lax.all_to_all(tokens, 'seq', split_axis=0, concat_axis=0, tiled=True)  31.6 us
    dot_general x2, matrix products, mm(): return lax.dot_general(left, right, dims, preferred_element_type=F32)  11.9 us
    pallas_call x1, Pallas kernels, move_labels(): pl.pallas_call(labels_kernel, in_specs=[inside, *[pl.BlockSpec(memory_spa...  11.7 us
  transfers between devices with their start and end apart: 5, of which 1 were waited for; matrix products, arithmetic and copies ran while one was open for 7% of the time, Pallas kernels for 10%

profile of v5, /device:TPU:0, one launch (start us, length us, event | category | flops | bytes accessed | tf_op | source)
XLA Modules:
  0.0 471.5 jit_solution(16926937840546202971)
XLA Ops:
  7.2 0.7 fusion.9
  7.9 0.7 fusion.10
  8.6 0.6 pad_add_fusion.labels_ref
  9.3 11.7 %labels.1 = (s32[8,4,128]{2,1,0:T(4,128)}, bf16[192,2304]{1,0:T(8,128)(2,1)}, bf16[192,768]{1,0:T(8,128)(2,1)}, bf16[192,3072]{1,0:T(8,128)(2,1)}, bf16[768,768]{1,0:T(8,128)(2,1)}) custom-call(s32[8,4,128]{2,1,0:T(4,128)} %pad_add_fusion.labels_ref, f32[192,768]{1,0:T(8,128)} %query_ref.1, f32[192,768]{1,0:T(8,128)} %key_ref.1, f32[192,768]{1,0:T(8,128)} %value_ref.1, ...), custom_call_target="tpu_custom_call" | custom-call | tf_op jit(solution)/shard_map/labels/pallas_call | solution.py:1768
  21.1 0.7 all-gather.11.cloned.1.call-update
  21.8 0.7 all-gather.13.cloned.1.call-update
  22.7 4.7 %all-to-all-start = ((bf16[8,256,768]{2,1,0:T(8,128)(2,1)}), bf16[8,256,768]{2,1,0:T(8,128)(2,1)S(1)}, u32[]{:S(2)}, u32[]{:S(2)}) async-start(bf16[8,256,768]{2,1,0:T(8,128)(2,1)} %param.26), calls=%async_computation | async-start | bytes 6291456 | tf_op jit(solution)/shard_map/all_to_all | solution.py:1843
  27.5 0.5 all-gather.15.cloned.1.call-update
  28.0 0.5 slice.137
  28.5 1.3 fusion.6
  29.8 1.3 reshape_reshape.7
  31.1 1.3 reshape_reshape.6
  32.6 0.1 reshape.263
  32.7 0.1 reshape.264
  32.8 0.1 reshape.265
  33.1 5.3 %all-gather.1 = bf16[4,192,16]{1,2,0:T(8,128)(2,1)S(1)} all-gather(bf16[1,192,16]{1,2,0:T(8,128)(2,1)S(1)} %bitcast.54), channel_id=1, replica_groups=mesh['seq'=8,'dp'=4] {'dp'}, dimensions={0}, use_global_device_ids=true | all-gather | bytes 30720 | tf_op jit(solution)/shard_map/all_gather | solution.py:1863
  38.5 0.1 reshape.287
  38.6 0.1 copy.60
  38.7 6.2 %all-gather.2 = bf16[4,192,64]{1,2,0:T(8,128)(2,1)S(1)} all-gather(bf16[1,192,64]{1,2,0:T(8,128)(2,1)S(1)} %copy.60), channel_id=1, replica_groups=mesh['seq'=8,'dp'=4] {'dp'}, dimensions={0}, use_global_device_ids=true | all-gather | bytes 122880 | tf_op jit(solution)/shard_map/all_gather | solution.py:1868
  44.9 0.8 copy.61
  45.8 5.2 %all-gather.3 = bf16[4,1,768]{2,1,0:T(2,128)(2,1)S(1)} all-gather(bf16[1,1,768]{2,1,0:T(2,128)(2,1)S(1)} %reshape.282), channel_id=2, replica_groups=mesh['seq'=8,'dp'=4] {'dp'}, dimensions={0}, use_global_device_ids=true | all-gather | bytes 7680 | tf_op jit(solution)/shard_map/all_gather | solution.py:1865
  51.0 0.6 convert.5.inner_add_ref
  51.7 0.6 fusion.8
  52.3 1.6 select_reduce_fusion.2
  53.9 4.1 add_reduce_fusion
  58.0 2.6 select_add_fusion
  60.6 0.1 iota_compare_fusion.4
  60.8 1.1 convert_select_fusion.query_side_ref
  61.9 1.1 select_convert_fusion.pool_ref
  63.0 2.3 fusion.5.key_side_ref
  65.3 31.6 %all-to-all-done = bf16[8,256,768]{2,1,0:T(8,128)(2,1)S(1)} async-done(((bf16[8,256,768]{2,1,0:T(8,128)(2,1)}), bf16[8,256,768]{2,1,0:T(8,128)(2,1)S(1)}, u32[]{:S(2)}, u32[]{:S(2)}) %all-to-all-start) | async-done | bytes 3145760 | tf_op jit(solution)/shard_map/all_to_all | solution.py:1843
  96.9 0.6 fusion.7
  97.6 2.0 copy-done.1
  99.6 1.3 bitcast_convert_fusion.pooled_ref
  100.9 4.9 %fusion.1.query_ref = f32[1024,768]{1,0:T(8,128)} fusion(bf16[1024,768]{1,0:T(8,128)(2,1)} %bitcast_convert_fusion.pooled_ref, bf16[768,2304]{1,0:T(8,128)(2,1)} %all-gather.9.cloned.1.call-done.weights_ref), kind=kOutput, calls=%fused_computation.2 | convolution fusion | flops 1207959552 | bytes 5898240 | tf_op jit(solution)/shard_map/dot_general | solution.py:566
  105.8 7.0 %add_convert_fusion.key_ref.value_ref = bf16[2048,1536]{1,0:T(8,128)(2,1)} fusion(bf16[2048,768]{1,0:T(8,128)(2,1)S(1)} %bitcast.36, f32[1536]{0:T(1024)S(1)} %pad_reduce_fusion, bf16[768,2304]{1,0:T(8,128)(2,1)S(1)} %copy-done.2), kind=kOutput, calls=%fused_computation | convolution fusion | flops 4838129664 | bytes 11804672 | tf_op jit(solution)/shard_map/dot_general | solution.py:566
  112.8 48.8 %attend_forward.1 = (bf16[1024,768]{1,0:T(8,128)(2,1)}, bf16[12,1024,256]{2,1,0:T(8,128)(2,1)}, bf16[8,128,768]{2,1,0:T(8,128)(2,1)}) custom-call(f32[1024,768]{1,0:T(8,128)} %fusion.1.query_ref, bf16[2048,1536]{1,0:T(8,128)(2,1)} %add_convert_fusion.key_ref.value_ref, bf16[2048,1536]{1,0:T(8,128)(2,1)} %add_convert_fusion.key_ref.value_ref, ...), custom_call_target="tpu_custom_call" | custom-call | flops 25769803776 | bytes 20000000 | tf_op jit(solution)/shard_map/attend_forward/pallas_call | solution.py:1120
  161.7 57.2 %mlp.1 = (bf16[8,128,768]{2,1,0:T(8,128)(2,1)}, bf16[1024,768]{1,0:T(8,128)(2,1)}, f32[1024,768]{1,0:T(8,128)}, bf16[3072,768]{1,0:T(8,128)(2,1)}, bf16[768,3072...) custom-call(bf16[1024,768]{1,0:T(8,128)(2,1)} %get-tuple-element.59.mixture_ref, ...), custom_call_target="tpu_custom_call" | custom-call | flops 32614907904 | bytes 40000000 | tf_op jit(solution)/shard_map/mlp/pallas_call | solution.py:1376
  218.9 0.5 broadcast.161
  219.5 1.4 reduce.38
  220.9 0.1 reshape.272
  221.0 1.4 maximum_maximum_fusion.mlp_sums_ref
  222.5 107.8 %attend_backward.1 = (bf16[1024,768]{1,0:T(8,128)(2,1)}, bf16[2048,768]{1,0:T(8,128)(2,1)}, bf16[2048,768]{1,0:T(8,128)(2,1)}, bf16[768,256]{1,0:T(8,128)(2,1)},...) custom-call(bf16[12,1024,256]{2,1,0:T(8,128)(2,1)} %get-tuple-elemen, ...), custom_call_target="tpu_custom_call" | custom-call | flops 64424509440 | bytes 32000000 | tf_op jit(solution)/shard_map/attend_backward/pallas_call | solution.py:1637
  330.3 115.1 %finish.1 = (bf16[8,256,768]{2,1,0:T(8,128)(2,1)}, bf16[192,1536]{1,0:T(8,128)(2,1)}, bf16[192,768]{1,0:T(8,128)(2,1)}, bf16[192,256]{1,0:T(8,128)(2,1)}, bf16[1...) custom-call(bf16[1024,768]{1,0:T(8,128)(2,1)} %get-tuple-element.72.grad_query_ref, ...), custom_call_target="tpu_custom_call" | custom-call | tf_op jit(solution)/shard_map/finish/pallas_call | solution.py:967
  445.4 1.0 convert_element_type.131
  446.5 0.1 slice.141
  446.6 0.1 slice.151
  446.7 1.3 slice_reduce_fusion
  448.0 1.4 slice.150
  449.4 1.8 convert_element_type.125
  451.3 0.9 convert_element_type.126
  452.1 0.9 convert_element_type.127
  453.0 0.9 convert_element_type.128
  453.9 0.7 reshape.273
  454.6 0.7 copy.64
  455.3 0.7 reshape_squeeze.10
  455.9 0.7 reshape_squeeze.11
  456.6 0.7 reshape_squeeze.9
  457.2 1.6 maximum_convert_fusion.1
  458.8 1.7 maximum_convert_fusion
  460.5 0.2 copy-done.4
  460.7 1.1 copy.69
  461.8 1.2 copy-done.3
  463.0 1.7 copy.70
  (100 shorter events, 1.1 us)
Async XLA Ops:
  7.2 93.7 %all-gather.9.cloned.1.call-start = ((), (), s32[]{:S(2)}) async-start(), calls=%async_computation.1 | async-start | bytes 4423680 | tf_op jit(solution)/shard_map/all_gather | solution.py:1869
  21.0 140.6 %all-gather.11.cloned.1.call-start = ((), (), s32[]{:S(2)}) async-start(), calls=%async_computation.2 | async-start | bytes 1474560 | tf_op jit(solution)/shard_map/all_gather | solution.py:1871
  21.8 139.9 %all-gather.13.cloned.1.call-start = ((), (), s32[]{:S(2)}) async-start(), calls=%async_computation.3 | async-start | bytes 5898240 | tf_op jit(solution)/shard_map/all_gather | solution.py:1870
  22.5 5.5 %copy-start.14 = (s32[8,4,128]{2,1,0:T(4,128)S(1)}, s32[8,4,128]{2,1,0:T(4,128)}, u32[]{:S(2)}) copy-start(s32[8,4,128]{2,1,0:T(4,128)} %get-tuple-element.56) | copy-start | bytes 49156
  22.5 6.0 %copy-start.16 = (f32[3,2,64]{2,1,0:T(2,128)S(1)}, f32[3,2,64]{2,1,0:T(2,128)}, u32[]{:S(2)}) copy-start(f32[3,2,64]{2,1,0:T(2,128)} %param.48) | copy-start | bytes 4612
  22.5 10.0 %copy-start.17 = (f32[3,64]{1,0:T(4,128)S(1)}, f32[3,64]{1,0:T(4,128)}, u32[]{:S(2)}) copy-start(f32[3,64]{1,0:T(4,128)} %param.44) | copy-start | bytes 2308
  22.6 10.1 %copy-start.18 = (f32[3,64]{1,0:T(4,128)S(1)}, f32[3,64]{1,0:T(4,128)}, u32[]{:S(2)}) copy-start(f32[3,64]{1,0:T(4,128)} %param.45) | copy-start | bytes 2308
  22.6 10.2 %copy-start.19 = (f32[3,64]{1,0:T(4,128)S(1)}, f32[3,64]{1,0:T(4,128)}, u32[]{:S(2)}) copy-start(f32[3,64]{1,0:T(4,128)} %param.46) | copy-start | bytes 2308
  22.6 10.3 %copy-start.20 = (f32[192]{0:T(256)S(1)}, f32[192]{0:T(256)}, u32[]{:S(2)}) copy-start(f32[192]{0:T(256)} %param.36) | copy-start | bytes 2308
  22.6 10.3 %copy-start.21 = (f32[192]{0:T(256)S(1)}, f32[192]{0:T(256)}, u32[]{:S(2)}) copy-start(f32[192]{0:T(256)} %param.37) | copy-start | bytes 2308
  22.6 10.3 %copy-start.22 = (f32[192]{0:T(256)S(1)}, f32[192]{0:T(256)}, u32[]{:S(2)}) copy-start(f32[192]{0:T(256)} %param.39) | copy-start | bytes 2308
  22.6 10.3 %copy-start.23 = (f32[192]{0:T(256)S(1)}, f32[192]{0:T(256)}, u32[]{:S(2)}) copy-start(f32[192]{0:T(256)} %param.40) | copy-start | bytes 2308
  22.6 10.3 %copy-start.24 = (f32[192]{0:T(256)S(1)}, f32[192]{0:T(256)}, u32[]{:S(2)}) copy-start(f32[192]{0:T(256)} %param.41) | copy-start | bytes 2308
  22.6 10.4 %copy-start.25 = (f32[192]{0:T(256)S(1)}, f32[192]{0:T(256)}, u32[]{:S(2)}) copy-start(f32[192]{0:T(256)} %param.42) | copy-start | bytes 2308
  22.7 10.4 %copy-start.26 = (f32[192]{0:T(256)S(1)}, f32[192]{0:T(256)}, u32[]{:S(2)}) copy-start(f32[192]{0:T(256)} %param.43) | copy-start | bytes 2308
  22.7 74.3 %all-to-all-start = ((bf16[8,256,768]{2,1,0:T(8,128)(2,1)}), bf16[8,256,768]{2,1,0:T(8,128)(2,1)S(1)}, u32[]{:S(2)}, u32[]{:S(2)}) async-start(bf16[8,256,768]{2,1,0:T(8,128)(2,1)} %param.26), calls=%async_computation | async-start | bytes 6291456 | tf_op jit(solution)/shard_map/all_to_all | solution.py:1843
  27.4 11.2 %copy-start.12 = (f32[3,64,64]{2,1,0:T(8,128)S(1)}, f32[3,64,64]{2,1,0:T(8,128)}, u32[]{:S(2)}) copy-start(f32[3,64,64]{2,1,0:T(8,128)} %param.47) | copy-start | bytes 147460
  27.4 18.4 %copy-start.15 = (f32[768]{0:T(1024)S(1)}, f32[768]{0:T(1024)}, u32[]{:S(2)}) copy-start(f32[768]{0:T(1024)} %param.38) | copy-start | bytes 9220
  27.4 134.3 %all-gather.15.cloned.1.call-start = ((), (), s32[]{:S(2)}) async-start(), calls=%async_computation.4 | async-start | bytes 5898240 | tf_op jit(solution)/shard_map/all_gather | solution.py:1872
  38.6 26.7 %copy-start.13 = (f32[768,16]{0,1:T(8,128)}, f32[768,16]{0,1:T(8,128)S(1)}, u32[]{:S(2)}) copy-start(f32[768,16]{0,1:T(8,128)S(1)} %reshape.287) | copy-start | bytes 147460
  96.9 8.9 %copy-start = (bf16[8,256,768]{2,1,0:T(8,128)(2,1)}, bf16[8,256,768]{2,1,0:T(8,128)(2,1)S(1)}, u32[]{:S(2)}) copy-start(bf16[8,256,768]{2,1,0:T(8,128)(2,1)S(1)} %all-to-all-done) | copy-start | bytes 9437188
  97.6 2.0 copy-start.1
  100.9 5.0 %copy-start.2 = (bf16[768,2304]{1,0:T(8,128)(2,1)S(1)}, bf16[768,2304]{1,0:T(8,128)(2,1)}, u32[]{:S(2)}) copy-start(bf16[768,2304]{1,0:T(8,128)(2,1)} %all-gather.9.cloned.1.call-done.weights_ref) | copy-start | bytes 10616836
  445.4 5.8 %copy-start.11 = (bf16[192,768]{1,0:T(8,128)(2,1)S(1)}, bf16[192,768]{1,0:T(8,128)(2,1)}, u32[]{:S(2)}) copy-start(bf16[192,768]{1,0:T(8,128)(2,1)} %get-tuple-element.81) | copy-start | bytes 884740
  445.4 6.7 %copy-start.10 = (bf16[192,768]{1,0:T(8,128)(2,1)S(1)}, bf16[192,768]{1,0:T(8,128)(2,1)}, u32[]{:S(2)}) copy-start(bf16[192,768]{1,0:T(8,128)(2,1)} %get-tuple-element.82) | copy-start | bytes 884740
  445.4 7.5 %copy-start.9 = (bf16[192,768]{1,0:T(8,128)(2,1)S(1)}, bf16[192,768]{1,0:T(8,128)(2,1)}, u32[]{:S(2)}) copy-start(bf16[192,768]{1,0:T(8,128)(2,1)} %get-tuple-element.83) | copy-start | bytes 884740
  446.7 10.5 %copy-start.6 = (bf16[384,768]{1,0:T(8,128)(2,1)S(1)}, bf16[384,768]{1,0:T(8,128)(2,1)}, u32[]{:S(2)}) copy-start(bf16[384,768]{1,0:T(8,128)(2,1)} %get-tuple-element.86) | copy-start | bytes 1769476
  446.7 10.5 %copy-start.7 = (bf16[384,768]{1,0:T(8,128)(2,1)S(1)}, bf16[384,768]{1,0:T(8,128)(2,1)}, u32[]{:S(2)}) copy-start(bf16[384,768]{1,0:T(8,128)(2,1)} %get-tuple-element.87) | copy-start | bytes 1769476
  453.0 5.8 %copy-start.5 = (bf16[192,1536]{1,0:T(8,128)(2,1)S(1)}, bf16[192,1536]{1,0:T(8,128)(2,1)}, u32[]{:S(2)}) copy-start(bf16[192,1536]{1,0:T(8,128)(2,1)} %get-tuple-element.84) | copy-start | bytes 1769476
  453.0 5.8 %copy-start.8 = (bf16[192,1536]{1,0:T(8,128)(2,1)S(1)}, bf16[192,1536]{1,0:T(8,128)(2,1)}, u32[]{:S(2)}) copy-start(bf16[192,1536]{1,0:T(8,128)(2,1)} %get-tuple-element.85) | copy-start | bytes 1769476
  458.8 1.9 copy-start.4
  460.5 2.5 copy-start.3
Sparse Core Ops, SparseCore 0:
  21.2 31.7 all-gather.8
  54.5 17.4 all-gather.10
  73.5 37.4 all-gather.12
  112.4 37.4 all-gather.14

commit v6 on v5

--- a/solution.py
+++ b/solution.py
@@ -1162,7 +1162,7 @@
     )(query, pairs, pairs, relative, vectors, query_side, key_side, phase, cosm, sinm, cotangent)
 
 
-FF_STEP = 768
+FF_STEP = 1024
 FF_TILES = FF // FF_STEP
 ROW_TILES = PQ // ROWS
 

time: 476 us -> 476 us (level)
  no operation moved by 1% of the time
where the time goes in v6:
time: 476 us; the launch traced here: 471 us
  Pallas kernels  341 us (72%)
  waiting for transfers between devices  33.6 us (7%)
  other arithmetic  28.3 us (6%)
  local copies, waits for them, and re-layouts  20.1 us (4%)
  blocking collectives  16.8 us (4%)
  between operations  14.6 us (3%)
  matrix products  12.6 us (3%)
  starting transfers between devices  4.87 us (1%)
    pallas_call x1, Pallas kernels, finish(): pl.pallas_call(finish_kernel, in_specs=[inside] * (9 + len(early)), out_s...  115 us
    pallas_call x1, Pallas kernels, attend_backward(): pl.pallas_call(attend_back_kernel, grid=(PAIRS,), in_specs=[pl.BlockSpec(...  108 us
    pallas_call x1, Pallas kernels, mlp(): pl.pallas_call(mlp_kernel, grid=(ROW_TILES + FF_TILES,), in_specs=[fixed(...  57.2 us
    pallas_call x1, Pallas kernels, attend_forward(): pl.pallas_call(attend_kernel, grid=(PAIRS,), in_specs=[pl.BlockSpec((PQ,...  48.8 us
    all_to_all x1, waiting for transfers between devices, sequence_body(): lax.all_to_all(tokens, 'seq', split_axis=0, concat_axis=0, tiled=True)  31.6 us
    dot_general x2, matrix products, mm(): return lax.dot_general(left, right, dims, preferred_element_type=F32)  11.9 us
    pallas_call x1, Pallas kernels, move_labels(): pl.pallas_call(labels_kernel, in_specs=[inside, *[pl.BlockSpec(memory_spa...  11.7 us
  transfers between devices with their start and end apart: 5, of which 1 were waited for; matrix products, arithmetic and copies ran while one was open for 7% of the time, Pallas kernels for 10%

profile of v6, /device:TPU:0, one launch (start us, length us, event | category | flops | bytes accessed | tf_op | source)
XLA Modules:
  0.0 471.4 jit_solution(12747880358440347916)
XLA Ops:
  7.2 0.7 fusion.9
  7.9 0.7 fusion.10
  8.6 0.6 pad_add_fusion.labels_ref
  9.3 11.7 %labels.1 = (s32[8,4,128]{2,1,0:T(4,128)}, bf16[192,2304]{1,0:T(8,128)(2,1)}, bf16[192,768]{1,0:T(8,128)(2,1)}, bf16[192,3072]{1,0:T(8,128)(2,1)}, bf16[768,768]{1,0:T(8,128)(2,1)}) custom-call(s32[8,4,128]{2,1,0:T(4,128)} %pad_add_fusion.labels_ref, f32[192,768]{1,0:T(8,128)} %query_ref.1, f32[192,768]{1,0:T(8,128)} %key_ref.1, f32[192,768]{1,0:T(8,128)} %value_ref.1, ...), custom_call_target="tpu_custom_call" | custom-call | tf_op jit(solution)/shard_map/labels/pallas_call | solution.py:1768
  21.1 0.7 all-gather.11.cloned.1.call-update
  21.8 0.7 all-gather.13.cloned.1.call-update
  22.7 4.7 %all-to-all-start = ((bf16[8,256,768]{2,1,0:T(8,128)(2,1)}), bf16[8,256,768]{2,1,0:T(8,128)(2,1)S(1)}, u32[]{:S(2)}, u32[]{:S(2)}) async-start(bf16[8,256,768]{2,1,0:T(8,128)(2,1)} %param.26), calls=%async_computation | async-start | bytes 6291456 | tf_op jit(solution)/shard_map/all_to_all | solution.py:1843
  27.5 0.5 all-gather.15.cloned.1.call-update
  28.0 0.5 slice.137
  28.5 1.3 fusion.6
  29.8 1.3 reshape_reshape.7
  31.1 1.3 reshape_reshape.6
  32.6 0.1 reshape.263
  32.7 0.1 reshape.264
  32.8 0.1 reshape.265
  33.1 5.3 %all-gather.1 = bf16[4,192,16]{1,2,0:T(8,128)(2,1)S(1)} all-gather(bf16[1,192,16]{1,2,0:T(8,128)(2,1)S(1)} %bitcast.54), channel_id=1, replica_groups=mesh['seq'=8,'dp'=4] {'dp'}, dimensions={0}, use_global_device_ids=true | all-gather | bytes 30720 | tf_op jit(solution)/shard_map/all_gather | solution.py:1863
  38.5 0.1 reshape.287
  38.6 0.1 copy.60
  38.7 6.2 %all-gather.2 = bf16[4,192,64]{1,2,0:T(8,128)(2,1)S(1)} all-gather(bf16[1,192,64]{1,2,0:T(8,128)(2,1)S(1)} %copy.60), channel_id=1, replica_groups=mesh['seq'=8,'dp'=4] {'dp'}, dimensions={0}, use_global_device_ids=true | all-gather | bytes 122880 | tf_op jit(solution)/shard_map/all_gather | solution.py:1868
  44.9 0.8 copy.61
  45.8 5.2 %all-gather.3 = bf16[4,1,768]{2,1,0:T(2,128)(2,1)S(1)} all-gather(bf16[1,1,768]{2,1,0:T(2,128)(2,1)S(1)} %reshape.282), channel_id=2, replica_groups=mesh['seq'=8,'dp'=4] {'dp'}, dimensions={0}, use_global_device_ids=true | all-gather | bytes 7680 | tf_op jit(solution)/shard_map/all_gather | solution.py:1865
  51.0 0.6 convert.5.inner_add_ref
  51.7 0.6 fusion.8
  52.3 1.6 select_reduce_fusion.2
  53.9 4.1 add_reduce_fusion
  58.0 2.6 select_add_fusion
  60.6 0.1 iota_compare_fusion.4
  60.8 1.1 convert_select_fusion.query_side_ref
  61.9 1.1 select_convert_fusion.pool_ref
  63.0 2.3 fusion.5.key_side_ref
  65.3 31.6 %all-to-all-done = bf16[8,256,768]{2,1,0:T(8,128)(2,1)S(1)} async-done(((bf16[8,256,768]{2,1,0:T(8,128)(2,1)}), bf16[8,256,768]{2,1,0:T(8,128)(2,1)S(1)}, u32[]{:S(2)}, u32[]{:S(2)}) %all-to-all-start) | async-done | bytes 3145760 | tf_op jit(solution)/shard_map/all_to_all | solution.py:1843
  96.9 0.6 fusion.7
  97.6 2.0 copy-done.1
  99.6 1.3 bitcast_convert_fusion.pooled_ref
  100.9 4.9 %fusion.1.query_ref = f32[1024,768]{1,0:T(8,128)} fusion(bf16[1024,768]{1,0:T(8,128)(2,1)} %bitcast_convert_fusion.pooled_ref, bf16[768,2304]{1,0:T(8,128)(2,1)} %all-gather.9.cloned.1.call-done.weights_ref), kind=kOutput, calls=%fused_computation.2 | convolution fusion | flops 1207959552 | bytes 5898240 | tf_op jit(solution)/shard_map/dot_general | solution.py:566
  105.8 7.0 %add_convert_fusion.key_ref.value_ref = bf16[2048,1536]{1,0:T(8,128)(2,1)} fusion(bf16[2048,768]{1,0:T(8,128)(2,1)S(1)} %bitcast.36, f32[1536]{0:T(1024)S(1)} %pad_reduce_fusion, bf16[768,2304]{1,0:T(8,128)(2,1)S(1)} %copy-done.2), kind=kOutput, calls=%fused_computation | convolution fusion | flops 4838129664 | bytes 11804672 | tf_op jit(solution)/shard_map/dot_general | solution.py:566
  112.8 48.8 %attend_forward.1 = (bf16[1024,768]{1,0:T(8,128)(2,1)}, bf16[12,1024,256]{2,1,0:T(8,128)(2,1)}, bf16[8,128,768]{2,1,0:T(8,128)(2,1)}) custom-call(f32[1024,768]{1,0:T(8,128)} %fusion.1.query_ref, bf16[2048,1536]{1,0:T(8,128)(2,1)} %add_convert_fusion.key_ref.value_ref, bf16[2048,1536]{1,0:T(8,128)(2,1)} %add_convert_fusion.key_ref.value_ref, ...), custom_call_target="tpu_custom_call" | custom-call | flops 25769803776 | bytes 20000000 | tf_op jit(solution)/shard_map/attend_forward/pallas_call | solution.py:1120
  161.7 57.2 %mlp.1 = (bf16[8,128,768]{2,1,0:T(8,128)(2,1)}, bf16[1024,768]{1,0:T(8,128)(2,1)}, f32[1024,768]{1,0:T(8,128)}, bf16[3072,768]{1,0:T(8,128)(2,1)}, bf16[768,3072...) custom-call(bf16[1024,768]{1,0:T(8,128)(2,1)} %get-tuple-element.59.mixture_ref, ...), custom_call_target="tpu_custom_call" | custom-call | flops 32614907904 | bytes 40000000 | tf_op jit(solution)/shard_map/mlp/pallas_call | solution.py:1376
  218.9 0.5 broadcast.161
  219.4 1.4 reduce.38
  220.9 0.1 reshape.272
  221.0 1.4 maximum_maximum_fusion.mlp_sums_ref
  222.4 107.8 %attend_backward.1 = (bf16[1024,768]{1,0:T(8,128)(2,1)}, bf16[2048,768]{1,0:T(8,128)(2,1)}, bf16[2048,768]{1,0:T(8,128)(2,1)}, bf16[768,256]{1,0:T(8,128)(2,1)},...) custom-call(bf16[12,1024,256]{2,1,0:T(8,128)(2,1)} %get-tuple-elemen, ...), custom_call_target="tpu_custom_call" | custom-call | flops 64424509440 | bytes 32000000 | tf_op jit(solution)/shard_map/attend_backward/pallas_call | solution.py:1637
  330.3 115.1 %finish.1 = (bf16[8,256,768]{2,1,0:T(8,128)(2,1)}, bf16[192,1536]{1,0:T(8,128)(2,1)}, bf16[192,768]{1,0:T(8,128)(2,1)}, bf16[192,256]{1,0:T(8,128)(2,1)}, bf16[1...) custom-call(bf16[1024,768]{1,0:T(8,128)(2,1)} %get-tuple-element.72.grad_query_ref, ...), custom_call_target="tpu_custom_call" | custom-call | tf_op jit(solution)/shard_map/finish/pallas_call | solution.py:967
  445.4 1.0 convert_element_type.131
  446.5 0.1 slice.141
  446.6 0.1 slice.151
  446.7 1.3 slice_reduce_fusion
  448.0 1.4 slice.150
  449.4 1.8 convert_element_type.125
  451.2 0.9 convert_element_type.126
  452.1 0.9 convert_element_type.127
  452.9 0.9 convert_element_type.128
  453.9 0.7 reshape.273
  454.6 0.7 copy.64
  455.2 0.7 reshape_squeeze.10
  455.9 0.7 reshape_squeeze.11
  456.5 0.7 reshape_squeeze.9
  457.2 1.6 maximum_convert_fusion.1
  458.8 1.7 maximum_convert_fusion
  460.5 0.2 copy-done.4
  460.6 1.1 copy.69
  461.8 1.2 copy-done.3
  463.0 1.7 copy.70
  (100 shorter events, 1.1 us)
Async XLA Ops:
  7.2 93.7 %all-gather.9.cloned.1.call-start = ((), (), s32[]{:S(2)}) async-start(), calls=%async_computation.1 | async-start | bytes 4423680 | tf_op jit(solution)/shard_map/all_gather | solution.py:1869
  21.0 140.6 %all-gather.11.cloned.1.call-start = ((), (), s32[]{:S(2)}) async-start(), calls=%async_computation.2 | async-start | bytes 1474560 | tf_op jit(solution)/shard_map/all_gather | solution.py:1871
  21.8 139.9 %all-gather.13.cloned.1.call-start = ((), (), s32[]{:S(2)}) async-start(), calls=%async_computation.3 | async-start | bytes 5898240 | tf_op jit(solution)/shard_map/all_gather | solution.py:1870
  22.5 5.5 %copy-start.14 = (s32[8,4,128]{2,1,0:T(4,128)S(1)}, s32[8,4,128]{2,1,0:T(4,128)}, u32[]{:S(2)}) copy-start(s32[8,4,128]{2,1,0:T(4,128)} %get-tuple-element.56) | copy-start | bytes 49156
  22.5 6.0 %copy-start.16 = (f32[3,2,64]{2,1,0:T(2,128)S(1)}, f32[3,2,64]{2,1,0:T(2,128)}, u32[]{:S(2)}) copy-start(f32[3,2,64]{2,1,0:T(2,128)} %param.48) | copy-start | bytes 4612
  22.5 10.0 %copy-start.17 = (f32[3,64]{1,0:T(4,128)S(1)}, f32[3,64]{1,0:T(4,128)}, u32[]{:S(2)}) copy-start(f32[3,64]{1,0:T(4,128)} %param.44) | copy-start | bytes 2308
  22.6 10.1 %copy-start.18 = (f32[3,64]{1,0:T(4,128)S(1)}, f32[3,64]{1,0:T(4,128)}, u32[]{:S(2)}) copy-start(f32[3,64]{1,0:T(4,128)} %param.45) | copy-start | bytes 2308
  22.6 10.2 %copy-start.19 = (f32[3,64]{1,0:T(4,128)S(1)}, f32[3,64]{1,0:T(4,128)}, u32[]{:S(2)}) copy-start(f32[3,64]{1,0:T(4,128)} %param.46) | copy-start | bytes 2308
  22.6 10.3 %copy-start.20 = (f32[192]{0:T(256)S(1)}, f32[192]{0:T(256)}, u32[]{:S(2)}) copy-start(f32[192]{0:T(256)} %param.36) | copy-start | bytes 2308
  22.6 10.3 %copy-start.21 = (f32[192]{0:T(256)S(1)}, f32[192]{0:T(256)}, u32[]{:S(2)}) copy-start(f32[192]{0:T(256)} %param.37) | copy-start | bytes 2308
  22.6 10.3 %copy-start.22 = (f32[192]{0:T(256)S(1)}, f32[192]{0:T(256)}, u32[]{:S(2)}) copy-start(f32[192]{0:T(256)} %param.39) | copy-start | bytes 2308
  22.6 10.3 %copy-start.23 = (f32[192]{0:T(256)S(1)}, f32[192]{0:T(256)}, u32[]{:S(2)}) copy-start(f32[192]{0:T(256)} %param.40) | copy-start | bytes 2308
  22.6 10.3 %copy-start.24 = (f32[192]{0:T(256)S(1)}, f32[192]{0:T(256)}, u32[]{:S(2)}) copy-start(f32[192]{0:T(256)} %param.41) | copy-start | bytes 2308
  22.6 10.4 %copy-start.25 = (f32[192]{0:T(256)S(1)}, f32[192]{0:T(256)}, u32[]{:S(2)}) copy-start(f32[192]{0:T(256)} %param.42) | copy-start | bytes 2308
  22.7 10.4 %copy-start.26 = (f32[192]{0:T(256)S(1)}, f32[192]{0:T(256)}, u32[]{:S(2)}) copy-start(f32[192]{0:T(256)} %param.43) | copy-start | bytes 2308
  22.7 74.3 %all-to-all-start = ((bf16[8,256,768]{2,1,0:T(8,128)(2,1)}), bf16[8,256,768]{2,1,0:T(8,128)(2,1)S(1)}, u32[]{:S(2)}, u32[]{:S(2)}) async-start(bf16[8,256,768]{2,1,0:T(8,128)(2,1)} %param.26), calls=%async_computation | async-start | bytes 6291456 | tf_op jit(solution)/shard_map/all_to_all | solution.py:1843
  27.4 11.2 %copy-start.12 = (f32[3,64,64]{2,1,0:T(8,128)S(1)}, f32[3,64,64]{2,1,0:T(8,128)}, u32[]{:S(2)}) copy-start(f32[3,64,64]{2,1,0:T(8,128)} %param.47) | copy-start | bytes 147460
  27.4 18.4 %copy-start.15 = (f32[768]{0:T(1024)S(1)}, f32[768]{0:T(1024)}, u32[]{:S(2)}) copy-start(f32[768]{0:T(1024)} %param.38) | copy-start | bytes 9220
  27.4 134.3 %all-gather.15.cloned.1.call-start = ((), (), s32[]{:S(2)}) async-start(), calls=%async_computation.4 | async-start | bytes 5898240 | tf_op jit(solution)/shard_map/all_gather | solution.py:1872
  38.6 26.7 %copy-start.13 = (f32[768,16]{0,1:T(8,128)}, f32[768,16]{0,1:T(8,128)S(1)}, u32[]{:S(2)}) copy-start(f32[768,16]{0,1:T(8,128)S(1)} %reshape.287) | copy-start | bytes 147460
  96.9 8.9 %copy-start = (bf16[8,256,768]{2,1,0:T(8,128)(2,1)}, bf16[8,256,768]{2,1,0:T(8,128)(2,1)S(1)}, u32[]{:S(2)}) copy-start(bf16[8,256,768]{2,1,0:T(8,128)(2,1)S(1)} %all-to-all-done) | copy-start | bytes 9437188
  97.6 2.0 copy-start.1
  100.9 5.0 %copy-start.2 = (bf16[768,2304]{1,0:T(8,128)(2,1)S(1)}, bf16[768,2304]{1,0:T(8,128)(2,1)}, u32[]{:S(2)}) copy-start(bf16[768,2304]{1,0:T(8,128)(2,1)} %all-gather.9.cloned.1.call-done.weights_ref) | copy-start | bytes 10616836
  445.4 5.8 %copy-start.11 = (bf16[192,768]{1,0:T(8,128)(2,1)S(1)}, bf16[192,768]{1,0:T(8,128)(2,1)}, u32[]{:S(2)}) copy-start(bf16[192,768]{1,0:T(8,128)(2,1)} %get-tuple-element.81) | copy-start | bytes 884740
  445.4 6.7 %copy-start.10 = (bf16[192,768]{1,0:T(8,128)(2,1)S(1)}, bf16[192,768]{1,0:T(8,128)(2,1)}, u32[]{:S(2)}) copy-start(bf16[192,768]{1,0:T(8,128)(2,1)} %get-tuple-element.82) | copy-start | bytes 884740
  445.4 7.5 %copy-start.9 = (bf16[192,768]{1,0:T(8,128)(2,1)S(1)}, bf16[192,768]{1,0:T(8,128)(2,1)}, u32[]{:S(2)}) copy-start(bf16[192,768]{1,0:T(8,128)(2,1)} %get-tuple-element.83) | copy-start | bytes 884740
  446.7 10.5 %copy-start.6 = (bf16[384,768]{1,0:T(8,128)(2,1)S(1)}, bf16[384,768]{1,0:T(8,128)(2,1)}, u32[]{:S(2)}) copy-start(bf16[384,768]{1,0:T(8,128)(2,1)} %get-tuple-element.86) | copy-start | bytes 1769476
  446.7 10.5 %copy-start.7 = (bf16[384,768]{1,0:T(8,128)(2,1)S(1)}, bf16[384,768]{1,0:T(8,128)(2,1)}, u32[]{:S(2)}) copy-start(bf16[384,768]{1,0:T(8,128)(2,1)} %get-tuple-element.87) | copy-start | bytes 1769476
  452.9 5.8 %copy-start.5 = (bf16[192,1536]{1,0:T(8,128)(2,1)S(1)}, bf16[192,1536]{1,0:T(8,128)(2,1)}, u32[]{:S(2)}) copy-start(bf16[192,1536]{1,0:T(8,128)(2,1)} %get-tuple-element.84) | copy-start | bytes 1769476
  452.9 5.8 %copy-start.8 = (bf16[192,1536]{1,0:T(8,128)(2,1)S(1)}, bf16[192,1536]{1,0:T(8,128)(2,1)}, u32[]{:S(2)}) copy-start(bf16[192,1536]{1,0:T(8,128)(2,1)} %get-tuple-element.85) | copy-start | bytes 1769476
  458.8 1.9 copy-start.4
  460.5 2.5 copy-start.3
Sparse Core Ops, SparseCore 0:
  21.2 31.7 all-gather.8
  54.5 17.4 all-gather.10
  73.5 37.4 all-gather.12
  112.4 37.4 all-gather.14
